TPU v7x, 32 devices: a whole 2x2x4 slice. The times are simulated.
32 devices in a mesh: gx: 4 (over z), gy: 8 (over y, x, core).
Axes of the slice: x: 2, y: 2, z: 4, core: 2. Of those that a mesh axis runs over, the one named last changes fastest.
Arguments:
- tokens: bfloat16 [8, 512, 1536], P('gy', 'gx'), may hold values from -6 to 6
- first_gain: float32 [1536], replicated, may hold values from 0.5 to 1.5
- query_weight: bfloat16 [1536, 1536], P('gy', 'gx'), may hold values from -0.4375 to 0.4375
- key_matrix: bfloat16 [1536, 512], P('gy', 'gx'), may hold values from -0.4375 to 0.4375
- value_matrix: bfloat16 [1536, 512], P('gy', 'gx'), may hold values from -0.15625 to 0.15625
- out_weight: bfloat16 [1536, 1536], P('gx', 'gy'), may hold values from -2.5 to 2.5
- second_gain: float32 [1536], replicated, may hold values from 0.5 to 1.5
- gate_weight: bfloat16 [40, 1536, 512], P('gx', 'gy'), may hold values from -0.15625 to 0.15625
- up_weight: bfloat16 [40, 1536, 512], P('gx', 'gy'), may hold values from -0.15625 to 0.15625
- down_weight: bfloat16 [40, 512, 1536], P('gx', None, 'gy'), may hold values from -3 to 3
- routes: int32 [8, 512, 8], P('gy', 'gx'), may hold values from 0 to 39, all different within a row; in each aligned block of 128 rows (0 to 127, 128 to 255, ..., all dimensions but the last counted through in order) at most 48 rows name the same one
- route_logits: float32 [8, 512, 8], P('gy', 'gx'), may hold values from -1.25 to 1.25
- cotangent: bfloat16 [8, 512, 1536], P('gy', 'gx'), may hold values from -6 to 6
Outputs:
- output: bfloat16 [8, 512, 1536], P('gy', 'gx')
- tokens_grad: float32 [8, 512, 1536], P('gy', 'gx')
- first_gain_grad: float32 [1536], replicated
- query_grad: float32 [1536, 1536], P('gy', 'gx')
- key_grad: float32 [1536, 512], P('gy', 'gx')
- value_grad: float32 [1536, 512], P('gy', 'gx')
- out_weight_grad: float32 [1536, 1536], P('gx', 'gy')
- second_gain_grad: float32 [1536], replicated
- gate_grad: float32 [40, 1536, 512], P('gx', 'gy')
- up_grad: float32 [40, 1536, 512], P('gx', 'gy')
- down_grad: float32 [40, 512, 1536], P('gx', None, 'gy')
- logit_grad: float32 [8, 512, 8], P('gy', 'gx')
Inputs may be any that keep to these rules, and one draw needn't show every extreme that they name: `routes`: each token names 8 different experts. In the 128 tokens of one device no expert is named by more than 48 of them, and in every draw some expert is named by exactly 48 tokens of some device.
All inputs are finite; a program needn't handle non-finite values.
Results may differ from a plain program's by a relative error of at most 0.015.
Values may be sent and summed in bfloat16 or wider, within the bound.
No kernel may reach another device: no remote copies, remote signals or barrier semaphores. Data moves between devices by JAX's collectives and lax.ppermute only.
A program may use at most 256 MiB of HBM per device.

v0:
```python
import jax
import jax.numpy as jnp
from jax import lax
from jax.sharding import PartitionSpec as P

HEAD_SIZE = 64
EXPERTS = 40
TOPK = 8
CAP = 48


epsilon = 1e-06
rope_base = 10000.0
residual_factor = 0.22
score_factor = 0.015625
masked_value = -1e30


def rms_factor(rows):
    return lax.rsqrt(jnp.mean(rows * rows, axis=-1, keepdims=True) + epsilon)


def norm_back(rows, factor, gain, upstream):
    scaled = upstream * gain
    inner = jnp.mean(scaled * rows, axis=-1, keepdims=True)
    rows_back = factor * scaled - rows * factor * factor * factor * inner
    gain_back = jnp.sum(upstream * rows * factor, axis=0)
    return (rows_back, gain_back)


def rotary_embedding(rows, sign):
    width = rows.shape[-1]
    half = width // 2
    length_total = rows.shape[0]
    freq = rope_base ** (-(jnp.arange(half, dtype=jnp.float32) * 2.0 / width))
    angle = jnp.arange(length_total, dtype=jnp.float32)[:, None] * freq[None, :]
    cosine = jnp.cos(angle)[:, None, :]
    sine = sign * jnp.sin(angle)[:, None, :]
    first = rows[..., :half]
    second = rows[..., half:]
    return jnp.concatenate(
        [first * cosine - second * sine, first * sine + second * cosine], axis=-1
    )


def contract_rows(left, right):
    return lax.dot_general(
        left, right, (((0,), (0,)), ((), ())), preferred_element_type=jnp.float32
    )


def contract_cols(left, right):
    return lax.dot_general(
        left, right, (((1,), (1,)), ((), ())), preferred_element_type=jnp.float32
    )


def block_scores(query_block, key_rows, offset):
    raw = jnp.einsum("qhgd,khd->hgqk", query_block, key_rows, preferred_element_type=jnp.float32)
    positions = offset + jnp.arange(query_block.shape[0], dtype=jnp.int32)
    columns = jnp.arange(key_rows.shape[0], dtype=jnp.int32)
    return jnp.where(columns[None, :] <= positions[:, None], raw * score_factor, masked_value)


def attend_forward(query_rows, key_rows, value_rows, block_slice):
    length_total = query_rows.shape[0]
    count_total = length_total // block_slice
    block_list = query_rows.reshape((count_total, block_slice) + query_rows.shape[1:])
    offsets = jnp.arange(count_total, dtype=jnp.int32) * block_slice

    def one_block(pair):
        scores = block_scores(pair[0], key_rows, pair[1])
        top = jnp.max(scores, axis=-1, keepdims=True)
        weights = jnp.exp(scores - top)
        total = jnp.sum(weights, axis=-1, keepdims=True)
        probs = (weights / total).astype(jnp.bfloat16)
        mixed = jnp.einsum("hgqk,khd->qhgd", probs, value_rows, preferred_element_type=jnp.float32)
        return (mixed.astype(jnp.bfloat16), (top + jnp.log(total))[..., 0])

    heads, spread = lax.map(one_block, (block_list, offsets))
    return (heads.reshape(length_total, -1), spread)


def attend_backward(query_rows, key_rows, value_rows, heads_back, spread, block_slice):
    length_total = query_rows.shape[0]
    count_total = length_total // block_slice
    block_list = query_rows.reshape((count_total, block_slice) + query_rows.shape[1:])
    back_blocks = heads_back.reshape((count_total, block_slice) + query_rows.shape[1:])
    offsets = jnp.arange(count_total, dtype=jnp.int32) * block_slice

    def one_block(carry, inputs):
        key_total, value_total = carry
        query_block, back_block, spread_block, offset = inputs
        scores = block_scores(query_block, key_rows, offset)
        probs = jnp.exp(scores - spread_block[..., None])
        prob_back = jnp.einsum(
            "qhgd,khd->hgqk", back_block, value_rows, preferred_element_type=jnp.float32
        )
        inner = jnp.sum(probs * prob_back, axis=-1, keepdims=True)
        score_back = (probs * (prob_back - inner)).astype(jnp.bfloat16)
        query_grad = (
            jnp.einsum("hgqk,khd->qhgd", score_back, key_rows, preferred_element_type=jnp.float32)
            * score_factor
        )
        key_total = (
            key_total
            + jnp.einsum(
                "hgqk,qhgd->khd", score_back, query_block, preferred_element_type=jnp.float32
            )
            * score_factor
        )
        value_total = value_total + jnp.einsum(
            "hgqk,qhgd->khd",
            probs.astype(jnp.bfloat16),
            back_block,
            preferred_element_type=jnp.float32,
        )
        return ((key_total, value_total), query_grad)

    zeros = jnp.zeros(key_rows.shape, jnp.float32)
    totals, query_back = lax.scan(
        one_block, (zeros, zeros), (block_list, back_blocks, spread, offsets)
    )
    return (query_back.reshape(query_rows.shape), totals[0], totals[1])


def route_slots(route_rows, experts, capacity):
    flat = route_rows.reshape(-1)
    total = flat.shape[0]
    hits = (flat[:, None] == jnp.arange(experts, dtype=jnp.int32)[None, :]).astype(jnp.int32)
    before = jnp.cumsum(hits, axis=0) - hits
    place = jnp.sum(before * hits, axis=1)
    target = flat * capacity + place
    owner = (
        jnp.zeros((experts * capacity,), jnp.int32)
        .at[target]
        .set(jnp.arange(total, dtype=jnp.int32))
    )
    filled = (
        jnp.zeros((experts * capacity,), jnp.int32).at[target].set(jnp.ones((total,), jnp.int32))
    )
    return (target, owner, filled)


def local(
    tokens,
    first_gain,
    query_weight,
    key_matrix,
    value_matrix,
    out_weight,
    second_gain,
    gate_weight,
    up_weight,
    down_weight,
    routes,
    route_logits,
    cotangent,
):
    hidden = tokens[0].astype(jnp.float32)
    local_rows = hidden.shape[0]
    width = hidden.shape[1]
    groups = lax.axis_size("gx")
    factor_one = rms_factor(hidden)
    normed_one = (hidden * factor_one * first_gain).astype(jnp.bfloat16)
    query_full, key_full, value_full, out_full, gate_full, up_full, down_full = (
        lax.all_gather(query_weight, "gy", axis=0, tiled=True),
        lax.all_gather(key_matrix, "gy", axis=0, tiled=True),
        lax.all_gather(value_matrix, "gy", axis=0, tiled=True),
        lax.all_gather(out_weight, "gy", axis=1, tiled=True),
        lax.all_gather(gate_weight, "gy", axis=1, tiled=True),
        lax.all_gather(up_weight, "gy", axis=1, tiled=True),
        lax.all_gather(down_weight, "gy", axis=2, tiled=True),
    )
    query_cols = query_full.shape[1]
    key_cols = key_full.shape[1]
    joined = jnp.concatenate([query_full, key_full, value_full], axis=1)
    sequence_rows = lax.all_gather(normed_one, "gx", axis=0, tiled=True)
    projected = jnp.dot(sequence_rows, joined, preferred_element_type=jnp.float32)
    length_total = projected.shape[0]
    query_heads = query_cols // HEAD_SIZE
    pair_heads = key_cols // HEAD_SIZE
    ratio_factor = query_heads // pair_heads
    query_rows = rotary_embedding(
        projected[:, :query_cols].reshape(length_total, query_heads, HEAD_SIZE), 1.0
    )
    query_rows = query_rows.astype(jnp.bfloat16).reshape(
        length_total, pair_heads, ratio_factor, HEAD_SIZE
    )
    key_rows = rotary_embedding(
        projected[:, query_cols : query_cols + key_cols].reshape(
            length_total, pair_heads, HEAD_SIZE
        ),
        1.0,
    ).astype(jnp.bfloat16)
    value_rows = (
        projected[:, query_cols + key_cols :]
        .reshape(length_total, pair_heads, HEAD_SIZE)
        .astype(jnp.bfloat16)
    )
    block_slice = min(512, length_total)
    heads, spread = attend_forward(query_rows, key_rows, value_rows, block_slice)
    branch = lax.psum_scatter(
        jnp.dot(heads, out_full, preferred_element_type=jnp.float32),
        "gx",
        scatter_dimension=0,
        tiled=True,
    )
    middle = hidden + residual_factor * branch
    factor_two = rms_factor(middle)
    normed_two = (middle * factor_two * second_gain).astype(jnp.bfloat16)
    local_experts = gate_full.shape[0]
    target, owner, filled = route_slots(routes[0], EXPERTS, CAP)
    live = (filled > 0)[:, None]
    send = jnp.where(live, normed_two[owner // TOPK], jnp.zeros((), jnp.bfloat16))
    received = lax.all_to_all(
        send.reshape(groups, local_experts, CAP, width),
        "gx",
        split_axis=0,
        concat_axis=2,
        tiled=True,
    )
    slots_all = received.shape[2]
    received = received.reshape(local_experts, slots_all, width)
    gate = jnp.einsum("emd,edf->emf", received, gate_full, preferred_element_type=jnp.float32)
    upper = jnp.einsum("emd,edf->emf", received, up_full, preferred_element_type=jnp.float32)
    sigma = jax.nn.sigmoid(gate)
    active = (gate * sigma * upper).astype(jnp.bfloat16)
    produced = jnp.einsum(
        "emf,efd->emd", active, down_full, preferred_element_type=jnp.float32
    ).astype(jnp.bfloat16)
    returned = lax.all_to_all(
        produced.reshape(1, local_experts, slots_all, width),
        "gx",
        split_axis=2,
        concat_axis=0,
        tiled=True,
    )
    picked = returned.reshape(-1, width)[target].reshape(local_rows, TOPK, width)
    logit_rows = route_logits[0]
    weights = jnp.exp(logit_rows - jnp.max(logit_rows, axis=-1, keepdims=True))
    chance = weights / jnp.sum(weights, axis=-1, keepdims=True)
    mixed = jnp.einsum("tk,tkd->td", chance, picked, preferred_element_type=jnp.float32)
    output = (middle + residual_factor * mixed).astype(jnp.bfloat16)
    upstream = cotangent[0].astype(jnp.float32)
    mixed_back = residual_factor * upstream
    chance_back = jnp.einsum("td,tkd->tk", mixed_back, picked, preferred_element_type=jnp.float32)
    logit_back = chance * (chance_back - jnp.sum(chance * chance_back, axis=-1, keepdims=True))
    route_back = (
        (chance[:, :, None] * mixed_back[:, None, :]).astype(jnp.bfloat16).reshape(-1, width)
    )
    back_send = jnp.where(live, route_back[owner], jnp.zeros((), jnp.bfloat16))
    back_received = lax.all_to_all(
        back_send.reshape(groups, local_experts, CAP, width),
        "gx",
        split_axis=0,
        concat_axis=2,
        tiled=True,
    )
    back_received = back_received.reshape(local_experts, slots_all, width)
    active_back = jnp.einsum(
        "emd,efd->emf", back_received, down_full, preferred_element_type=jnp.float32
    )
    down_grad = jnp.einsum(
        "emf,emd->efd", active, back_received, preferred_element_type=jnp.float32
    )
    gate_back = (active_back * upper * sigma * (1.0 + gate * (1.0 - sigma))).astype(jnp.bfloat16)
    upper_back = (active_back * gate * sigma).astype(jnp.bfloat16)
    gate_grad = jnp.einsum("emd,emf->edf", received, gate_back, preferred_element_type=jnp.float32)
    up_grad = jnp.einsum("emd,emf->edf", received, upper_back, preferred_element_type=jnp.float32)
    rows_back = jnp.einsum("emf,edf->emd", gate_back, gate_full, preferred_element_type=jnp.float32)
    rows_back = (
        rows_back
        + jnp.einsum("emf,edf->emd", upper_back, up_full, preferred_element_type=jnp.float32)
    ).astype(jnp.bfloat16)
    returned_back = lax.all_to_all(
        rows_back.reshape(1, local_experts, slots_all, width),
        "gx",
        split_axis=2,
        concat_axis=0,
        tiled=True,
    )
    routed_back = returned_back.reshape(-1, width)[target].reshape(local_rows, TOPK, width)
    normed_two_back = jnp.sum(routed_back.astype(jnp.float32), axis=1)
    middle_norm_back, second_part = norm_back(middle, factor_two, second_gain, normed_two_back)
    middle_back = upstream + middle_norm_back
    branch_back = (residual_factor * middle_back).astype(jnp.bfloat16)
    piece = lax.all_gather(branch_back, "gx", axis=0, tiled=True)
    heads_grad = contract_cols(piece, out_full)
    weight_total = contract_rows(heads, piece)
    heads_back = heads_grad
    heads_back = heads_back.astype(jnp.bfloat16).reshape(
        length_total, pair_heads, ratio_factor, HEAD_SIZE
    )
    query_back, key_back, value_back = attend_backward(
        query_rows, key_rows, value_rows, heads_back, spread, block_slice
    )
    query_back = rotary_embedding(
        query_back.reshape(length_total, query_heads, HEAD_SIZE), -1.0
    ).reshape(length_total, query_cols)
    key_back = rotary_embedding(key_back, -1.0).reshape(length_total, key_cols)
    value_back = value_back.reshape(length_total, key_cols)
    projected_back = jnp.concatenate([query_back, key_back, value_back], axis=1).astype(
        jnp.bfloat16
    )
    joined_grad = contract_rows(sequence_rows, projected_back)
    normed_one_back = lax.psum_scatter(
        contract_cols(projected_back, joined), "gx", scatter_dimension=0, tiled=True
    )
    tokens_norm_back, first_part = norm_back(hidden, factor_one, first_gain, normed_one_back)
    tokens_back = middle_back + tokens_norm_back
    gain_one, gain_two = lax.psum((first_part, second_part), ("gx", "gy"))
    query_part = joined_grad[:, :query_cols]
    key_part = joined_grad[:, query_cols : query_cols + key_cols]
    value_part = joined_grad[:, query_cols + key_cols :]
    query_sum, key_sum, value_sum, out_sum, gate_sum, up_sum, down_sum = (
        lax.psum_scatter(query_part, "gy", scatter_dimension=0, tiled=True),
        lax.psum_scatter(key_part, "gy", scatter_dimension=0, tiled=True),
        lax.psum_scatter(value_part, "gy", scatter_dimension=0, tiled=True),
        lax.psum_scatter(weight_total, "gy", scatter_dimension=1, tiled=True),
        lax.psum_scatter(gate_grad, "gy", scatter_dimension=1, tiled=True),
        lax.psum_scatter(up_grad, "gy", scatter_dimension=1, tiled=True),
        lax.psum_scatter(down_grad, "gy", scatter_dimension=2, tiled=True),
    )
    return (
        output[None],
        tokens_back[None],
        gain_one,
        query_sum,
        key_sum,
        value_sum,
        out_sum,
        gain_two,
        gate_sum,
        up_sum,
        down_sum,
        logit_back[None],
    )


def solution(mesh):
    in_specs = (
        P("gy", "gx", None),
        P(),
        P("gy", "gx"),
        P("gy", "gx"),
        P("gy", "gx"),
        P("gx", "gy"),
        P(),
        P("gx", "gy", None),
        P("gx", "gy", None),
        P("gx", None, "gy"),
        P("gy", "gx", None),
        P("gy", "gx", None),
        P("gy", "gx", None),
    )
    out_specs = (
        P("gy", "gx", None),
        P("gy", "gx", None),
        P(),
        P("gy", "gx"),
        P("gy", "gx"),
        P("gy", "gx"),
        P("gx", "gy"),
        P(),
        P("gx", "gy", None),
        P("gx", "gy", None),
        P("gx", None, "gy"),
        P("gy", "gx", None),
    )
    return jax.shard_map(local, mesh=mesh, in_specs=in_specs, out_specs=out_specs, check_vma=False)
```

profile of v0, /device:TPU:0, one launch (start us, length us, event | category | flops | bytes accessed | tf_op | source)
XLA Modules:
  0.0 1644.9 jit_solution(5930508468256142257)
XLA Ops:
  13.5 11.9 all_gather.29
  41.8 35.4 %all-gather.8.cloned.1.call-done = bf16[512,1536]{1,0:T(8,128)(2,1)} async-done(((bf16[128,1536]{1,0:T(8,128)(2,1)}), bf16[512,1536]{1,0:T(8,128)(2,1)}) %all-gather.8.cloned.1.call-update) | async-done | bytes 1572880 | tf_op jit(solution)/shard_map/all_gather | solution.py:178
  86.4 15.6 all-gather.12.cloned.1.call-done
  109.2 11.3 reduce-window.6
  139.4 26.9 %reduce-scatter.10.cloned.1.call-done = f32[128,1536]{1,0:T(8,128)} async-done(((f32[512,1536]{1,0:T(8,128)}), f32[128,1536]{1,0:T(8,128)}) %reduce-scatter.10.cloned.1.call-update) | async-done | bytes 786448 | tf_op jit(solution)/shard_map/reduce_scatter | solution.py:203
  183.8 134.5 %all_to_all.60 = bf16[4,10,48,1536]{3,2,1,0:T(8,128)(2,1)} all-to-all(bf16[4,10,48,1536]{3,2,1,0:T(8,128)(2,1)S(1)} %get-tuple-element.80), channel_id=1, replica_groups=mesh['gx'=4,'gy'=8] {'gx'}, dimensions={0} | all-to-all | bytes 11796480 | tf_op jit(solution)/shard_map/all_to_all | solution.py:253
  329.2 123.5 %all-to-all-done = bf16[4,10,48,1536]{3,2,1,0:T(8,128)(2,1)} async-done(((bf16[4,10,48,1536]{3,2,1,0:T(8,128)(2,1)}), bf16[4,10,48,1536]{3,2,1,0:T(8,128)(2,1)}, u32[]{:S(2)}, u32[]{:S(2)}) %all-to-all-start) | async-done | bytes 5898272 | tf_op jit(solution)/shard_map/all_to_all | solution.py:216
  458.4 12.3 fusion.72
  470.8 12.3 fusion.71
  483.1 12.8 multiply_convert_fusion
  496.0 11.8 fusion.73
  507.8 13.7 fusion.4
  537.6 204.9 %all-to-all-done.3 = bf16[1,10,192,1536]{3,1,0,2:T(8,128)(2,1)} async-done(((bf16[1,10,192,1536]{3,1,0,2:T(8,128)(2,1)}), bf16[1,10,192,1536]{3,1,0,2:T(8,128)(2,1)}, u32[]{:S(2)}, u32[]{:S(2)}) %all-to-all-start.3) | async-done | bytes 5898272 | tf_op jit(solution)/shard_map/all_to_all | solution.py:276
  752.0 10.7 gather_fusion.3
  769.3 35.8 %all-gather.20.cloned.1.call-done = bf16[512,1536]{1,0:T(8,128)(2,1)} async-done(((bf16[128,1536]{1,0:T(8,128)(2,1)}), bf16[512,1536]{1,0:T(8,128)(2,1)}) %all-gather.20.cloned.1.call-update) | async-done | bytes 1572880 | tf_op jit(solution)/shard_map/all_gather | solution.py:288
  839.6 18.2 %fusion.77 = f32[10,512,1536]{1,2,0:T(8,128)} fusion(bf16[10,192,512]{2,1,0:T(8,128)(2,1)} %get-tuple-element.67, bf16[10,192,1536]{2,1,0:T(8,128)(2,1)} %bitcast.214), kind=kOutput, calls=%fused_computation.157 | convolution fusion | flops 3019898880 | bytes 39321600 | tf_op jit(solution)/shard_map/emf,emd->efd/dot_general | solution.py:264
  857.9 15.6 fusion.76
  875.0 15.7 fusion.75
  914.0 205.5 %all-to-all-done.1 = bf16[1,10,192,1536]{3,1,0,2:T(8,128)(2,1)} async-done(((bf16[1,10,192,1536]{3,1,0,2:T(8,128)(2,1)}), bf16[1,10,192,1536]{3,1,0,2:T(8,128)(2,1)}, u32[]{:S(2)}, u32[]{:S(2)}) %all-to-all-start.1) | async-done | bytes 5898272 | tf_op jit(solution)/shard_map/all_to_all | solution.py:232
  1128.9 10.8 gather_fusion.1
  1148.8 39.4 %all-reduce = (f32[1536]{0:T(1024)}, f32[1536]{0:T(1024)}) all-reduce(f32[1536]{0:T(1024)S(1)} %get-tuple-element.50, f32[1536]{0:T(1024)S(1)} %copy-done.34), channel_id=1, replica_groups=mesh['gx'=4,'gy'=8] {'gx','gy'}, use_global_device_ids=true, to_apply=%region_18.19 | all-reduce | flops 3072 | bytes 24576 | tf_op jit(solution)/shard_map/psum | solution.py:312
  1190.9 59.4 %reduce-scatter.26.cloned.1.call-done = f32[10,512,192]{1,2,0:T(8,128)} async-done(((f32[10,512,1536]{1,2,0:T(8,128)}), f32[10,512,192]{1,2,0:T(8,128)}) %reduce-scatter.26.cloned.1.call-update) | async-done | bytes 3932176 | tf_op jit(solution)/shard_map/reduce_scatter | solution.py:323
  1250.3 193.9 %reduce-scatter.24.cloned.1.call-done = f32[10,192,512]{2,1,0:T(8,128)} async-done(((f32[10,1536,512]{2,1,0:T(8,128)}), f32[10,192,512]{2,1,0:T(8,128)}) %reduce-scatter.24.cloned.1.call-update) | async-done | bytes 3932176 | tf_op jit(solution)/shard_map/reduce_scatter | solution.py:322
  1444.2 193.9 %reduce-scatter.22.cloned.1.call-done = f32[10,192,512]{2,1,0:T(8,128)} async-done(((f32[10,1536,512]{2,1,0:T(8,128)}), f32[10,192,512]{2,1,0:T(8,128)}) %reduce-scatter.22.cloned.1.call-update) | async-done | bytes 3932176 | tf_op jit(solution)/shard_map/reduce_scatter | solution.py:321
  (247 shorter events, 203.8 us)
Async XLA Ops:
  7.2 30.6 %all-gather.10.cloned.1.call-start = ((), (), s32[]{:S(2)}) async-start(), calls=%async_computation.14 | async-start | bytes 1327104 | tf_op jit(solution)/shard_map/all_gather | solution.py:167
  7.9 69.2 %all-gather.8.cloned.1.call-start = ((), (), s32[]{:S(2)}) async-start(), calls=%async_computation.13 | async-start | bytes 1966080 | tf_op jit(solution)/shard_map/all_gather | solution.py:178
  11.7 90.3 %all-gather.12.cloned.1.call-start = ((), (), s32[]{:S(2)}) async-start(), calls=%async_computation.15 | async-start | bytes 1327104 | tf_op jit(solution)/shard_map/all_gather | solution.py:170
  12.4 154.0 %reduce-scatter.10.cloned.1.call-start = ((), (), s32[]{:S(2)}) async-start(), calls=%async_computation.16 | async-start | bytes 3932160 | tf_op jit(solution)/shard_map/reduce_scatter | solution.py:203
  13.5 67.8 %copy-start.10 = (f32[512,32]{0,1:T(8,128)}, f32[512,32]{0,1:T(8,128)S(1)}, u32[]{:S(2)}) copy-start(f32[512,32]{0,1:T(8,128)S(1)} %get-tuple-element.86) | copy-start | bytes 196612
  106.0 352.4 %all-gather.16.cloned.1.call-start = ((), (), s32[]{:S(2)}) async-start(), calls=%async_computation.18 | async-start | bytes 17694720 | tf_op jit(solution)/shard_map/all_gather | solution.py:172
  106.6 364.2 %all-gather.14.cloned.1.call-start = ((), (), s32[]{:S(2)}) async-start(), calls=%async_computation.17 | async-start | bytes 17694720 | tf_op jit(solution)/shard_map/all_gather | solution.py:171
  107.2 376.0 %all-gather.18.cloned.1.call-start = ((), (), s32[]{:S(2)}) async-start(), calls=%async_computation.19 | async-start | bytes 17694720 | tf_op jit(solution)/shard_map/all_gather | solution.py:173
  167.8 599.8 %copy-start.42 = (f32[128]{0:T(128)}, f32[128]{0:T(128)S(1)}, u32[]{:S(2)}) copy-start(f32[128]{0:T(128)S(1)} %add_rsqrt_fusion) | copy-start | bytes 1540
  318.3 134.4 %all-to-all-start = ((bf16[4,10,48,1536]{3,2,1,0:T(8,128)(2,1)}), bf16[4,10,48,1536]{3,2,1,0:T(8,128)(2,1)}, u32[]{:S(2)}, u32[]{:S(2)}) async-start(bf16[4,10,48,1536]{3,2,1,0:T(8,128)(2,1)} %get-tuple-element.81), calls=%async_computation.1 | async-start | bytes 11796480 | tf_op jit(solution)/shard_map/all_to_all | solution.py:216
  531.5 211.0 %all-to-all-start.3 = ((bf16[1,10,192,1536]{3,1,0,2:T(8,128)(2,1)}), bf16[1,10,192,1536]{3,1,0,2:T(8,128)(2,1)}, u32[]{:S(2)}, u32[]{:S(2)}) async-start(bf16[1,10,192,1536]{3,1,0,2:T(8,128)(2,1)} %copy.82), calls=%async_computation.4 | async-start | bytes 18874368 | tf_op jit(solution)/shard_map/all_to_all | solution.py:276
  537.5 267.6 %all-gather.20.cloned.1.call-start = ((), (), s32[]{:S(2)}) async-start(), calls=%async_computation.20 | async-start | bytes 1966080 | tf_op jit(solution)/shard_map/all_gather | solution.py:288
  537.6 214.5 %copy-start.31 = (s32[1024]{0:T(1024)}, s32[1024]{0:T(1024)S(1)}, u32[]{:S(2)}) copy-start(s32[1024]{0:T(1024)S(1)} %broadcast_clamp_fusion) | copy-start | bytes 12292
  768.8 378.6 %reduce-scatter.12.cloned.1.call-start = ((), (), s32[]{:S(2)}) async-start(), calls=%async_computation.21 | async-start | bytes 3932160 | tf_op jit(solution)/shard_map/reduce_scatter | solution.py:307
  825.3 365.5 %reduce-scatter.18.cloned.1.call-start = ((), (), s32[]{:S(2)}) async-start(), calls=%async_computation.24 | async-start | bytes 884736 | tf_op jit(solution)/shard_map/reduce_scatter | solution.py:319
  831.4 359.4 %reduce-scatter.16.cloned.1.call-start = ((), (), s32[]{:S(2)}) async-start(), calls=%async_computation.23 | async-start | bytes 884736 | tf_op jit(solution)/shard_map/reduce_scatter | solution.py:318
  832.2 358.7 %reduce-scatter.20.cloned.1.call-start = ((), (), s32[]{:S(2)}) async-start(), calls=%async_computation.25 | async-start | bytes 2654208 | tf_op jit(solution)/shard_map/reduce_scatter | solution.py:320
  836.1 354.8 %reduce-scatter.14.cloned.1.call-start = ((), (), s32[]{:S(2)}) async-start(), calls=%async_computation.22 | async-start | bytes 2654208 | tf_op jit(solution)/shard_map/reduce_scatter | solution.py:317
  839.4 411.0 %reduce-scatter.26.cloned.1.call-start = ((), (), s32[]{:S(2)}) async-start(), calls=%async_computation.28 | async-start | bytes 35389440 | tf_op jit(solution)/shard_map/reduce_scatter | solution.py:323
  857.8 586.4 %reduce-scatter.24.cloned.1.call-start = ((), (), s32[]{:S(2)}) async-start(), calls=%async_computation.27 | async-start | bytes 35389440 | tf_op jit(solution)/shard_map/reduce_scatter | solution.py:322
  873.4 764.7 %reduce-scatter.22.cloned.1.call-start = ((), (), s32[]{:S(2)}) async-start(), calls=%async_computation.26 | async-start | bytes 35389440 | tf_op jit(solution)/shard_map/reduce_scatter | solution.py:321
  907.4 212.1 %all-to-all-start.1 = ((bf16[1,10,192,1536]{3,1,0,2:T(8,128)(2,1)}), bf16[1,10,192,1536]{3,1,0,2:T(8,128)(2,1)}, u32[]{:S(2)}, u32[]{:S(2)}) async-start(bf16[1,10,192,1536]{3,1,0,2:T(8,128)(2,1)} %copy.76), calls=%async_computation.2 | async-start | bytes 18874368 | tf_op jit(solution)/shard_map/all_to_all | solution.py:232
  1143.4 44.8 %copy-start.43 = (f32[128]{0:T(128)S(1)}, f32[128]{0:T(128)}, u32[]{:S(2)}) copy-start(f32[128]{0:T(128)} %copy-done.42) | copy-start | bytes 1540
  1143.4 44.8 %copy-start.47 = (f32[128]{0:T(128)S(1)}, f32[128]{0:T(128)}, u32[]{:S(2)}) copy-start(f32[128]{0:T(128)} %copy-done.46) | copy-start | bytes 1540
  (45 other events, 335.2 us)
Sparse Core Ops, SparseCore 0:
  9.9 27.8 all-gather.9
  39.9 37.1 all-gather.7
  79.0 22.9 all-gather.11
  106.1 60.2 reduce-scatter.9
  168.1 85.4 all-gather.15
  255.4 85.4 all-gather.13
  342.7 85.4 all-gather.17
  768.9 36.1 all-gather.19
  825.4 59.1 reduce-scatter.11
  888.2 35.0 reduce-scatter.17
  927.0 34.9 reduce-scatter.15
  965.8 42.4 reduce-scatter.19
  1012.5 42.4 reduce-scatter.13
  1059.1 191.1 reduce-scatter.25
  1254.4 189.8 reduce-scatter.23
  1448.3 189.7 reduce-scatter.21
where the time goes:
time: 1650 us; the launch traced here: 1640 us
  waiting for transfers between devices  1100 us (67%)
  blocking collectives  196 us (12%)
  matrix products  163 us (10%)
  local copies, waits for them, and re-layouts  111 us (7%)
  other arithmetic  40.1 us (2%)
  starting transfers between devices  18.9 us (1%)
    all_to_all x1, waiting for transfers between devices, local(): lax.all_to_all(produced.reshape(1, local_experts, slots_all, width), 'gx'...  205 us
    all_to_all x1, waiting for transfers between devices, local(): lax.all_to_all(rows_back.reshape(1, local_experts, slots_all, width), 'gx...  205 us
    reduce_scatter x1, waiting for transfers between devices, local(): lax.psum_scatter(up_grad, 'gy', scatter_dimension=1, tiled=True)  194 us
    reduce_scatter x1, waiting for transfers between devices, local(): lax.psum_scatter(gate_grad, 'gy', scatter_dimension=1, tiled=True)  194 us
    all_to_all x1, blocking collectives, local(): lax.all_to_all(back_send.reshape(groups, local_experts, CAP, width), 'gx'...  134 us
    all_to_all x1, waiting for transfers between devices, local(): lax.all_to_all(send.reshape(groups, local_experts, CAP, width), 'gx', spl...  124 us
    reduce_scatter x1, waiting for transfers between devices, local(): lax.psum_scatter(down_grad, 'gy', scatter_dimension=2, tiled=True)  59.4 us
    psum x1, blocking collectives, local(): gain_one, gain_two = lax.psum((first_part, second_part), ('gx', 'gy'))  39.4 us
  transfers between devices with their start and end apart: 19, of which 11 were waited for; matrix products, arithmetic and copies ran while one was open for 13% of the time, Pallas kernels for 0%

commit v1 on v0

v1 whole, which is shorter than its diff:
```python
import jax
import jax.numpy as jnp
import numpy as np
from jax import lax
from jax.sharding import Mesh, PartitionSpec as P

HEAD_SIZE = 64
EXPERTS = 40
TOPK = 8

epsilon = 1e-06
rope_base = 10000.0
residual_factor = 0.22
score_factor = 0.015625
masked_value = -1e30

f32 = jnp.float32
bf16 = jnp.bfloat16


def swap(value, axis, step):
    count = lax.axis_size(axis)
    return lax.ppermute(value, axis, [(i, i ^ step) for i in range(count)])


def after(value, *others):
    return lax.optimization_barrier((value,) + others)[0]


def pick(array, index, dim):
    return lax.dynamic_index_in_dim(array, index, dim, keepdims=False)


def rms_factor(rows):
    return lax.rsqrt(jnp.mean(rows * rows, axis=-1, keepdims=True) + epsilon)


def norm_back(rows, factor, gain, upstream):
    scaled = upstream * gain
    inner = jnp.mean(scaled * rows, axis=-1, keepdims=True)
    return factor * scaled - rows * factor * factor * factor * inner


def rotary(rows, cosine, sine):
    half = rows.shape[-1] // 2
    first = rows[..., :half]
    second = rows[..., half:]
    return jnp.concatenate(
        [first * cosine - second * sine, first * sine + second * cosine], axis=-1
    )


def contract_rows(left, right):
    return lax.dot_general(left, right, (((0,), (0,)), ((), ())), preferred_element_type=f32)


def contract_cols(left, right):
    return lax.dot_general(left, right, (((1,), (1,)), ((), ())), preferred_element_type=f32)


def gather_gx(block):
    return [block] + [swap(block, "gx", s) for s in range(1, lax.axis_size("gx"))]


def scatter_gx(blocks):
    total = blocks[0].astype(f32)
    for s in range(1, len(blocks)):
        total = total + swap(blocks[s].astype(bf16), "gx", s).astype(f32)
    return total


def gather_gy(block):
    parts = [block, swap(block, "gw", 1)]
    for s in range(1, lax.axis_size("gt")):
        parts = parts + [swap(p, "gt", s) for p in parts[:2]]
    parts = [q for p in parts for q in (p, swap(p, "co", 1))]
    me = (lax.axis_index("gt") * 2 + lax.axis_index("gw")) * 2 + lax.axis_index("co")
    stacked = jnp.stack(parts)
    return jnp.concatenate([lax.dynamic_index_in_dim(stacked, j ^ me, 0) for j in range(len(parts))])


def gather_halves(weight):
    side = lax.axis_index("gw")
    half = weight.shape[2] // 2
    keep = lax.dynamic_slice_in_dim(weight, side * half, half, 2)
    give = lax.dynamic_slice_in_dim(weight, (1 - side) * half, half, 2)
    parts = [keep, swap(give, "gw", 1)]
    for s in range(1, lax.axis_size("gt")):
        parts = parts + [swap(p, "gt", s) for p in parts[:2]]
    parts = [q for p in parts for q in (p, swap(p, "co", 1))]
    me = (lax.axis_index("gt") * 2 + side) * 2 + lax.axis_index("co")
    stacked = jnp.stack(parts, axis=1)
    ordered = jnp.concatenate(
        [lax.dynamic_index_in_dim(stacked, j ^ me, 1) for j in range(len(parts))], axis=1
    )
    return ordered.reshape(weight.shape[0], -1, half)


def scatter_halves(grad):
    many = lax.axis_size("gt")
    t, w, k = lax.axis_index("gt"), lax.axis_index("gw"), lax.axis_index("co")
    experts, _, half = grad.shape
    grad = grad.reshape(experts, many * 2, 2, -1, half)
    total = pick(grad, k, 2).astype(f32) + swap(pick(grad, 1 - k, 2), "co", 1).astype(f32)
    total = total.astype(bf16).reshape(experts, many, 2, -1, half)
    own = pick(total, t, 1).astype(f32)
    for s in range(1, many):
        own = own + swap(pick(total, t ^ s, 1), "gt", s).astype(f32)
    mine = pick(own, w, 1)
    other = swap(pick(own, 1 - w, 1).astype(bf16), "gw", 1).astype(f32)
    low = jnp.where(w == 0, mine, other)
    high = jnp.where(w == 0, other, mine)
    return jnp.concatenate([low, high], axis=2)


def scatter_gy(grad):
    many = lax.axis_size("gt")
    t, w, k = lax.axis_index("gt"), lax.axis_index("gw"), lax.axis_index("co")
    cols = grad.shape[1]
    grad = grad.reshape(many * 2, 2, -1, cols)
    total = pick(grad, k, 1).astype(f32) + swap(pick(grad, 1 - k, 1), "co", 1).astype(f32)
    total = total.astype(bf16).reshape(many, 2, -1, cols)
    own = pick(total, t, 0).astype(f32)
    for s in range(1, many):
        own = own + swap(pick(total, t ^ s, 0), "gt", s).astype(f32)
    own = own.astype(bf16)
    return pick(own, w, 0).astype(f32) + swap(pick(own, 1 - w, 0), "gw", 1).astype(f32)


def block_scores(query_rows, key_rows, positions):
    raw = jnp.einsum("qhgd,khd->hgqk", query_rows, key_rows, preferred_element_type=f32)
    return jnp.where(positions[None, :] <= positions[:, None], raw * score_factor, masked_value)


def attend_forward(query_rows, key_rows, value_rows, positions):
    scores = block_scores(query_rows, key_rows, positions)
    top = jnp.max(scores, axis=-1, keepdims=True)
    weights = jnp.exp(scores - top)
    total = jnp.sum(weights, axis=-1, keepdims=True)
    probs = (weights / total).astype(bf16)
    mixed = jnp.einsum("hgqk,khd->qhgd", probs, value_rows, preferred_element_type=f32)
    return (mixed.astype(bf16).reshape(query_rows.shape[0], -1), top + jnp.log(total))


def attend_backward(query_rows, key_rows, value_rows, heads_back, spread, positions):
    scores = block_scores(query_rows, key_rows, positions)
    probs = jnp.exp(scores - spread)
    prob_back = jnp.einsum("qhgd,khd->hgqk", heads_back, value_rows, preferred_element_type=f32)
    inner = jnp.sum(probs * prob_back, axis=-1, keepdims=True)
    score_back = (probs * (prob_back - inner)).astype(bf16)
    query_back = jnp.einsum("hgqk,khd->qhgd", score_back, key_rows, preferred_element_type=f32)
    key_back = jnp.einsum("hgqk,qhgd->khd", score_back, query_rows, preferred_element_type=f32)
    value_back = jnp.einsum(
        "hgqk,qhgd->khd", probs.astype(bf16), heads_back, preferred_element_type=f32
    )
    return (query_back * score_factor, key_back * score_factor, value_back)


def local(
    tokens,
    first_gain,
    query_weight,
    key_matrix,
    value_matrix,
    out_weight,
    second_gain,
    gate_weight,
    up_weight,
    down_weight,
    routes,
    route_logits,
    cotangent,
):
    groups = lax.axis_size("gx")
    me_x = lax.axis_index("gx")
    own_tokens = tokens[0]
    rows, width = own_tokens.shape
    query_cols = query_weight.shape[1]
    key_cols = key_matrix.shape[1]
    query_heads = query_cols // HEAD_SIZE
    pair_heads = key_cols // HEAD_SIZE
    ratio = query_heads // pair_heads

    token_blocks = gather_gx(own_tokens)
    attention = jnp.concatenate(
        [query_weight, key_matrix, value_matrix, out_weight.T], axis=1
    )
    attention_full = gather_gy(attention).reshape(width, -1)
    joined = attention_full[:, : query_cols + 2 * key_cols]
    out_full = attention_full[:, query_cols + 2 * key_cols :]

    gate_full = gather_halves(after(gate_weight, attention_full))
    up_full = gather_halves(after(up_weight, attention_full))
    down_full = gather_halves(jnp.swapaxes(after(down_weight, attention_full), 1, 2))

    logits = route_logits[0]
    weights = jnp.exp(logits - jnp.max(logits, axis=-1, keepdims=True))
    chance = weights / jnp.sum(weights, axis=-1, keepdims=True)
    routing = jnp.concatenate([routes[0].astype(f32), chance], axis=1)

    def gather_tokens(block):
        parts = gather_gx(block)
        return jnp.concatenate(parts + [swap(p, "gw", 1) for p in parts], axis=0)

    cotangent_rows = gather_tokens(after(cotangent[0], token_blocks[groups - 1]))
    routing_rows = gather_tokens(after(routing, token_blocks[groups - 1]))

    sequence = jnp.concatenate(token_blocks, axis=0).astype(f32)
    length = sequence.shape[0]
    factor_all = rms_factor(sequence)
    sequence_rows = (sequence * factor_all * first_gain).astype(bf16)
    projected = jnp.dot(sequence_rows, joined, preferred_element_type=f32)
    positions = jnp.concatenate(
        [(me_x ^ s) * rows + jnp.arange(rows, dtype=jnp.int32) for s in range(groups)]
    )
    half = HEAD_SIZE // 2
    freq = rope_base ** (-(jnp.arange(half, dtype=f32) * 2.0 / HEAD_SIZE))
    angle = positions.astype(f32)[:, None] * freq[None, :]
    cosine = jnp.cos(angle)[:, None, :]
    sine = jnp.sin(angle)[:, None, :]
    query_rows = rotary(projected[:, :query_cols].reshape(length, query_heads, HEAD_SIZE), cosine, sine)
    query_rows = query_rows.astype(bf16).reshape(length, pair_heads, ratio, HEAD_SIZE)
    key_rows = rotary(
        projected[:, query_cols : query_cols + key_cols].reshape(length, pair_heads, HEAD_SIZE),
        cosine,
        sine,
    ).astype(bf16)
    value_rows = (
        projected[:, query_cols + key_cols :].reshape(length, pair_heads, HEAD_SIZE).astype(bf16)
    )
    heads, spread = attend_forward(query_rows, key_rows, value_rows, positions)
    branch_parts = contract_cols(heads, out_full).astype(bf16)
    branch = scatter_gx([branch_parts[s * rows : (s + 1) * rows] for s in range(groups)])

    hidden = own_tokens.astype(f32)
    middle = hidden + residual_factor * branch
    factor_two = rms_factor(middle)
    normed_two = (middle * factor_two * second_gain).astype(bf16)
    normed_rows = gather_tokens(normed_two)

    experts = gate_weight.shape[0]
    first_expert = me_x * experts
    ids = (first_expert + jnp.arange(experts, dtype=jnp.int32)).astype(f32)
    same = routing_rows[None, :, :TOPK] == ids[:, None, None]
    chosen = jnp.sum(jnp.where(same, routing_rows[None, :, TOPK:], 0.0), axis=2)[:, :, None]
    back = jnp.einsum("td,edf->etf", cotangent_rows, down_full, preferred_element_type=f32)
    gate = jnp.einsum("td,edf->etf", normed_rows, gate_full, preferred_element_type=f32)
    upper = jnp.einsum("td,edf->etf", normed_rows, up_full, preferred_element_type=f32)
    sigma = jax.nn.sigmoid(gate)
    active = gate * sigma * upper
    back = back * residual_factor
    chance_part = jnp.sum(active * back, axis=2)
    scaled = (active * chosen).astype(bf16)
    active_back = back * chosen
    gate_back = (active_back * upper * sigma * (1.0 + gate * (1.0 - sigma))).astype(bf16)
    upper_back = (active_back * gate * sigma).astype(bf16)

    rows_back = jnp.einsum("etf,edf->td", gate_back, gate_full, preferred_element_type=f32)
    rows_back = rows_back + jnp.einsum("etf,edf->td", upper_back, up_full, preferred_element_type=f32)
    rows_back = rows_back.astype(bf16)

    def scatter_tokens(parts, kind):
        cut = [parts[s * rows : (s + 1) * rows] for s in range(2 * groups)]
        own = [
            cut[s].astype(f32) + swap(cut[groups + s], "gw", 1).astype(f32) for s in range(groups)
        ]
        total = own[0]
        for s in range(1, groups):
            total = total + swap(own[s].astype(kind), "gx", s).astype(f32)
        return total

    normed_two_back = scatter_tokens(rows_back, bf16)

    mixed_parts = jnp.einsum("etf,edf->td", scaled, down_full, preferred_element_type=f32)
    mixed = scatter_tokens(mixed_parts.astype(bf16), bf16)
    output = (middle + residual_factor * mixed).astype(bf16)
    chance_rows = jnp.sum(jnp.where(same, chance_part[:, :, None], 0.0), axis=0)
    chance_back = scatter_tokens(chance_rows, f32)
    logit_back = chance * (chance_back - jnp.sum(chance * chance_back, axis=-1, keepdims=True))

    gate_grad = jnp.einsum("td,etf->edf", normed_rows, gate_back, preferred_element_type=f32)
    up_grad = jnp.einsum("td,etf->edf", normed_rows, upper_back, preferred_element_type=f32)
    down_grad = jnp.einsum("td,etf->edf", cotangent_rows, scaled, preferred_element_type=f32)
    gate_sum = scatter_halves(gate_grad.astype(bf16))
    up_sum = scatter_halves(up_grad.astype(bf16))
    down_sum = scatter_halves((residual_factor * down_grad).astype(bf16))

    upstream = cotangent[0].astype(f32)
    middle_back = upstream + norm_back(middle, factor_two, second_gain, normed_two_back)
    second_part = jnp.sum(normed_two_back * middle * factor_two, axis=0)
    branch_back = (residual_factor * middle_back).astype(bf16)
    piece = jnp.concatenate(gather_gx(branch_back), axis=0)
    heads_back = jnp.dot(piece, out_full, preferred_element_type=f32)
    out_grad = contract_rows(piece, heads)
    heads_back = heads_back.astype(bf16).reshape(length, pair_heads, ratio, HEAD_SIZE)
    query_back, key_back, value_back = attend_backward(
        query_rows, key_rows, value_rows, heads_back, spread, positions
    )
    query_back = rotary(query_back.reshape(length, query_heads, HEAD_SIZE), cosine, -sine)
    key_back = rotary(key_back, cosine, -sine)
    projected_back = jnp.concatenate(
        [
            query_back.reshape(length, query_cols),
            key_back.reshape(length, key_cols),
            value_back.reshape(length, key_cols),
        ],
        axis=1,
    ).astype(bf16)
    normed_one_parts = contract_cols(projected_back, joined)
    first_part = jnp.sum(normed_one_parts * (sequence * factor_all), axis=0)
    normed_one_back = scatter_gx(
        [normed_one_parts[s * rows : (s + 1) * rows] for s in range(groups)]
    )
    tokens_back = middle_back + norm_back(hidden, factor_all[:rows], first_gain, normed_one_back)
    gains = lax.psum(jnp.stack([first_part, second_part]), ("gx", "gt", "gw", "co"))
    joined_grad = contract_rows(sequence_rows, projected_back)
    attention_sum = scatter_gy(jnp.concatenate([joined_grad, out_grad], axis=1).astype(bf16))
    return (
        output[None],
        tokens_back[None],
        gains[0],
        attention_sum[:, :query_cols],
        attention_sum[:, query_cols : query_cols + key_cols],
        attention_sum[:, query_cols + key_cols : query_cols + 2 * key_cols],
        attention_sum[:, query_cols + 2 * key_cols :].T,
        gains[1],
        gate_sum,
        up_sum,
        jnp.swapaxes(down_sum, 1, 2),
        logit_back[None],
    )


def solution(mesh):
    groups, others = mesh.shape["gx"], mesh.shape["gy"]
    split = Mesh(mesh.devices.reshape(groups, others // 4, 2, 2), ("gx", "gt", "gw", "co"))
    gy = ("gt", "gw", "co")
    in_specs = (
        P(gy, "gx", None),
        P(),
        P(gy, "gx"),
        P(gy, "gx"),
        P(gy, "gx"),
        P("gx", gy),
        P(),
        P("gx", gy, None),
        P("gx", gy, None),
        P("gx", None, gy),
        P(gy, "gx", None),
        P(gy, "gx", None),
        P(gy, "gx", None),
    )
    out_specs = (
        P(gy, "gx", None),
        P(gy, "gx", None),
        P(),
        P(gy, "gx"),
        P(gy, "gx"),
        P(gy, "gx"),
        P("gx", gy),
        P(),
        P("gx", gy, None),
        P("gx", gy, None),
        P("gx", None, gy),
        P(gy, "gx", None),
    )
    return jax.shard_map(local, mesh=split, in_specs=in_specs, out_specs=out_specs, check_vma=False)
```

time: 1650 us -> 932 us (0.56)
  waiting for transfers between devices: 1100 us -> 433 us
  blocking collectives: 196 us -> 59 us
  starting transfers between devices: 18.9 us -> 110 us
  other arithmetic: 40.1 us -> 68.2 us
  matrix products: 163 us -> 144 us
    all_to_all x3 -> x0, waiting for transfers between devices: 534 us -> none  [the longest x1 205 us: local(): lax.all_to_all(produced.reshape(1, local_experts, slots_all, width), 'gx'...]
    reduce_scatter x9 -> x0, waiting for transfers between devices: 474 us -> none  [the longest x1 194 us: local(): lax.psum_scatter(up_grad, 'gy', scatter_dimension=1, tiled=True)]
    ppermute x0 -> x94, waiting for transfers between devices: none -> 433 us  [swap(): return lax.ppermute(value, axis, [(i, i ^ step) for i in range(count)])]
    all_to_all x1 -> x0, blocking collectives: 134 us -> none  [local(): lax.all_to_all(back_send.reshape(groups, local_experts, CAP, width), 'gx'...]
    ppermute x0 -> x94, starting transfers between devices: none -> 110 us  [swap(): return lax.ppermute(value, axis, [(i, i ^ step) for i in range(count)])]
    all_gather x7 -> x0, waiting for transfers between devices: 88.9 us -> none  [the longest x1 35.8 us: local(): piece = lax.all_gather(branch_back, 'gx', axis=0, tiled=True)]
    gather x4 -> x0, local copies, waits for them, and re-layouts: 37.1 us -> none  [the longest x1 10.8 us: local(): returned.reshape(-1, width)[target].reshape(local_rows, TOPK, width)]
    convert_element_type x0 -> x6, local copies, waits for them, and re-layouts: none -> 32.6 us  [the longest x1 10.8 us: local(): down_sum = scatter_halves((residual_factor * down_grad).astype(bf16))]
  transfers between devices with their start and end apart: 19 -> 94, of which waited for: 11 -> 34; matrix products, arithmetic and copies ran while one was open for 13% -> 20% of each run, Pallas kernels for 0% -> 0%
where the time goes in v1:
time: 932 us; the launch traced here: 922 us
  waiting for transfers between devices  433 us (46%)
  matrix products  144 us (15%)
  starting transfers between devices  110 us (12%)
  local copies, waits for them, and re-layouts  106 us (11%)
  other arithmetic  68.2 us (7%)
  blocking collectives  59 us (6%)
    ppermute x94, waiting for transfers between devices, swap(): return lax.ppermute(value, axis, [(i, i ^ step) for i in range(count)])  433 us
    ppermute x94, starting transfers between devices, swap(): return lax.ppermute(value, axis, [(i, i ^ step) for i in range(count)])  110 us
    psum x1, blocking collectives, local(): lax.psum(jnp.stack([first_part, second_part]), ('gx', 'gt', 'gw', 'co'))  59 us
    unnamed x310, local copies, waits for them, and re-layouts  32.5 us
    dot_general x1, matrix products, local(): jnp.einsum('td,edf->etf', cotangent_rows, down_full, preferred_element_ty...  18.7 us
  transfers between devices with their start and end apart: 94, of which 34 were waited for; matrix products, arithmetic and copies ran while one was open for 20% of the time, Pallas kernels for 0%

profile of v1, /device:TPU:0, one launch (start us, length us, event | category | flops | bytes accessed | tf_op | source)
XLA Modules:
  0.0 922.1 jit_solution(3968512727264437386)
XLA Ops:
  22.1 20.7 %collective-permute-done.1 = bf16[128,1536]{1,0:T(8,128)(2,1)S(1)} collective-permute-done((bf16[128,1536]{1,0:T(8,128)(2,1)}, bf16[128,1536]{1,0:T(8,128)(2,1)S(1)}, u32[]{:S(2)}, u32[]{:S(2)}) %collective-permute-start.1) | collective-permute-done | bytes 393248 | tf_op jit(solution)/shard_map/ppermute | solution.py:23
  73.0 15.0 %collective-permute-done.56 = bf16[128,1536]{1,0:T(8,128)(2,1)S(1)} collective-permute-done((bf16[128,1536]{1,0:T(8,128)(2,1)S(1)}, bf16[128,1536]{1,0:T(8,128)(2,1)S(1)}, u32[]{:S(2)}, u32[]{:S(2)}) %collective-permute-start.56) | collective-permute-done | bytes 393248 | tf_op jit(solution)/shard_map/ppermute | solution.py:23
  126.2 16.9 %collective-permute-done.11 = bf16[128,1536]{1,0:T(8,128)(2,1)S(1)} collective-permute-done((bf16[128,1536]{1,0:T(8,128)(2,1)S(1)}, bf16[128,1536]{1,0:T(8,128)(2,1)S(1)}, u32[]{:S(2)}, u32[]{:S(2)}) %collective-permute-start.11) | collective-permute-done | bytes 393248 | tf_op jit(solution)/shard_map/ppermute | solution.py:23
  149.8 13.1 %collective-permute-done.20 = bf16[128,1536]{1,0:T(8,128)(2,1)S(1)} collective-permute-done((bf16[128,1536]{1,0:T(8,128)(2,1)S(1)}, bf16[128,1536]{1,0:T(8,128)(2,1)S(1)}, u32[]{:S(2)}, u32[]{:S(2)}) %collective-permute-start.20) | collective-permute-done | bytes 393248 | tf_op jit(solution)/shard_map/ppermute | solution.py:23
  183.1 20.7 %collective-permute-done.14 = bf16[10,192,256]{2,1,0:T(8,128)(2,1)S(1)} collective-permute-done((bf16[10,192,256]{2,1,0:T(8,128)(2,1)S(1)}, bf16[10,192,256]{2,1,0:T(8,128)(2,1)S(1)}, u32[]{:S(2)}, u32[]{:S(2)}) %collective-permute-start.14) | collective-permute-done | bytes 983072 | tf_op jit(solution)/shard_map/ppermute | solution.py:23
  206.0 18.8 %collective-permute-done.28 = bf16[10,192,256]{2,1,0:T(8,128)(2,1)S(1)} collective-permute-done((bf16[10,192,256]{2,1,0:T(8,128)(2,1)S(1)}, bf16[10,192,256]{2,1,0:T(8,128)(2,1)S(1)}, u32[]{:S(2)}, u32[]{:S(2)}) %collective-permute-start.28) | collective-permute-done | bytes 983072 | tf_op jit(solution)/shard_map/ppermute | solution.py:23
  224.9 21.9 %collective-permute-done.24 = bf16[128,1536]{1,0:T(8,128)(2,1)S(1)} collective-permute-done((bf16[128,1536]{1,0:T(8,128)(2,1)S(1)}, bf16[128,1536]{1,0:T(8,128)(2,1)S(1)}, u32[]{:S(2)}, u32[]{:S(2)}) %collective-permute-start.24) | collective-permute-done | bytes 393248 | tf_op jit(solution)/shard_map/ppermute | solution.py:23
  251.0 20.5 %collective-permute-done.16 = bf16[10,192,256]{2,1,0:T(8,128)(2,1)S(1)} collective-permute-done((bf16[10,192,256]{2,1,0:T(8,128)(2,1)S(1)}, bf16[10,192,256]{2,1,0:T(8,128)(2,1)S(1)}, u32[]{:S(2)}, u32[]{:S(2)}) %collective-permute-start.16) | collective-permute-done | bytes 983072 | tf_op jit(solution)/shard_map/ppermute | solution.py:23
  273.0 19.5 %collective-permute-done.30 = bf16[10,192,256]{2,1,0:T(8,128)(2,1)S(1)} collective-permute-done((bf16[10,192,256]{2,1,0:T(8,128)(2,1)S(1)}, bf16[10,192,256]{2,1,0:T(8,128)(2,1)S(1)}, u32[]{:S(2)}, u32[]{:S(2)}) %collective-permute-start.30) | collective-permute-done | bytes 983072 | tf_op jit(solution)/shard_map/ppermute | solution.py:23
  294.9 18.7 %collective-permute-done.46 = bf16[10,192,256]{2,1,0:T(8,128)(2,1)S(1)} collective-permute-done((bf16[10,192,256]{2,1,0:T(8,128)(2,1)S(1)}, bf16[10,192,256]{2,1,0:T(8,128)(2,1)S(1)}, u32[]{:S(2)}, u32[]{:S(2)}) %collective-permute-start.46) | collective-permute-done | bytes 983072 | tf_op jit(solution)/shard_map/ppermute | solution.py:23
  313.7 21.0 %collective-permute-done.32 = bf16[10,192,256]{2,1,0:T(8,128)(2,1)S(1)} collective-permute-done((bf16[10,192,256]{2,1,0:T(8,128)(2,1)S(1)}, bf16[10,192,256]{2,1,0:T(8,128)(2,1)S(1)}, u32[]{:S(2)}, u32[]{:S(2)}) %collective-permute-start.32) | collective-permute-done | bytes 983072 | tf_op jit(solution)/shard_map/ppermute | solution.py:23
  334.7 16.9 %collective-permute-done.18 = bf16[10,192,256]{2,1,0:T(8,128)(2,1)S(1)} collective-permute-done((bf16[10,192,256]{2,1,0:T(8,128)(2,1)S(1)}, bf16[10,192,256]{2,1,0:T(8,128)(2,1)S(1)}, u32[]{:S(2)}, u32[]{:S(2)}) %collective-permute-start.18) | collective-permute-done | bytes 983072 | tf_op jit(solution)/shard_map/ppermute | solution.py:23
  378.2 13.8 %fusion.35 = f32[10,256,1024]{2,1,0:T(8,128)} fusion(bf16[10,1536,256]{2,1,0:T(8,128)(2,1)S(1)} %bitcast.434, bf16[1024,1536]{1,0:T(8,128)(2,1)} %copy-done.80), kind=kOutput, calls=%fused_computation.73 | convolution fusion | flops 8053063680 | bytes 21495808 | tf_op jit(solution)/shard_map/td,edf->etf/dot_general | solution.py:247
  403.0 18.7 %fusion = (f32[10,1024]{1,0:T(8,128)S(1)}, f32[10,256,1024]{2,1,0:T(8,128)}) fusion(f32[10,256,1024]{2,1,0:T(8,128)} %fusion.33, f32[10,256,1024]{2,1,0:T(8,128)} %fusion.35, bf16[10,1536,256]{2,1,0:T(8,128)(2,1)S(1)} %bitcast.397, bf16[1024,1536]{1,0:T(8,128)(2,1)} %constant_dynamic-update-slice_fusion.16), kind=kOutput, calls=%fused_computation.2 | convolution fusion | flops 8074024960 | bytes 42508288 | tf_op jit(solution)/shard_map/td,edf->etf/dot_general | solution.py:246
  421.9 16.3 %bitcast_convert_fusion = bf16[1024,1536]{1,0:T(8,128)(2,1)} fusion(bf16[10,1536,256]{2,1,0:T(8,128)(2,1)} %bitcast.394, f32[10,1024]{1,0:T(8,128)S(1)} %get-tuple-element.25, f32[10,256,1024]{2,1,0:T(8,128)} %fusion.33, f32[10,256,1024]{2,1,0:T(8,128)} %fusion.35), kind=kOutput, calls=%fused_computation.34 | convolution fusion | flops 8072986624 | bytes 32022528 | tf_op jit(solution)/shard_map/etf,edf->td/dot_general | solution.py:274
  438.3 16.2 %fusion.18 = bf16[10,1536,256]{1,2,0:T(8,128)(2,1)} fusion(bf16[1024,1536]{1,0:T(8,128)(2,1)} %constant_dynamic-update-slice_fusion.16, f32[10,1024]{1,0:T(8,128)S(1)} %get-tuple-element.25, f32[10,256,1024]{2,1,0:T(8,128)} %fusion.33, f32[10,256,1024]{2,1,0:T(8,128)} %fusion.35), kind=kOutput, calls=%fused_computation.40 | convolution fusion | flops 8079278080 | bytes 32022528 | tf_op jit(solution)/shard_map/td,etf->edf/dot_general | solution.py:283
  466.6 14.2 %fusion.101 = f32[1024,1536,1]{1,0,2:T(8,128)} fusion(bf16[10,1024,256]{1,2,0:T(8,128)(2,1)} %get-tuple-element.40, bf16[10,1536,256]{2,1,0:T(8,128)(2,1)} %bitcast.435), kind=kOutput, calls=%fused_computation.322 | convolution fusion | flops 8053063680 | bytes 19398656 | tf_op jit(solution)/shard_map/etf,edf->td/dot_general | solution.py:258
  614.0 18.2 %collective-permute-done.70 = bf16[128,1536]{1,0:T(8,128)(2,1)S(1)} collective-permute-done((bf16[128,1536]{1,0:T(8,128)(2,1)S(1)}, bf16[128,1536]{1,0:T(8,128)(2,1)S(1)}, u32[]{:S(2)}, u32[]{:S(2)}) %collective-permute-start.70) | collective-permute-done | bytes 393248 | tf_op jit(solution)/shard_map/ppermute | solution.py:23
  671.4 13.3 %collective-permute-done.72 = bf16[128,1536]{1,0:T(8,128)(2,1)S(1)} collective-permute-done((bf16[128,1536]{1,0:T(8,128)(2,1)S(1)}, bf16[128,1536]{1,0:T(8,128)(2,1)S(1)}, u32[]{:S(2)}, u32[]{:S(2)}) %collective-permute-start.72) | collective-permute-done | bytes 393248 | tf_op jit(solution)/shard_map/ppermute | solution.py:23
  689.1 59.0 %psum.7 = f32[2,1536]{1,0:T(2,128)S(1)} all-reduce(f32[2,1536]{1,0:T(2,128)S(1)} %pad_maximum_fusion.14), channel_id=1, replica_groups=mesh['gx'=4,'gt'=2,'gw'=2,'co'=2] {'gx','gt','gw','co'}, use_global_device_ids=true, to_apply=%region_12.13 | all-reduce | flops 3072 | bytes 24576 | tf_op jit(solution)/shard_map/psum | solution.py:315
  796.7 21.1 %collective-permute-done.85 = bf16[10,2,192,256]{3,2,0,1:T(8,128)(2,1)} collective-permute-done((bf16[10,2,192,256]{3,2,0,1:T(8,128)(2,1)}, bf16[10,2,192,256]{3,2,0,1:T(8,128)(2,1)}, u32[]{:S(2)}, u32[]{:S(2)}) %collective-permute-start.85) | collective-permute-done | bytes 1966112 | tf_op jit(solution)/shard_map/ppermute | solution.py:23
  820.1 39.7 %collective-permute-done.79 = bf16[10,2,192,256]{3,2,0,1:T(8,128)(2,1)S(1)} collective-permute-done((bf16[10,2,192,256]{3,2,0,1:T(8,128)(2,1)S(1)}, bf16[10,2,192,256]{3,2,0,1:T(8,128)(2,1)S(1)}, u32[]{:S(2)}, u32[]{:S(2)}) %collective-permute-start.79) | collective-permute-done | bytes 1966112 | tf_op jit(solution)/shard_map/ppermute | solution.py:23
  860.7 37.5 %collective-permute-done.82 = bf16[10,2,192,256]{3,2,0,1:T(8,128)(2,1)S(1)} collective-permute-done((bf16[10,2,192,256]{3,2,0,1:T(8,128)(2,1)S(1)}, bf16[10,2,192,256]{3,2,0,1:T(8,128)(2,1)S(1)}, u32[]{:S(2)}, u32[]{:S(2)}) %collective-permute-start.82) | collective-permute-done | bytes 1966112 | tf_op jit(solution)/shard_map/ppermute | solution.py:23
  905.3 13.5 %collective-permute-done.83 = bf16[10,192,256]{2,1,0:T(8,128)(2,1)S(1)} collective-permute-done((bf16[10,192,256]{2,1,0:T(8,128)(2,1)S(1)}, bf16[10,192,256]{2,1,0:T(8,128)(2,1)S(1)}, u32[]{:S(2)}, u32[]{:S(2)}) %collective-permute-start.83) | collective-permute-done | bytes 983072 | tf_op jit(solution)/shard_map/ppermute | solution.py:23
  (614 shorter events, 413.5 us)
Async XLA Ops:
  1.8 45.6 %collective-permute-start.4 = (bf16[192,1024]{1,0:T(8,128)(2,1)S(1)}, bf16[192,1024]{1,0:T(8,128)(2,1)S(1)}, u32[]{:S(2)}, u32[]{:S(2)}) collective-permute-start(bf16[192,1024]{1,0:T(8,128)(2,1)S(1)} %pad_maximum_fusion.5), channel_id=1, source_target_pairs={{0,2},{2,0},{1,3},{3,1},{4,6},{6,4},{5,7},{7,5},{8,10},{10,8},{9,1... | collective-permute-start | bytes 1179656 | tf_op jit(solution)/shard_map/ppermute | solution.py:23
  18.9 52.4 %collective-permute-start.6 = (bf16[192,1024]{1,0:T(8,128)(2,1)S(1)}, bf16[192,1024]{1,0:T(8,128)(2,1)S(1)}, u32[]{:S(2)}, u32[]{:S(2)}) collective-permute-start(bf16[192,1024]{1,0:T(8,128)(2,1)S(1)} %pad_maximum_fusion.5), channel_id=1, source_target_pairs={{0,4},{4,0},{1,5},{5,1},{2,6},{6,2},{3,7},{7,3},{8,12},{12,8},{9,1... | collective-permute-start | bytes 1179656 | tf_op jit(solution)/shard_map/ppermute | solution.py:23
  119.2 61.4 %collective-permute-start.41 = (bf16[10,192,256]{2,1,0:T(8,128)(2,1)S(1)}, bf16[10,192,256]{2,1,0:T(8,128)(2,1)S(1)}, u32[]{:S(2)}, u32[]{:S(2)}) collective-permute-start(bf16[10,192,256]{2,1,0:T(8,128)(2,1)S(1)} %get-tuple-element.70), channel_id=1, source_target_pairs={{0,1},{1,0},{2,3},{3,2},{4,5},{5,4},{6,7},{7,6},{8,9},{9,8},{10,11... | collective-permute-start | bytes 2949128 | tf_op jit(solution)/shard_map/ppermute | solution.py:23
  119.4 129.6 %collective-permute-start.44 = (bf16[10,192,256]{2,1,0:T(8,128)(2,1)S(1)}, bf16[10,192,256]{2,1,0:T(8,128)(2,1)S(1)}, u32[]{:S(2)}, u32[]{:S(2)}) collective-permute-start(bf16[10,192,256]{2,1,0:T(8,128)(2,1)S(1)} %get-tuple-element.70), channel_id=1, source_target_pairs={{0,4},{4,0},{1,5},{5,1},{2,6},{6,2},{3,7},{7,3},{8,12},{12,8},{9,1... | collective-permute-start | bytes 2949128 | tf_op jit(solution)/shard_map/ppermute | solution.py:23
  181.4 66.9 %collective-permute-start.26 = (bf16[128,1536]{1,0:T(8,128)(2,1)S(1)}, bf16[128,1536]{1,0:T(8,128)(2,1)S(1)}, u32[]{:S(2)}, u32[]{:S(2)}) collective-permute-start(bf16[128,1536]{1,0:T(8,128)(2,1)S(1)} %collective-permute-done.22), channel_id=1, source_target_pairs={{0,2},{2,0},{1,3},{3,1},{4,6},{6,4},{5,7},{7,5},{8,10},{10,8},{9,1... | collective-permute-start | bytes 1179656 | tf_op jit(solution)/shard_map/ppermute | solution.py:23
  203.7 45.2 %collective-permute-start.25 = (bf16[128,1536]{1,0:T(8,128)(2,1)S(1)}, bf16[128,1536]{1,0:T(8,128)(2,1)S(1)}, u32[]{:S(2)}, u32[]{:S(2)}) collective-permute-start(bf16[128,1536]{1,0:T(8,128)(2,1)S(1)} %collective-permute-done.21), channel_id=1, source_target_pairs={{0,2},{2,0},{1,3},{3,1},{4,6},{6,4},{5,7},{7,5},{8,10},{10,8},{9,1... | collective-permute-start | bytes 1179656 | tf_op jit(solution)/shard_map/ppermute | solution.py:23
  249.0 45.1 %collective-permute-start.15 = (bf16[10,192,256]{2,1,0:T(8,128)(2,1)S(1)}, bf16[10,192,256]{2,1,0:T(8,128)(2,1)S(1)}, u32[]{:S(2)}, u32[]{:S(2)}) collective-permute-start(bf16[10,192,256]{2,1,0:T(8,128)(2,1)S(1)} %collective-permute-done.14), channel_id=1, source_target_pairs={{0,1},{1,0},{2,3},{3,2},{4,5},{5,4},{6,7},{7,6},{8,9},{9,8},{10,11... | collective-permute-start | bytes 2949128 | tf_op jit(solution)/shard_map/ppermute | solution.py:23
  249.1 64.6 %collective-permute-start.46 = (bf16[10,192,256]{2,1,0:T(8,128)(2,1)S(1)}, bf16[10,192,256]{2,1,0:T(8,128)(2,1)S(1)}, u32[]{:S(2)}, u32[]{:S(2)}) collective-permute-start(bf16[10,192,256]{2,1,0:T(8,128)(2,1)S(1)} %collective-permute-done.42), channel_id=1, source_target_pairs={{0,4},{4,0},{1,5},{5,1},{2,6},{6,2},{3,7},{7,3},{8,12},{12,8},{9,1... | collective-permute-start | bytes 2949128 | tf_op jit(solution)/shard_map/ppermute | solution.py:23
  271.5 63.2 %collective-permute-start.32 = (bf16[10,192,256]{2,1,0:T(8,128)(2,1)S(1)}, bf16[10,192,256]{2,1,0:T(8,128)(2,1)S(1)}, u32[]{:S(2)}, u32[]{:S(2)}) collective-permute-start(bf16[10,192,256]{2,1,0:T(8,128)(2,1)S(1)} %collective-permute-done.28), channel_id=1, source_target_pairs={{0,4},{4,0},{1,5},{5,1},{2,6},{6,2},{3,7},{7,3},{8,12},{12,8},{9,1... | collective-permute-start | bytes 2949128 | tf_op jit(solution)/shard_map/ppermute | solution.py:23
  292.6 59.0 %collective-permute-start.18 = (bf16[10,192,256]{2,1,0:T(8,128)(2,1)S(1)}, bf16[10,192,256]{2,1,0:T(8,128)(2,1)S(1)}, u32[]{:S(2)}, u32[]{:S(2)}) collective-permute-start(bf16[10,192,256]{2,1,0:T(8,128)(2,1)S(1)} %collective-permute-done.14), channel_id=1, source_target_pairs={{0,4},{4,0},{1,5},{5,1},{2,6},{6,2},{3,7},{7,3},{8,12},{12,8},{9,1... | collective-permute-start | bytes 2949128 | tf_op jit(solution)/shard_map/ppermute | solution.py:23
  294.1 57.5 %collective-permute-start.17 = (bf16[10,192,256]{2,1,0:T(8,128)(2,1)S(1)}, bf16[10,192,256]{2,1,0:T(8,128)(2,1)S(1)}, u32[]{:S(2)}, u32[]{:S(2)}) collective-permute-start(bf16[10,192,256]{2,1,0:T(8,128)(2,1)S(1)} %collective-permute-done.16), channel_id=1, source_target_pairs={{0,1},{1,0},{2,3},{3,2},{4,5},{5,4},{6,7},{7,6},{8,9},{9,8},{10,11... | collective-permute-start | bytes 2949128 | tf_op jit(solution)/shard_map/ppermute | solution.py:23
  294.3 58.0 %collective-permute-start.29 = (bf16[10,192,256]{2,1,0:T(8,128)(2,1)S(1)}, bf16[10,192,256]{2,1,0:T(8,128)(2,1)S(1)}, u32[]{:S(2)}, u32[]{:S(2)}) collective-permute-start(bf16[10,192,256]{2,1,0:T(8,128)(2,1)S(1)} %collective-permute-done.28), channel_id=1, source_target_pairs={{0,1},{1,0},{2,3},{3,2},{4,5},{5,4},{6,7},{7,6},{8,9},{9,8},{10,11... | collective-permute-start | bytes 2949128 | tf_op jit(solution)/shard_map/ppermute | solution.py:23
  492.6 69.9 %collective-permute-start.92 = (f32[128,8]{0,1:T(8,128)S(1)}, f32[128,8]{0,1:T(8,128)S(1)}, u32[]{:S(2)}, u32[]{:S(2)}) collective-permute-start(f32[128,8]{0,1:T(8,128)S(1)} %get-tuple-element.94), channel_id=1, source_target_pairs={{0,2},{2,0},{1,3},{3,1},{4,6},{6,4},{5,7},{7,5},{8,10},{10,8},{9,1... | collective-permute-start | bytes 12296 | tf_op jit(solution)/shard_map/ppermute | solution.py:23
  494.2 70.7 %collective-permute-start.90 = (f32[128,8]{0,1:T(8,128)S(1)}, f32[128,8]{0,1:T(8,128)S(1)}, u32[]{:S(2)}, u32[]{:S(2)}) collective-permute-start(f32[128,8]{0,1:T(8,128)S(1)} %get-tuple-element.95), channel_id=1, source_target_pairs={{0,2},{2,0},{1,3},{3,1},{4,6},{6,4},{5,7},{7,5},{8,10},{10,8},{9,1... | collective-permute-start | bytes 12296 | tf_op jit(solution)/shard_map/ppermute | solution.py:23
  610.0 45.2 %collective-permute-start.51 = (bf16[128,1536]{1,0:T(8,128)(2,1)}, bf16[128,1536]{1,0:T(8,128)(2,1)}, u32[]{:S(2)}, u32[]{:S(2)}) collective-permute-start(bf16[128,1536]{1,0:T(8,128)(2,1)} %get-tuple-element.64), channel_id=1, source_target_pairs={{0,2},{2,0},{1,3},{3,1},{4,6},{6,4},{5,7},{7,5},{8,10},{10,8},{9,1... | collective-permute-start | bytes 1179656 | tf_op jit(solution)/shard_map/ppermute | solution.py:23
  614.0 143.3 %collective-permute-start.84 = (bf16[10,4,192,256]{3,2,1,0:T(8,128)(2,1)}, bf16[10,4,192,256]{3,2,1,0:T(8,128)(2,1)}, u32[]{:S(2)}, u32[]{:S(2)}) collective-permute-start(bf16[10,4,192,256]{3,2,1,0:T(8,128)(2,1)} %dynamic-slice_bitcast_fusion), channel_id=1, source_target_pairs={{0,1},{1,0},{2,3},{3,2},{4,5},{5,4},{6,7},{7,6},{8,9},{9,8},{10,11... | collective-permute-start | bytes 11796488 | tf_op jit(solution)/shard_map/ppermute | solution.py:23
  632.3 134.1 %collective-permute-start.78 = (bf16[10,4,192,256]{3,2,1,0:T(8,128)(2,1)}, bf16[10,4,192,256]{3,2,1,0:T(8,128)(2,1)}, u32[]{:S(2)}, u32[]{:S(2)}) collective-permute-start(bf16[10,4,192,256]{3,2,1,0:T(8,128)(2,1)} %dynamic-slice_bitcast_fusion.2), channel_id=1, source_target_pairs={{0,1},{1,0},{2,3},{3,2},{4,5},{5,4},{6,7},{7,6},{8,9},{9,8},{10,11... | collective-permute-start | bytes 11796488 | tf_op jit(solution)/shard_map/ppermute | solution.py:23
  651.8 119.8 %collective-permute-start.81 = (bf16[10,4,192,256]{3,2,1,0:T(8,128)(2,1)}, bf16[10,4,192,256]{3,2,1,0:T(8,128)(2,1)}, u32[]{:S(2)}, u32[]{:S(2)}) collective-permute-start(bf16[10,4,192,256]{3,2,1,0:T(8,128)(2,1)} %dynamic-slice_bitcast_fusion.1), channel_id=1, source_target_pairs={{0,1},{1,0},{2,3},{3,2},{4,5},{5,4},{6,7},{7,6},{8,9},{9,8},{10,11... | collective-permute-start | bytes 11796488 | tf_op jit(solution)/shard_map/ppermute | solution.py:23
  684.7 64.0 %collective-permute-start.73 = (bf16[128,1536]{1,0:T(8,128)(2,1)}, bf16[128,1536]{1,0:T(8,128)(2,1)S(1)}, u32[]{:S(2)}, u32[]{:S(2)}) collective-permute-start(bf16[128,1536]{1,0:T(8,128)(2,1)} %get-tuple-element.73), channel_id=1, source_target_pairs={{0,16},{8,24},{16,0},{24,8},{1,17},{9,25},{17,1},{25,9},{2,18},{10... | collective-permute-start | bytes 1179656 | tf_op jit(solution)/shard_map/ppermute | solution.py:23
  687.4 65.4 %collective-permute-start.76 = (bf16[2,192,1024]{2,1,0:T(8,128)(2,1)}, bf16[2,192,1024]{2,1,0:T(8,128)(2,1)S(1)}, u32[]{:S(2)}, u32[]{:S(2)}) collective-permute-start(bf16[2,192,1024]{2,1,0:T(8,128)(2,1)} %dynamic-slice_bitcast_fusion.5), channel_id=1, source_target_pairs={{0,4},{4,0},{1,5},{5,1},{2,6},{6,2},{3,7},{7,3},{8,12},{12,8},{9,1... | collective-permute-start | bytes 2359304 | tf_op jit(solution)/shard_map/ppermute | solution.py:23
  771.6 46.1 %collective-permute-start.85 = (bf16[10,2,192,256]{3,2,0,1:T(8,128)(2,1)}, bf16[10,2,192,256]{3,2,0,1:T(8,128)(2,1)}, u32[]{:S(2)}, u32[]{:S(2)}) collective-permute-start(bf16[10,2,192,256]{3,2,0,1:T(8,128)(2,1)} %bitcast.372), channel_id=1, source_target_pairs={{0,4},{4,0},{1,5},{5,1},{2,6},{6,2},{3,7},{7,3},{8,12},{12,8},{9,1... | collective-permute-start | bytes 5898248 | tf_op jit(solution)/shard_map/ppermute | solution.py:23
  779.4 80.4 %collective-permute-start.79 = (bf16[10,2,192,256]{3,2,0,1:T(8,128)(2,1)S(1)}, bf16[10,2,192,256]{3,2,0,1:T(8,128)(2,1)S(1)}, u32[]{:S(2)}, u32[]{:S(2)}) collective-permute-start(bf16[10,2,192,256]{3,2,0,1:T(8,128)(2,1)S(1)} %bitcast.415), channel_id=1, source_target_pairs={{0,4},{4,0},{1,5},{5,1},{2,6},{6,2},{3,7},{7,3},{8,12},{12,8},{9,1... | collective-permute-start | bytes 5898248 | tf_op jit(solution)/shard_map/ppermute | solution.py:23
  779.5 118.6 %collective-permute-start.82 = (bf16[10,2,192,256]{3,2,0,1:T(8,128)(2,1)S(1)}, bf16[10,2,192,256]{3,2,0,1:T(8,128)(2,1)S(1)}, u32[]{:S(2)}, u32[]{:S(2)}) collective-permute-start(bf16[10,2,192,256]{3,2,0,1:T(8,128)(2,1)S(1)} %bitcast.414), channel_id=1, source_target_pairs={{0,4},{4,0},{1,5},{5,1},{2,6},{6,2},{3,7},{7,3},{8,12},{12,8},{9,1... | collective-permute-start | bytes 5898248 | tf_op jit(solution)/shard_map/ppermute | solution.py:23
  819.9 79.7 %collective-permute-start.86 = (bf16[10,192,256]{2,1,0:T(8,128)(2,1)S(1)}, bf16[10,192,256]{2,1,0:T(8,128)(2,1)S(1)}, u32[]{:S(2)}, u32[]{:S(2)}) collective-permute-start(bf16[10,192,256]{2,1,0:T(8,128)(2,1)S(1)} %fusion.61), channel_id=1, source_target_pairs={{0,2},{2,0},{1,3},{3,1},{4,6},{6,4},{5,7},{7,5},{8,10},{10,8},{9,1... | collective-permute-start | bytes 2949128 | tf_op jit(solution)/shard_map/ppermute | solution.py:23
  (189 other events, 3059.4 us)

commit v2 on v1

--- a/solution.py
+++ b/solution.py
@@ -1,12 +1,16 @@
+import functools
+
 import jax
 import jax.numpy as jnp
-import numpy as np
 from jax import lax
+from jax.experimental import pallas as pl
+from jax.experimental.pallas import tpu as pltpu
 from jax.sharding import Mesh, PartitionSpec as P
 
 HEAD_SIZE = 64
 EXPERTS = 40
 TOPK = 8
+CAP = 48
 
 epsilon = 1e-06
 rope_base = 10000.0
@@ -71,46 +75,113 @@
 
 def gather_gy(block):
     parts = [block, swap(block, "gw", 1)]
-    for s in range(1, lax.axis_size("gt")):
-        parts = parts + [swap(p, "gt", s) for p in parts[:2]]
-    parts = [q for p in parts for q in (p, swap(p, "co", 1))]
+    many = lax.axis_size("gt")
+    for s in range(1, many):
+        parts.append(swap(block, "gt", s))
+    for s in range(1, many):
+        parts.append(swap(parts[1], "gt", s))
+    parts = parts + [swap(p, "co", 1) for p in parts]
+    places = [0, 2] + [4 * s for s in range(1, many)] + [4 * s + 2 for s in range(1, many)]
+    places = places + [p + 1 for p in places]
     me = (lax.axis_index("gt") * 2 + lax.axis_index("gw")) * 2 + lax.axis_index("co")
-    stacked = jnp.stack(parts)
-    return jnp.concatenate([lax.dynamic_index_in_dim(stacked, j ^ me, 0) for j in range(len(parts))])
-
-
-def gather_halves(weight):
-    side = lax.axis_index("gw")
-    half = weight.shape[2] // 2
-    keep = lax.dynamic_slice_in_dim(weight, side * half, half, 2)
-    give = lax.dynamic_slice_in_dim(weight, (1 - side) * half, half, 2)
-    parts = [keep, swap(give, "gw", 1)]
-    for s in range(1, lax.axis_size("gt")):
-        parts = parts + [swap(p, "gt", s) for p in parts[:2]]
-    parts = [q for p in parts for q in (p, swap(p, "co", 1))]
-    me = (lax.axis_index("gt") * 2 + side) * 2 + lax.axis_index("co")
-    stacked = jnp.stack(parts, axis=1)
-    ordered = jnp.concatenate(
-        [lax.dynamic_index_in_dim(stacked, j ^ me, 1) for j in range(len(parts))], axis=1
-    )
-    return ordered.reshape(weight.shape[0], -1, half)
-
-
-def scatter_halves(grad):
+    count = len(parts)
+
+    def kernel(me_ref, *refs):
+        for place, ref in zip(places, refs[:count]):
+            refs[count][me_ref[0] ^ place] = ref[...]
+
+    full = pl.BlockSpec(memory_space=pltpu.VMEM)
+    stacked = pl.pallas_call(
+        kernel,
+        out_shape=jax.ShapeDtypeStruct((count,) + block.shape, block.dtype),
+        in_specs=[pl.BlockSpec(memory_space=pltpu.SMEM)] + [full] * count,
+        out_specs=full,
+        compiler_params=pltpu.CompilerParams(vmem_limit_bytes=40 * 2**20),
+        name="place_attention_weights",
+    )(jnp.full((1,), me, jnp.int32), *parts)
+    return stacked, parts[1], parts[many + 1 if many > 1 else 1]
+
+
+def halve_weights(gate, up, down):
+    experts, rows, full = gate.shape
+    half = full // 2
+
+    def kernel(side_ref, gate_ref, up_ref, down_ref, keep_gu, give_gu, keep_d, give_d):
+        flipped = down_ref[0].astype(f32).T.astype(bf16)
+        pieces = []
+        for low in (0, half):
+            pieces.append((gate_ref[0, :, low : low + half], up_ref[0, :, low : low + half], flipped[:, low : low + half]))
+
+        def put(piece, gu, d):
+            gu[0, :, :half] = piece[0]
+            gu[0, :, half:] = piece[1]
+            d[0] = piece[2]
+
+        @pl.when(side_ref[0] == 0)
+        def _():
+            put(pieces[0], keep_gu, keep_d)
+            put(pieces[1], give_gu, give_d)
+
+        @pl.when(side_ref[0] != 0)
+        def _():
+            put(pieces[1], keep_gu, keep_d)
+            put(pieces[0], give_gu, give_d)
+
+    def block(shape):
+        return pl.BlockSpec((1,) + shape, lambda e, *_: (e, 0, 0))
+
+    wide = jax.ShapeDtypeStruct((experts, rows, full), bf16)
+    thin = jax.ShapeDtypeStruct((experts, rows, half), bf16)
+    return pl.pallas_call(
+        kernel,
+        grid_spec=pltpu.PrefetchScalarGridSpec(
+            num_scalar_prefetch=1,
+            grid=(experts,),
+            in_specs=[block((rows, full)), block((rows, full)), block((full, rows))],
+            out_specs=[block((rows, full)), block((rows, full)), block((rows, half)), block((rows, half))],
+        ),
+        out_shape=[wide, wide, thin, thin],
+        name="halve_weights",
+    )(jnp.full((1,), lax.axis_index("gw"), jnp.int32), gate, up, down)
+
+
+def gather_weights(gate, up, down, first_x, first_y):
     many = lax.axis_size("gt")
-    t, w, k = lax.axis_index("gt"), lax.axis_index("gw"), lax.axis_index("co")
-    experts, _, half = grad.shape
-    grad = grad.reshape(experts, many * 2, 2, -1, half)
-    total = pick(grad, k, 2).astype(f32) + swap(pick(grad, 1 - k, 2), "co", 1).astype(f32)
-    total = total.astype(bf16).reshape(experts, many, 2, -1, half)
-    own = pick(total, t, 1).astype(f32)
-    for s in range(1, many):
-        own = own + swap(pick(total, t ^ s, 1), "gt", s).astype(f32)
-    mine = pick(own, w, 1)
-    other = swap(pick(own, 1 - w, 1).astype(bf16), "gw", 1).astype(f32)
-    low = jnp.where(w == 0, mine, other)
-    high = jnp.where(w == 0, other, mine)
-    return jnp.concatenate([low, high], axis=2)
+    keep_gu, give_gu, keep_d, give_d = halve_weights(gate, up, down)
+    got_gu = swap(after(give_gu, first_x), "gw", 1)
+    got_d = swap(after(give_d, got_gu), "gw", 1)
+    wide, thin = [keep_gu, got_gu], [keep_d, got_d]
+    places = [0, 2]
+    last = first_y
+    for bulk, many_parts in ((wide, True), (thin, False)):
+        for w in range(2):
+            for s in range(1, many):
+                last = swap(after(bulk[w], last), "gt", s)
+                bulk.append(last)
+    for w in range(2):
+        for s in range(1, many):
+            places.append(4 * s + 2 * w)
+    wide = wide + [swap(p, "co", 1) for p in wide]
+    thin = thin + [swap(p, "co", 1) for p in thin]
+    return wide, thin, places + [p + 1 for p in places]
+
+
+def scatter_gradients(parts, rows):
+    many = lax.axis_size("gt")
+    total = {}
+    order = [(t, w) for t in range(many - 1, -1, -1) for w in (1, 0)]
+    for t, w in order:
+        got = swap(parts[t, w, 1], "co", 1)
+        total[t, w] = parts[t, w, 0].astype(f32) + got.astype(f32)
+    own = {}
+    last = None
+    for w in (1, 0):
+        own[w] = total[0, w]
+        for t in range(1, many):
+            send = total[t, w].astype(bf16)
+            last = swap(send if last is None else after(send, last), "gt", t)
+            own[w] = own[w] + last.astype(f32)
+    return own[0], swap(own[1].astype(bf16), "gw", 1).astype(f32)
 
 
 def scatter_gy(grad):
@@ -125,6 +196,169 @@
         own = own + swap(pick(total, t ^ s, 0), "gt", s).astype(f32)
     own = own.astype(bf16)
     return pick(own, w, 0).astype(f32) + swap(pick(own, 1 - w, 0), "gw", 1).astype(f32)
+
+
+def sum_everywhere(value):
+    for axis in ("co", "gw", "gt", "gx"):
+        step = 1
+        while step < lax.axis_size(axis):
+            value = value + swap(value, axis, step)
+            step = step * 2
+    return value
+
+
+def slot_mask(slot_row):
+    wanted = lax.broadcasted_iota(jnp.int32, (CAP, slot_row.shape[1]), 0).astype(f32)
+    return slot_row == wanted
+
+
+def gather_slots(rows_all, slots):
+    blocks, experts, tokens = slots.shape
+    width = rows_all.shape[1]
+
+    def kernel(slots_ref, rows_ref, out_ref):
+        mask = jnp.concatenate([slot_mask(slots_ref[0, e : e + 1, :]) for e in range(experts)], axis=0)
+        found = jnp.dot(mask.astype(f32).astype(bf16), rows_ref[...], preferred_element_type=f32)
+        out_ref[...] = found.astype(bf16).reshape(experts, 1, CAP, width)
+
+    return pl.pallas_call(
+        kernel,
+        grid=(blocks,),
+        in_specs=[
+            pl.BlockSpec((1, experts, tokens), lambda b: (b, 0, 0)),
+            pl.BlockSpec((tokens, width), lambda b: (b, 0)),
+        ],
+        out_specs=pl.BlockSpec((experts, 1, CAP, width), lambda b: (0, b, 0, 0)),
+        out_shape=jax.ShapeDtypeStruct((experts, blocks, CAP, width), bf16),
+        compiler_params=pltpu.CompilerParams(vmem_limit_bytes=40 * 2**20),
+        cost_estimate=pl.CostEstimate(
+            flops=2 * blocks * tokens * experts * CAP * width,
+            bytes_accessed=2 * blocks * (tokens + experts * CAP) * width,
+            transcendentals=0,
+        ),
+        name="gather_slots",
+    )(slots, rows_all)
+
+
+def sum_slots(slot_rows, slots):
+    blocks, experts, tokens = slots.shape
+    width = slot_rows.shape[3]
+
+    def kernel(slots_ref, rows_ref, out_ref):
+        mask = jnp.concatenate([slot_mask(slots_ref[0, e : e + 1, :]) for e in range(experts)], axis=0)
+        total = contract_rows(mask.astype(f32).astype(bf16), rows_ref[...].reshape(experts * CAP, width))
+        out_ref[...] = total.astype(bf16)
+
+    return pl.pallas_call(
+        kernel,
+        grid=(blocks,),
+        in_specs=[
+            pl.BlockSpec((1, experts, tokens), lambda b: (b, 0, 0)),
+            pl.BlockSpec((experts, 1, CAP, width), lambda b: (0, b, 0, 0)),
+        ],
+        out_specs=pl.BlockSpec((tokens, width), lambda b: (b, 0)),
+        out_shape=jax.ShapeDtypeStruct((blocks * tokens, width), bf16),
+        compiler_params=pltpu.CompilerParams(vmem_limit_bytes=40 * 2**20),
+        cost_estimate=pl.CostEstimate(
+            flops=2 * blocks * tokens * experts * CAP * width,
+            bytes_accessed=2 * blocks * (tokens + experts * CAP) * width,
+            transcendentals=0,
+        ),
+        name="sum_slots",
+    )(slots, slot_rows)
+
+
+def run_experts(rows_in, back_in, wide, thin, places, slots, chances):
+    experts, blocks, _, width = rows_in.shape
+    tokens = slots.shape[2]
+    cut, half = thin[0].shape[1:]
+    count = len(places)
+    total_slots = blocks * CAP
+    me = (lax.axis_index("gt") * 2 + lax.axis_index("gw")) * 2 + lax.axis_index("co")
+
+    def kernel(me_ref, rows_ref, back_ref, slots_ref, chances_ref, *refs):
+        wide_refs, thin_refs = refs[:count], refs[count : 2 * count]
+        rows_out, mixed_out, chance_out = refs[2 * count : 2 * count + 3]
+        grads = refs[2 * count + 3 : 3 * count + 3]
+        gu_full, d_full, gu_total, d_total = refs[3 * count + 3 :]
+        spots = [pl.ds(pl.multiple_of((me_ref[0] ^ place) * cut, cut), cut) for place in places]
+        for spot, gu, d in zip(spots, wide_refs, thin_refs):
+            gu_full[spot, :] = gu[0]
+            d_full[spot, :] = d[0]
+        rows = rows_ref[0].reshape(total_slots, width)
+        back = back_ref[0].reshape(total_slots, width)
+        masks = [slot_mask(slots_ref[0, b : b + 1, :]) for b in range(blocks)]
+        chance = jnp.concatenate(
+            [
+                jnp.sum(jnp.where(masks[b], chances_ref[0, b : b + 1, :], 0.0), axis=1, keepdims=True)
+                for b in range(blocks)
+            ],
+            axis=0,
+        )
+        both = jnp.dot(rows, gu_full[...], preferred_element_type=f32)
+        active_back = jnp.dot(back, d_full[...], preferred_element_type=f32) * residual_factor
+        gate, upper = both[:, :half], both[:, half:]
+        sigma = jax.nn.sigmoid(gate)
+        silu = gate * sigma
+        active = silu * upper
+        chance_back = jnp.sum(active * active_back, axis=1, keepdims=True)
+        for b in range(blocks):
+            column = chance_back[b * CAP : (b + 1) * CAP]
+            chance_out[0, b : b + 1, :] = jnp.sum(jnp.where(masks[b], column, 0.0), axis=0, keepdims=True)
+        scaled = (active * chance).astype(bf16)
+        active_back = active_back * chance
+        gate_back = active_back * upper * (sigma * (1.0 + gate * (1.0 - sigma)))
+        upper_back = active_back * silu
+        both_back = jnp.concatenate([gate_back.astype(bf16), upper_back.astype(bf16)], axis=1)
+        rows_out[0] = contract_cols(both_back, gu_full[...]).astype(bf16).reshape(blocks, CAP, width)
+        mixed_out[0] = contract_cols(scaled, d_full[...]).astype(bf16).reshape(blocks, CAP, width)
+        gu_total[...] = contract_rows(rows, both_back).astype(bf16)
+        d_total[...] = (contract_rows(back, scaled) * residual_factor).astype(bf16)
+        for spot, grad in zip(spots, grads):
+            grad[0, :, : 2 * half] = gu_total[spot, :]
+            grad[0, :, 2 * half :] = d_total[spot, :]
+
+    def block(shape):
+        zeros = (0,) * len(shape)
+        return pl.BlockSpec((1,) + shape, lambda e, *_: (e,) + zeros)
+
+    flops = 2 * experts * total_slots * width * half * 9
+    grad_shape = jax.ShapeDtypeStruct((experts, cut, 3 * half), bf16)
+    slot_shape = jax.ShapeDtypeStruct((experts, blocks, CAP, width), bf16)
+    out = pl.pallas_call(
+        kernel,
+        grid_spec=pltpu.PrefetchScalarGridSpec(
+            num_scalar_prefetch=1,
+            grid=(experts,),
+            in_specs=[
+                block((blocks, CAP, width)),
+                block((blocks, CAP, width)),
+                block((blocks, tokens)),
+                block((blocks, tokens)),
+            ]
+            + [block((cut, 2 * half))] * count
+            + [block((cut, half))] * count,
+            out_specs=[block((blocks, CAP, width)), block((blocks, CAP, width)), block((blocks, tokens))]
+            + [block((cut, 3 * half))] * count,
+            scratch_shapes=[
+                pltpu.VMEM((width, 2 * half), bf16),
+                pltpu.VMEM((width, half), bf16),
+                pltpu.VMEM((width, 2 * half), bf16),
+                pltpu.VMEM((width, half), bf16),
+            ],
+        ),
+        out_shape=[slot_shape, slot_shape, jax.ShapeDtypeStruct((experts, blocks, tokens), f32)]
+        + [grad_shape] * count,
+        compiler_params=pltpu.CompilerParams(vmem_limit_bytes=60 * 2**20),
+        cost_estimate=pl.CostEstimate(
+            flops=flops,
+            bytes_accessed=2 * experts * (4 * total_slots * width + 6 * half * width),
+            transcendentals=experts * total_slots * half,
+        ),
+        name="run_experts",
+    )(jnp.full((1,), me, jnp.int32), rows_in, back_in, slots, chances, *wide, *thin)
+    gradients = {(p // 4, (p // 2) % 2, p % 2): g for p, g in zip(places, out[3:])}
+    return out[0], out[1], out[2], gradients
 
 
 def block_scores(query_rows, key_rows, positions):
@@ -185,25 +419,27 @@
     attention = jnp.concatenate(
         [query_weight, key_matrix, value_matrix, out_weight.T], axis=1
     )
-    attention_full = gather_gy(attention).reshape(width, -1)
+    attention_full, first_x, first_y = gather_gy(attention)
+    attention_full = attention_full.reshape(width, -1)
     joined = attention_full[:, : query_cols + 2 * key_cols]
     out_full = attention_full[:, query_cols + 2 * key_cols :]
 
-    gate_full = gather_halves(after(gate_weight, attention_full))
-    up_full = gather_halves(after(up_weight, attention_full))
-    down_full = gather_halves(jnp.swapaxes(after(down_weight, attention_full), 1, 2))
+    wide, thin, places = gather_weights(gate_weight, up_weight, down_weight, first_x, first_y)
 
     logits = route_logits[0]
     weights = jnp.exp(logits - jnp.max(logits, axis=-1, keepdims=True))
     chance = weights / jnp.sum(weights, axis=-1, keepdims=True)
     routing = jnp.concatenate([routes[0].astype(f32), chance], axis=1)
-
-    def gather_tokens(block):
-        parts = gather_gx(block)
-        return jnp.concatenate(parts + [swap(p, "gw", 1) for p in parts], axis=0)
-
-    cotangent_rows = gather_tokens(after(cotangent[0], token_blocks[groups - 1]))
-    routing_rows = gather_tokens(after(routing, token_blocks[groups - 1]))
+    last_token = token_blocks[groups - 1]
+    me_w = lax.axis_index("gw")
+    turned = [((me_x ^ s) * 2 + (me_w ^ w)) for w in range(2) for s in range(groups)]
+
+    def gather_early(block):
+        whole = lax.all_gather(after(block, last_token), ("gx", "gw"), axis=0)
+        return jnp.stack([lax.dynamic_index_in_dim(whole, j, 0, keepdims=False) for j in turned])
+
+    cotangent_rows = gather_early(cotangent[0]).reshape(-1, width)
+    routing_rows = gather_early(routing)
 
     sequence = jnp.concatenate(token_blocks, axis=0).astype(f32)
     length = sequence.shape[0]
@@ -213,8 +449,7 @@
     positions = jnp.concatenate(
         [(me_x ^ s) * rows + jnp.arange(rows, dtype=jnp.int32) for s in range(groups)]
     )
-    half = HEAD_SIZE // 2
-    freq = rope_base ** (-(jnp.arange(half, dtype=f32) * 2.0 / HEAD_SIZE))
+    freq = rope_base ** (-(jnp.arange(HEAD_SIZE // 2, dtype=f32) * 2.0 / HEAD_SIZE))
     angle = positions.astype(f32)[:, None] * freq[None, :]
     cosine = jnp.cos(angle)[:, None, :]
     sine = jnp.sin(angle)[:, None, :]
@@ -236,54 +471,65 @@
     middle = hidden + residual_factor * branch
     factor_two = rms_factor(middle)
     normed_two = (middle * factor_two * second_gain).astype(bf16)
-    normed_rows = gather_tokens(normed_two)
+    parts = gather_gx(normed_two)
+    normed_rows = jnp.concatenate(parts + [swap(p, "gw", 1) for p in parts], axis=0)
 
     experts = gate_weight.shape[0]
-    first_expert = me_x * experts
-    ids = (first_expert + jnp.arange(experts, dtype=jnp.int32)).astype(f32)
-    same = routing_rows[None, :, :TOPK] == ids[:, None, None]
-    chosen = jnp.sum(jnp.where(same, routing_rows[None, :, TOPK:], 0.0), axis=2)[:, :, None]
-    back = jnp.einsum("td,edf->etf", cotangent_rows, down_full, preferred_element_type=f32)
-    gate = jnp.einsum("td,edf->etf", normed_rows, gate_full, preferred_element_type=f32)
-    upper = jnp.einsum("td,edf->etf", normed_rows, up_full, preferred_element_type=f32)
-    sigma = jax.nn.sigmoid(gate)
-    active = gate * sigma * upper
-    back = back * residual_factor
-    chance_part = jnp.sum(active * back, axis=2)
-    scaled = (active * chosen).astype(bf16)
-    active_back = back * chosen
-    gate_back = (active_back * upper * sigma * (1.0 + gate * (1.0 - sigma))).astype(bf16)
-    upper_back = (active_back * gate * sigma).astype(bf16)
-
-    rows_back = jnp.einsum("etf,edf->td", gate_back, gate_full, preferred_element_type=f32)
-    rows_back = rows_back + jnp.einsum("etf,edf->td", upper_back, up_full, preferred_element_type=f32)
-    rows_back = rows_back.astype(bf16)
-
-    def scatter_tokens(parts, kind):
-        cut = [parts[s * rows : (s + 1) * rows] for s in range(2 * groups)]
-        own = [
-            cut[s].astype(f32) + swap(cut[groups + s], "gw", 1).astype(f32) for s in range(groups)
+    ids = (me_x * experts + jnp.arange(experts, dtype=jnp.int32)).astype(f32)
+    same = routing_rows[:, None, :, :TOPK] == ids[None, :, None, None]
+    hits = jnp.sum(same.astype(f32), axis=3)
+    before = jnp.triu(jnp.ones((rows, rows), f32), 1)
+    slots = jnp.where(hits > 0.0, jnp.einsum("beu,ut->bet", hits, before), -1.0)
+    chosen = jnp.sum(jnp.where(same, routing_rows[:, None, :, TOPK:], 0.0), axis=3)
+    rows_in = gather_slots(normed_rows, slots)
+    back_in = gather_slots(cotangent_rows, slots)
+    rows_back, mixed_parts, chance_part, gradients = run_experts(
+        rows_in, back_in, wide, thin, places, jnp.swapaxes(slots, 0, 1), jnp.swapaxes(chosen, 0, 1)
+    )
+    rows_back = sum_slots(rows_back, slots)
+
+    def cut(whole, s):
+        return whole[s * rows : (s + 1) * rows]
+
+    order = list(range(1, groups)) + [0]
+    crossed = {s: swap(cut(rows_back, groups + s), "gw", 1) for s in order}
+    normed_two_back = scatter_gx(
+        [cut(rows_back, s).astype(f32) + crossed[s].astype(f32) for s in range(groups)]
+    )
+
+    mixed_rows = sum_slots(mixed_parts, slots).reshape(2 * groups, rows, width)
+    mixed_rows = jnp.concatenate(
+        [
+            lax.dynamic_index_in_dim(mixed_rows, (w ^ me_w) * groups + (x ^ me_x), 0)
+            for x in range(groups)
+            for w in range(2)
         ]
-        total = own[0]
-        for s in range(1, groups):
-            total = total + swap(own[s].astype(kind), "gx", s).astype(f32)
-        return total
-
-    normed_two_back = scatter_tokens(rows_back, bf16)
-
-    mixed_parts = jnp.einsum("etf,edf->td", scaled, down_full, preferred_element_type=f32)
-    mixed = scatter_tokens(mixed_parts.astype(bf16), bf16)
+    )
+    mixed = lax.psum_scatter(mixed_rows, ("gx", "gw"), scatter_dimension=0).astype(f32)
     output = (middle + residual_factor * mixed).astype(bf16)
-    chance_rows = jnp.sum(jnp.where(same, chance_part[:, :, None], 0.0), axis=0)
-    chance_back = scatter_tokens(chance_rows, f32)
+    chance_rows = jnp.sum(jnp.where(same, jnp.swapaxes(chance_part, 0, 1)[:, :, :, None], 0.0), axis=1)
+    chance_rows = jnp.stack(
+        [
+            lax.dynamic_index_in_dim(chance_rows, (w ^ me_w) * groups + (x ^ me_x), 0, keepdims=False)
+            for x in range(groups)
+            for w in range(2)
+        ]
+    )
+    chance_back = lax.psum_scatter(chance_rows, ("gx", "gw"), scatter_dimension=0)
     logit_back = chance * (chance_back - jnp.sum(chance * chance_back, axis=-1, keepdims=True))
 
-    gate_grad = jnp.einsum("td,etf->edf", normed_rows, gate_back, preferred_element_type=f32)
-    up_grad = jnp.einsum("td,etf->edf", normed_rows, upper_back, preferred_element_type=f32)
-    down_grad = jnp.einsum("td,etf->edf", cotangent_rows, scaled, preferred_element_type=f32)
-    gate_sum = scatter_halves(gate_grad.astype(bf16))
-    up_sum = scatter_halves(up_grad.astype(bf16))
-    down_sum = scatter_halves((residual_factor * down_grad).astype(bf16))
+    mine, other = scatter_gradients(gradients, rows)
+    half = mine.shape[2] // 3
+    gate_sum, up_sum, down_sum = [
+        jnp.concatenate(
+            [
+                jnp.where(me_w == 0, mine[:, :, c : c + half], other[:, :, c : c + half]),
+                jnp.where(me_w == 0, other[:, :, c : c + half], mine[:, :, c : c + half]),
+            ],
+            axis=2,
+        )
+        for c in (0, half, 2 * half)
+    ]
 
     upstream = cotangent[0].astype(f32)
     middle_back = upstream + norm_back(middle, factor_two, second_gain, normed_two_back)
@@ -312,7 +558,7 @@
         [normed_one_parts[s * rows : (s + 1) * rows] for s in range(groups)]
     )
     tokens_back = middle_back + norm_back(hidden, factor_all[:rows], first_gain, normed_one_back)
-    gains = lax.psum(jnp.stack([first_part, second_part]), ("gx", "gt", "gw", "co"))
+    gains = sum_everywhere(jnp.stack([first_part, second_part]))
     joined_grad = contract_rows(sequence_rows, projected_back)
     attention_sum = scatter_gy(jnp.concatenate([joined_grad, out_grad], axis=1).astype(bf16))
     return (

time: 932 us -> 735 us (0.79)
  waiting for transfers between devices: 433 us -> 303 us
  matrix products: 144 us -> 24.6 us
  Pallas kernels: 0 us -> 87.2 us
  starting transfers between devices: 110 us -> 45.9 us
  blocking collectives: 59 us -> 122 us
  local copies, waits for them, and re-layouts: 106 us -> 58.6 us
  between operations: 3.31 us -> 15.9 us
    ppermute x94 -> x62, waiting for transfers between devices: 433 us -> 303 us  [swap(): return lax.ppermute(value, axis, [(i, i ^ step) for i in range(count)])]
    dot_general x9 -> x1, matrix products: 123 us -> 0.13 us  [local(): slots = jnp.where(hits > 0.0, jnp.einsum('beu,ut->bet', hits, before), -1.0)]
    unnamed x0 -> x1, blocking collectives: none -> 89.5 us
    pallas_call x0 -> x7, Pallas kernels: none -> 87.2 us  [the longest x1 46.9 us: run_experts(): pl.pallas_call(kernel, grid_spec=pltpu.PrefetchScalarGridSpec(num_scalar_...]
    ppermute x94 -> x62, starting transfers between devices: 110 us -> 45.8 us  [swap(): return lax.ppermute(value, axis, [(i, i ^ step) for i in range(count)])]
    psum x1 -> x0, blocking collectives: 59 us -> none  [local(): lax.psum(jnp.stack([first_part, second_part]), ('gx', 'gt', 'gw', 'co'))]
    convert_element_type x6 -> x0, local copies, waits for them, and re-layouts: 32.6 us -> none  [the longest x1 10.8 us: local(): down_sum = scatter_halves((residual_factor * down_grad).astype(bf16))]
    all_gather x0 -> x1, blocking collectives: none -> 32.2 us  [gather_early(): whole = lax.all_gather(after(block, last_token), ('gx', 'gw'), axis=0)]
  transfers between devices with their start and end apart: 94 -> 64, of which waited for: 34 -> 24; matrix products, arithmetic and copies ran while one was open for 20% -> 16% of each run, Pallas kernels for 0% -> 3%
where the time goes in v2:
time: 735 us; the launch traced here: 725 us
  waiting for transfers between devices  303 us (41%)
  blocking collectives  122 us (17%)
  Pallas kernels  87.2 us (12%)
  other arithmetic  68.2 us (9%)
  local copies, waits for them, and re-layouts  58.6 us (8%)
  starting transfers between devices  45.9 us (6%)
  matrix products  24.6 us (3%)
  between operations  15.9 us (2%)
    ppermute x62, waiting for transfers between devices, swap(): return lax.ppermute(value, axis, [(i, i ^ step) for i in range(count)])  303 us
    unnamed x1, blocking collectives  89.5 us
    pallas_call x1, Pallas kernels, run_experts(): pl.pallas_call(kernel, grid_spec=pltpu.PrefetchScalarGridSpec(num_scalar_...  46.9 us
    ppermute x62, starting transfers between devices, swap(): return lax.ppermute(value, axis, [(i, i ^ step) for i in range(count)])  45.8 us
    unnamed x216, local copies, waits for them, and re-layouts  36.2 us
    all_gather x1, blocking collectives, gather_early(): whole = lax.all_gather(after(block, last_token), ('gx', 'gw'), axis=0)  32.2 us
    pallas_call x2, Pallas kernels, sum_slots(): pl.pallas_call(kernel, grid=(blocks,), in_specs=[pl.BlockSpec((1, experts...  15.9 us
  transfers between devices with their start and end apart: 64, of which 24 were waited for; matrix products, arithmetic and copies ran while one was open for 16% of the time, Pallas kernels for 3%

profile of v2, /device:TPU:0, one launch (start us, length us, event | category | flops | bytes accessed | tf_op | source)
XLA Modules:
  0.0 724.8 jit_solution(3620264729274848575)
XLA Ops:
  27.6 9.5 %halve_weights.1 = (bf16[10,192,512]{2,1,0:T(8,128)(2,1)}, bf16[10,192,512]{2,1,0:T(8,128)(2,1)}, bf16[10,192,256]{2,1,0:T(8,128)(2,1)}, bf16[10,192,256]{2,1,0:T(8,128)(2,1)}) custom-call(s32[1]{0:T(128)} %bitcast.24.side_ref, bf16[10,192,512]{2,1,0:T(8,128)(2,1)} %gate_ref.1, bf16[10,192,512]{2,1,0:T(8,128)(2,1)} %up_ref.1, ...), custom_call_target="tpu_custom_call" | custom-call | tf_op jit(solution)/shard_map/halve_weights/pallas_call | solution.py:135
  38.2 32.2 %all-gather = f32[1024,16]{0,1:T(8,128)S(1)} all-gather(f32[128,16]{0,1:T(8,128)S(1)} %pad_maximum_fusion.15), channel_id=2, replica_groups=mesh['gx'=4,'gt'=2,'gw'=2,'co'=2] {'gx','gw'}, dimensions={0}, use_global_device_ids=true | all-gather | bytes 73728 | tf_op jit(solution)/shard_map/all_gather | solution.py:438
  108.8 18.9 %collective-permute-done.20.refs_1_ = bf16[10,192,512]{2,1,0:T(8,128)(2,1)} collective-permute-done((bf16[10,192,512]{2,1,0:T(8,128)(2,1)}, bf16[10,192,512]{2,1,0:T(8,128)(2,1)}, u32[]{:S(2)}, u32[]{:S(2)}) %collective-permute-start.20) | collective-permute-done | bytes 1966112 | tf_op jit(solution)/shard_map/ppermute | solution.py:27
  132.3 16.7 %collective-permute-done.11 = bf16[128,1536]{1,0:T(8,128)(2,1)} collective-permute-done((bf16[128,1536]{1,0:T(8,128)(2,1)}, bf16[128,1536]{1,0:T(8,128)(2,1)}, u32[]{:S(2)}, u32[]{:S(2)}) %collective-permute-start.11) | collective-permute-done | bytes 393248 | tf_op jit(solution)/shard_map/ppermute | solution.py:27
  155.0 15.4 %collective-permute-done.14 = bf16[128,1536]{1,0:T(8,128)(2,1)S(1)} collective-permute-done((bf16[128,1536]{1,0:T(8,128)(2,1)S(1)}, bf16[128,1536]{1,0:T(8,128)(2,1)S(1)}, u32[]{:S(2)}, u32[]{:S(2)}) %collective-permute-start.14) | collective-permute-done | bytes 393248 | tf_op jit(solution)/shard_map/ppermute | solution.py:27
  175.3 8.0 %collective-permute-done.15 = bf16[128,1536]{1,0:T(8,128)(2,1)S(1)} collective-permute-done((bf16[128,1536]{1,0:T(8,128)(2,1)S(1)}, bf16[128,1536]{1,0:T(8,128)(2,1)S(1)}, u32[]{:S(2)}, u32[]{:S(2)}) %collective-permute-start.15) | collective-permute-done | bytes 393248 | tf_op jit(solution)/shard_map/ppermute | solution.py:27
  184.4 8.0 %collective-permute-done.17 = bf16[128,1536]{1,0:T(8,128)(2,1)S(1)} collective-permute-done((bf16[128,1536]{1,0:T(8,128)(2,1)S(1)}, bf16[128,1536]{1,0:T(8,128)(2,1)S(1)}, u32[]{:S(2)}, u32[]{:S(2)}) %collective-permute-start.17) | collective-permute-done | bytes 393248 | tf_op jit(solution)/shard_map/ppermute | solution.py:27
  192.5 28.0 %collective-permute-done.19 = bf16[128,1536]{1,0:T(8,128)(2,1)S(1)} collective-permute-done((bf16[128,1536]{1,0:T(8,128)(2,1)S(1)}, bf16[128,1536]{1,0:T(8,128)(2,1)S(1)}, u32[]{:S(2)}, u32[]{:S(2)}) %collective-permute-start.19) | collective-permute-done | bytes 393248 | tf_op jit(solution)/shard_map/ppermute | solution.py:27
  221.7 7.4 %gather_slots.2.rows_ref = bf16[10,8,48,1536]{3,2,1,0:T(8,128)(2,1)} custom-call(f32[8,10,128]{2,1,0:T(8,128)S(1)} %convolution_select_fusion.slots_ref, bf16[1024,1536]{1,0:T(8,128)(2,1)S(1)} %constant_dynamic-update-slice_fusion.rows_ref), custom_call_target="tpu_custom_call" | custom-call | flops 1509949440 | bytes 14942208 | tf_op jit(solution)/shard_map/gather_slots/pallas_call | solution.py:224
  235.4 9.7 %collective-permute-done.29.refs_11_ = bf16[10,192,256]{2,1,0:T(8,128)(2,1)} collective-permute-done((bf16[10,192,256]{2,1,0:T(8,128)(2,1)}, bf16[10,192,256]{2,1,0:T(8,128)(2,1)}, u32[]{:S(2)}, u32[]{:S(2)}) %collective-permute-start.29) | collective-permute-done | bytes 983072 | tf_op jit(solution)/shard_map/ppermute | solution.py:27
  245.3 7.2 gather_slots.3.back_ref
  252.6 46.9 %run_experts.1 = (bf16[10,8,48,1536]{3,2,1,0:T(8,128)(2,1)}, bf16[10,8,48,1536]{3,2,1,0:T(8,128)(2,1)}, f32[10,8,128]{2,1,0:T(8,128)}, bf16[10,192,768]{2,1,0:T(...) custom-call(s32[1]{0:T(128)} %bitcast.1.me_ref, ...), custom_call_target="tpu_custom_call" | custom-call | flops 27179089920 | bytes 94371840 | tf_op jit(solution)/shard_map/run_experts/pallas_call | solution.py:328
  299.5 7.9 %sum_slots.2 = bf16[1024,1536]{1,0:T(8,128)(2,1)S(1)} custom-call(f32[8,10,128]{2,1,0:T(8,128)S(1)} %convolution_select_fusion.slots_ref, bf16[10,8,48,1536]{3,2,1,0:T(8,128)(2,1)} %get-tuple-element.48.rows_ref), custom_call_target="tpu_custom_call" | custom-call | flops 1509949440 | bytes 14942208 | tf_op jit(solution)/shard_map/sum_slots/pallas_call | solution.py:252
  307.4 7.9 %sum_slots.3 = bf16[1024,1536]{1,0:T(8,128)(2,1)S(1)} custom-call(f32[8,10,128]{2,1,0:T(8,128)S(1)} %convolution_select_fusion.slots_ref, bf16[10,8,48,1536]{3,2,1,0:T(8,128)(2,1)} %get-tuple-element.49.rows_ref), custom_call_target="tpu_custom_call" | custom-call | flops 1509949440 | bytes 14942208 | tf_op jit(solution)/shard_map/sum_slots/pallas_call | solution.py:252
  323.5 12.4 %collective-permute-done.39 = bf16[128,1536]{1,0:T(8,128)(2,1)S(1)} collective-permute-done((bf16[128,1536]{1,0:T(8,128)(2,1)S(1)}, bf16[128,1536]{1,0:T(8,128)(2,1)S(1)}, u32[]{:S(2)}, u32[]{:S(2)}) %collective-permute-start.39) | collective-permute-done | bytes 393248 | tf_op jit(solution)/shard_map/ppermute | solution.py:27
  335.9 8.4 %collective-permute-done.37 = bf16[128,1536]{1,0:T(8,128)(2,1)S(1)} collective-permute-done((bf16[128,1536]{1,0:T(8,128)(2,1)S(1)}, bf16[128,1536]{1,0:T(8,128)(2,1)S(1)}, u32[]{:S(2)}, u32[]{:S(2)}) %collective-permute-start.37) | collective-permute-done | bytes 393248 | tf_op jit(solution)/shard_map/ppermute | solution.py:27
  344.3 8.0 %collective-permute-done.35 = bf16[128,1536]{1,0:T(8,128)(2,1)S(1)} collective-permute-done((bf16[128,1536]{1,0:T(8,128)(2,1)S(1)}, bf16[128,1536]{1,0:T(8,128)(2,1)S(1)}, u32[]{:S(2)}, u32[]{:S(2)}) %collective-permute-start.35) | collective-permute-done | bytes 393248 | tf_op jit(solution)/shard_map/ppermute | solution.py:27
  364.7 8.9 %collective-permute-done.40 = bf16[128,1536]{1,0:T(8,128)(2,1)S(1)} collective-permute-done((bf16[128,1536]{1,0:T(8,128)(2,1)S(1)}, bf16[128,1536]{1,0:T(8,128)(2,1)S(1)}, u32[]{:S(2)}, u32[]{:S(2)}) %collective-permute-start.40) | collective-permute-done | bytes 393248 | tf_op jit(solution)/shard_map/ppermute | solution.py:27
  373.6 16.4 %collective-permute-done.38 = bf16[128,1536]{1,0:T(8,128)(2,1)S(1)} collective-permute-done((bf16[128,1536]{1,0:T(8,128)(2,1)S(1)}, bf16[128,1536]{1,0:T(8,128)(2,1)S(1)}, u32[]{:S(2)}, u32[]{:S(2)}) %collective-permute-start.38) | collective-permute-done | bytes 393248 | tf_op jit(solution)/shard_map/ppermute | solution.py:27
  406.2 45.1 %collective-permute-done.42 = bf16[128,1536]{1,0:T(8,128)(2,1)} collective-permute-done((bf16[128,1536]{1,0:T(8,128)(2,1)S(1)}, bf16[128,1536]{1,0:T(8,128)(2,1)}, u32[]{:S(2)}, u32[]{:S(2)}) %collective-permute-start.42) | collective-permute-done | bytes 393248 | tf_op jit(solution)/shard_map/ppermute | solution.py:27
  488.9 54.0 %collective-permute-done.49 = f32[2,1536]{1,0:T(2,128)S(1)} collective-permute-done((f32[2,1536]{1,0:T(2,128)S(1)}, f32[2,1536]{1,0:T(2,128)S(1)}, u32[]{:S(2)}, u32[]{:S(2)}) %collective-permute-start.49) | collective-permute-done | bytes 12320 | tf_op jit(solution)/shard_map/ppermute | solution.py:27
  564.2 89.5 %all-reduce = f32[8,128,8]{1,2,0:T(8,128)} all-reduce(f32[8,128,8]{1,2,0:T(8,128)} %constant_dynamic-update-slice_fusion.8), channel_id=5, replica_groups=mesh['gx'=4,'gt'=2,'gw'=2,'co'=2] {'gx','gw'}, use_global_device_ids=true, to_apply=%region_15.16.clone | all-reduce | flops 8192 | bytes 65536
  660.9 7.5 %collective-permute-done.46 = bf16[128,1536]{1,0:T(8,128)(2,1)S(1)} collective-permute-done((bf16[128,1536]{1,0:T(8,128)(2,1)}, bf16[128,1536]{1,0:T(8,128)(2,1)S(1)}, u32[]{:S(2)}, u32[]{:S(2)}) %collective-permute-start.46) | collective-permute-done | bytes 393248 | tf_op jit(solution)/shard_map/ppermute | solution.py:27
  668.4 17.4 %collective-permute-done.45 = bf16[128,1536]{1,0:T(8,128)(2,1)S(1)} collective-permute-done((bf16[128,1536]{1,0:T(8,128)(2,1)}, bf16[128,1536]{1,0:T(8,128)(2,1)S(1)}, u32[]{:S(2)}, u32[]{:S(2)}) %collective-permute-start.45) | collective-permute-done | bytes 393248 | tf_op jit(solution)/shard_map/ppermute | solution.py:27
  (433 shorter events, 217.4 us)
Async XLA Ops:
  7.2 223.5 %all-gather.4.cloned.1.call-start = ((), (), s32[]{:S(2)}) async-start(), calls=%async_computation.2 | async-start | bytes 3538944 | tf_op jit(solution)/shard_map/all_gather | solution.py:438
  8.3 62.7 %collective-permute-start.4 = (bf16[192,1024]{1,0:T(8,128)(2,1)S(1)}, bf16[192,1024]{1,0:T(8,128)(2,1)S(1)}, u32[]{:S(2)}, u32[]{:S(2)}) collective-permute-start(bf16[192,1024]{1,0:T(8,128)(2,1)S(1)} %pad_maximum_fusion.5.refs_0_), channel_id=1, source_target_pairs={{0,4},{4,0},{1,5},{5,1},{2,6},{6,2},{3,7},{7,3},{8,12},{12,8},{9,1... | collective-permute-start | bytes 1179656 | tf_op jit(solution)/shard_map/ppermute | solution.py:27
  16.4 55.1 %collective-permute-start.1 = (bf16[128,1536]{1,0:T(8,128)(2,1)}, bf16[128,1536]{1,0:T(8,128)(2,1)S(1)}, u32[]{:S(2)}, u32[]{:S(2)}) collective-permute-start(bf16[128,1536]{1,0:T(8,128)(2,1)} %bitcast.170), channel_id=1, source_target_pairs={{0,16},{8,24},{16,0},{24,8},{1,17},{9,25},{17,1},{25,9},{2,18},{10... | collective-permute-start | bytes 1179656 | tf_op jit(solution)/shard_map/ppermute | solution.py:27
  16.4 55.2 %collective-permute-start = (bf16[128,1536]{1,0:T(8,128)(2,1)}, bf16[128,1536]{1,0:T(8,128)(2,1)S(1)}, u32[]{:S(2)}, u32[]{:S(2)}) collective-permute-start(bf16[128,1536]{1,0:T(8,128)(2,1)} %bitcast.171), channel_id=1, source_target_pairs={{0,8},{8,0},{16,24},{24,16},{1,9},{9,1},{17,25},{25,17},{2,10},{10... | collective-permute-start | bytes 1179656 | tf_op jit(solution)/shard_map/ppermute | solution.py:27
  21.9 50.2 %collective-permute-start.5 = (bf16[192,1024]{1,0:T(8,128)(2,1)S(1)}, bf16[192,1024]{1,0:T(8,128)(2,1)S(1)}, u32[]{:S(2)}, u32[]{:S(2)}) collective-permute-start(bf16[192,1024]{1,0:T(8,128)(2,1)S(1)} %collective-permute-done.3.refs_1_), channel_id=1, source_target_pairs={{0,4},{4,0},{1,5},{5,1},{2,6},{6,2},{3,7},{7,3},{8,12},{12,8},{9,1... | collective-permute-start | bytes 1179656 | tf_op jit(solution)/shard_map/ppermute | solution.py:27
  38.1 651.5 %reduce-scatter.2.cloned.1.call-start = ((), (), s32[]{:S(2)}) async-start(), calls=%async_computation.1 | async-start | bytes 3538944 | tf_op jit(solution)/shard_map/reduce_scatter | solution.py:508
  71.0 56.7 %collective-permute-start.20 = (bf16[10,192,512]{2,1,0:T(8,128)(2,1)}, bf16[10,192,512]{2,1,0:T(8,128)(2,1)}, u32[]{:S(2)}, u32[]{:S(2)}) collective-permute-start(bf16[10,192,512]{2,1,0:T(8,128)(2,1)} %get-tuple-element.40), channel_id=1, source_target_pairs={{0,2},{2,0},{1,3},{3,1},{4,6},{6,4},{5,7},{7,5},{8,10},{10,8},{9,1... | collective-permute-start | bytes 5898248 | tf_op jit(solution)/shard_map/ppermute | solution.py:27
  73.5 54.3 %collective-permute-start.21 = (bf16[10,192,512]{2,1,0:T(8,128)(2,1)}, bf16[10,192,512]{2,1,0:T(8,128)(2,1)}, u32[]{:S(2)}, u32[]{:S(2)}) collective-permute-start(bf16[10,192,512]{2,1,0:T(8,128)(2,1)} %get-tuple-element.41.refs_0_), channel_id=1, source_target_pairs={{0,4},{4,0},{1,5},{5,1},{2,6},{6,2},{3,7},{7,3},{8,12},{12,8},{9,1... | collective-permute-start | bytes 5898248 | tf_op jit(solution)/shard_map/ppermute | solution.py:27
  127.7 102.8 %collective-permute-start.23 = (bf16[10,192,512]{2,1,0:T(8,128)(2,1)}, bf16[10,192,512]{2,1,0:T(8,128)(2,1)}, u32[]{:S(2)}, u32[]{:S(2)}) collective-permute-start(bf16[10,192,512]{2,1,0:T(8,128)(2,1)} %get-tuple-element.41.refs_0_), channel_id=1, source_target_pairs={{0,1},{1,0},{2,3},{3,2},{4,5},{5,4},{6,7},{7,6},{8,9},{9,8},{10,11... | collective-permute-start | bytes 5898248 | tf_op jit(solution)/shard_map/ppermute | solution.py:27
  127.7 45.5 %collective-permute-start.22 = (bf16[10,192,512]{2,1,0:T(8,128)(2,1)}, bf16[10,192,512]{2,1,0:T(8,128)(2,1)}, u32[]{:S(2)}, u32[]{:S(2)}) collective-permute-start(bf16[10,192,512]{2,1,0:T(8,128)(2,1)} %collective-permute-done.20.refs_1_), channel_id=1, source_target_pairs={{0,4},{4,0},{1,5},{5,1},{2,6},{6,2},{3,7},{7,3},{8,12},{12,8},{9,1... | collective-permute-start | bytes 5898248 | tf_op jit(solution)/shard_map/ppermute | solution.py:27
  174.1 46.5 %collective-permute-start.27 = (bf16[10,192,256]{2,1,0:T(8,128)(2,1)S(1)}, bf16[10,192,256]{2,1,0:T(8,128)(2,1)}, u32[]{:S(2)}, u32[]{:S(2)}) collective-permute-start(bf16[10,192,256]{2,1,0:T(8,128)(2,1)S(1)} %copy-done.85), channel_id=1, source_target_pairs={{0,2},{2,0},{1,3},{3,1},{4,6},{6,4},{5,7},{7,5},{8,10},{10,8},{9,1... | collective-permute-start | bytes 2949128 | tf_op jit(solution)/shard_map/ppermute | solution.py:27
  319.6 228.6 %collective-permute-start.56 = (bf16[10,192,768]{2,1,0:T(8,128)(2,1)}, bf16[10,192,768]{2,1,0:T(8,128)(2,1)}, u32[]{:S(2)}, u32[]{:S(2)}) collective-permute-start(bf16[10,192,768]{2,1,0:T(8,128)(2,1)} %get-tuple-element.53), channel_id=1, source_target_pairs={{0,1},{1,0},{2,3},{3,2},{4,5},{5,4},{6,7},{7,6},{8,9},{9,8},{10,11... | collective-permute-start | bytes 8847368 | tf_op jit(solution)/shard_map/ppermute | solution.py:27
  358.5 115.0 %collective-permute-start.57 = (bf16[10,192,768]{2,1,0:T(8,128)(2,1)}, bf16[10,192,768]{2,1,0:T(8,128)(2,1)}, u32[]{:S(2)}, u32[]{:S(2)}) collective-permute-start(bf16[10,192,768]{2,1,0:T(8,128)(2,1)} %get-tuple-element.55), channel_id=1, source_target_pairs={{0,1},{1,0},{2,3},{3,2},{4,5},{5,4},{6,7},{7,6},{8,9},{9,8},{10,11... | collective-permute-start | bytes 8847368 | tf_op jit(solution)/shard_map/ppermute | solution.py:27
  394.4 56.8 %collective-permute-start.42 = (bf16[128,1536]{1,0:T(8,128)(2,1)S(1)}, bf16[128,1536]{1,0:T(8,128)(2,1)}, u32[]{:S(2)}, u32[]{:S(2)}) collective-permute-start(bf16[128,1536]{1,0:T(8,128)(2,1)S(1)} %multiply_convert_fusion), channel_id=1, source_target_pairs={{0,16},{8,24},{16,0},{24,8},{1,17},{9,25},{17,1},{25,9},{2,18},{10... | collective-permute-start | bytes 1179656 | tf_op jit(solution)/shard_map/ppermute | solution.py:27
  394.4 56.8 %collective-permute-start.41 = (bf16[128,1536]{1,0:T(8,128)(2,1)S(1)}, bf16[128,1536]{1,0:T(8,128)(2,1)}, u32[]{:S(2)}, u32[]{:S(2)}) collective-permute-start(bf16[128,1536]{1,0:T(8,128)(2,1)S(1)} %multiply_convert_fusion), channel_id=1, source_target_pairs={{0,8},{8,0},{16,24},{24,16},{1,9},{9,1},{17,25},{25,17},{2,10},{10... | collective-permute-start | bytes 1179656 | tf_op jit(solution)/shard_map/ppermute | solution.py:27
  406.2 148.9 %collective-permute-start.60 = (bf16[10,192,768]{2,1,0:T(8,128)(2,1)}, bf16[10,192,768]{2,1,0:T(8,128)(2,1)}, u32[]{:S(2)}, u32[]{:S(2)}) collective-permute-start(bf16[10,192,768]{2,1,0:T(8,128)(2,1)} %get-tuple-element.58), channel_id=1, source_target_pairs={{0,1},{1,0},{2,3},{3,2},{4,5},{5,4},{6,7},{7,6},{8,9},{9,8},{10,11... | collective-permute-start | bytes 8847368 | tf_op jit(solution)/shard_map/ppermute | solution.py:27
  473.5 73.2 %collective-permute-start.52 = (bf16[4,192,1024]{2,1,0:T(8,128)(2,1)S(1)}, bf16[4,192,1024]{2,1,0:T(8,128)(2,1)S(1)}, u32[]{:S(2)}, u32[]{:S(2)}) collective-permute-start(bf16[4,192,1024]{2,1,0:T(8,128)(2,1)S(1)} %fusion.20), channel_id=1, source_target_pairs={{0,1},{1,0},{2,3},{3,2},{4,5},{5,4},{6,7},{7,6},{8,9},{9,8},{10,11... | collective-permute-start | bytes 4718600 | tf_op jit(solution)/shard_map/ppermute | solution.py:27
  477.8 76.0 %collective-permute-start.58 = (bf16[10,192,768]{2,1,0:T(8,128)(2,1)S(1)}, bf16[10,192,768]{2,1,0:T(8,128)(2,1)S(1)}, u32[]{:S(2)}, u32[]{:S(2)}) collective-permute-start(bf16[10,192,768]{2,1,0:T(8,128)(2,1)S(1)} %add_convert_fusion.1), channel_id=1, source_target_pairs={{0,4},{4,0},{1,5},{5,1},{2,6},{6,2},{3,7},{7,3},{8,12},{12,8},{9,1... | collective-permute-start | bytes 8847368 | tf_op jit(solution)/shard_map/ppermute | solution.py:27
  487.0 55.9 %collective-permute-start.49 = (f32[2,1536]{1,0:T(2,128)S(1)}, f32[2,1536]{1,0:T(2,128)S(1)}, u32[]{:S(2)}, u32[]{:S(2)}) collective-permute-start(f32[2,1536]{1,0:T(2,128)S(1)} %fusion.88), channel_id=1, source_target_pairs={{0,4},{4,0},{1,5},{5,1},{2,6},{6,2},{3,7},{7,3},{8,12},{12,8},{9,1... | collective-permute-start | bytes 36872 | tf_op jit(solution)/shard_map/ppermute | solution.py:27
  546.7 151.1 %collective-permute-start.55 = (bf16[10,192,768]{2,1,0:T(8,128)(2,1)}, bf16[10,192,768]{2,1,0:T(8,128)(2,1)}, u32[]{:S(2)}, u32[]{:S(2)}) collective-permute-start(bf16[10,192,768]{2,1,0:T(8,128)(2,1)} %get-tuple-element.51), channel_id=1, source_target_pairs={{0,1},{1,0},{2,3},{3,2},{4,5},{5,4},{6,7},{7,6},{8,9},{9,8},{10,11... | collective-permute-start | bytes 8847368 | tf_op jit(solution)/shard_map/ppermute | solution.py:27
  548.2 109.6 %collective-permute-start.53 = (bf16[2,192,1024]{2,1,0:T(8,128)(2,1)}, bf16[2,192,1024]{2,1,0:T(8,128)(2,1)S(1)}, u32[]{:S(2)}, u32[]{:S(2)}) collective-permute-start(bf16[2,192,1024]{2,1,0:T(8,128)(2,1)} %dynamic-slice_bitcast_fusion), channel_id=1, source_target_pairs={{0,4},{4,0},{1,5},{5,1},{2,6},{6,2},{3,7},{7,3},{8,12},{12,8},{9,1... | collective-permute-start | bytes 2359304 | tf_op jit(solution)/shard_map/ppermute | solution.py:27
  553.8 144.0 %collective-permute-start.59 = (bf16[10,192,768]{2,1,0:T(8,128)(2,1)}, bf16[10,192,768]{2,1,0:T(8,128)(2,1)}, u32[]{:S(2)}, u32[]{:S(2)}) collective-permute-start(bf16[10,192,768]{2,1,0:T(8,128)(2,1)} %add_convert_fusion.2), channel_id=1, source_target_pairs={{0,4},{4,0},{1,5},{5,1},{2,6},{6,2},{3,7},{7,3},{8,12},{12,8},{9,1... | collective-permute-start | bytes 8847368 | tf_op jit(solution)/shard_map/ppermute | solution.py:27
  559.8 133.0 %collective-permute-start.61 = (bf16[10,192,768]{2,1,0:T(8,128)(2,1)}, bf16[10,192,768]{2,1,0:T(8,128)(2,1)}, u32[]{:S(2)}, u32[]{:S(2)}) collective-permute-start(bf16[10,192,768]{2,1,0:T(8,128)(2,1)} %add_convert_fusion), channel_id=1, source_target_pairs={{0,2},{2,0},{1,3},{3,1},{4,6},{6,4},{5,7},{7,5},{8,10},{10,8},{9,1... | collective-permute-start | bytes 8847368 | tf_op jit(solution)/shard_map/ppermute | solution.py:27
  561.6 96.1 %collective-permute-start.44 = (bf16[128,1536]{1,0:T(8,128)(2,1)S(1)}, bf16[128,1536]{1,0:T(8,128)(2,1)S(1)}, u32[]{:S(2)}, u32[]{:S(2)}) collective-permute-start(bf16[128,1536]{1,0:T(8,128)(2,1)S(1)} %get-tuple-element.86), channel_id=1, source_target_pairs={{0,8},{8,0},{16,24},{24,16},{1,9},{9,1},{17,25},{25,17},{2,10},{10... | collective-permute-start | bytes 1179656 | tf_op jit(solution)/shard_map/ppermute | solution.py:27
  (133 other events, 2331.2 us)
Sparse Core Ops, SparseCore 0:
  38.2 88.7 all-gather.3
  397.4 90.1 reduce-scatter.1

commit v3 on v2

v3 whole, which is shorter than its diff:
```python
import functools

import jax
import jax.numpy as jnp
from jax import lax
from jax.experimental import pallas as pl
from jax.experimental.pallas import tpu as pltpu
from jax.sharding import Mesh, PartitionSpec as P

HEAD_SIZE = 64
EXPERTS = 40
TOPK = 8
CAP = 48

epsilon = 1e-06
rope_base = 10000.0
residual_factor = 0.22
score_factor = 0.015625
masked_value = -1e30

f32 = jnp.float32
bf16 = jnp.bfloat16


def swap(value, axis, step):
    count = lax.axis_size(axis)
    return lax.ppermute(value, axis, [(i, i ^ step) for i in range(count)])


def tie(*values):
    return lax.optimization_barrier(values)


def pick(array, index, dim):
    return lax.dynamic_index_in_dim(array, index, dim, keepdims=False)


def rms_factor(rows):
    return lax.rsqrt(jnp.mean(rows * rows, axis=-1, keepdims=True) + epsilon)


def norm_back(rows, factor, gain, upstream):
    scaled = upstream * gain
    inner = jnp.mean(scaled * rows, axis=-1, keepdims=True)
    return factor * scaled - rows * factor * factor * factor * inner


def rotary(rows, cosine, sine):
    half = rows.shape[-1] // 2
    first = rows[..., :half]
    second = rows[..., half:]
    return jnp.concatenate(
        [first * cosine - second * sine, first * sine + second * cosine], axis=-1
    )


def contract_rows(left, right):
    return lax.dot_general(left, right, (((0,), (0,)), ((), ())), preferred_element_type=f32)


def contract_cols(left, right):
    return lax.dot_general(left, right, (((1,), (1,)), ((), ())), preferred_element_type=f32)


def gather_gx(block):
    return [block] + [swap(block, "gx", s) for s in range(1, lax.axis_size("gx"))]


def over_y(value):
    return [swap(value, "gt", s) for s in range(1, lax.axis_size("gt"))]


def spread_y(values):
    return [swap(value, "gt", s) for s, value in enumerate(values, 1)]


def part_places():
    many = lax.axis_size("gt")
    places = [0, 2] + [4 * s for s in range(1, many)] + [4 * s + 2 for s in range(1, many)]
    return places + [p + 1 for p in places]


def own_place():
    me = (lax.axis_index("gt") * 2 + lax.axis_index("gw")) * 2 + lax.axis_index("co")
    return jnp.full((1,), me, jnp.int32)


def own_side():
    return jnp.full((1,), lax.axis_index("gw"), jnp.int32)


def place_parts(parts):
    places = part_places()
    count = len(parts)

    def kernel(me_ref, *refs):
        for place, ref in zip(places, refs[:count]):
            refs[count][me_ref[0] ^ place] = ref[...]

    full = pl.BlockSpec(memory_space=pltpu.VMEM)
    return pl.pallas_call(
        kernel,
        out_shape=jax.ShapeDtypeStruct((count,) + parts[0].shape, parts[0].dtype),
        in_specs=[pl.BlockSpec(memory_space=pltpu.SMEM)] + [full] * count,
        out_specs=full,
        compiler_params=pltpu.CompilerParams(vmem_limit_bytes=40 * 2**20),
        name="place_parts",
    )(own_place(), *parts)


def halve_weights(gate, up, down, start, experts):
    rows, full = gate.shape[1:]
    half = full // 2

    def kernel(side_ref, gate_ref, up_ref, down_ref, keep, give):
        def put(low, out):
            for i, ref in enumerate((gate_ref, up_ref, down_ref)):
                out[0, :, i * half : (i + 1) * half] = ref[0, :, low : low + half]

        @pl.when(side_ref[0] == 0)
        def _():
            put(0, keep)
            put(half, give)

        @pl.when(side_ref[0] != 0)
        def _():
            put(half, keep)
            put(0, give)

    def block(columns, first):
        return pl.BlockSpec((1, rows, columns), lambda e, *_: (e + first, 0, 0))

    shape = jax.ShapeDtypeStruct((experts, rows, 3 * half), bf16)
    return pl.pallas_call(
        kernel,
        grid_spec=pltpu.PrefetchScalarGridSpec(
            num_scalar_prefetch=1,
            grid=(experts,),
            in_specs=[block(full, start)] * 3,
            out_specs=[block(3 * half, 0)] * 2,
        ),
        out_shape=[shape, shape],
        name="halve_weights",
    )(own_side(), gate, up, down)


def finish_gradients(summed, crossed, start, before, total_experts):
    experts, rows, columns = crossed.shape
    half = columns // 3
    count = len(summed)
    aliased = 0 if before is None else 3

    def kernel(side_ref, *refs):
        total = refs[0][0].astype(f32)
        for ref in refs[1:count]:
            total = total + ref[0].astype(f32)
        other = refs[count][0].astype(f32)

        def put(low, value):
            for i, out in enumerate(refs[count + 1 + aliased :]):
                out[0, :, low : low + half] = value[:, i * half : (i + 1) * half]

        @pl.when(side_ref[0] == 0)
        def _():
            put(0, total)
            put(half, other)

        @pl.when(side_ref[0] != 0)
        def _():
            put(half, total)
            put(0, other)

    def block(columns, first):
        return pl.BlockSpec((1, rows, columns), lambda e, *_: (e + first, 0, 0))

    shape = jax.ShapeDtypeStruct((total_experts, rows, 2 * half), f32)
    return pl.pallas_call(
        kernel,
        grid_spec=pltpu.PrefetchScalarGridSpec(
            num_scalar_prefetch=1,
            grid=(experts,),
            in_specs=[block(columns, 0)] * (count + 1) + [pl.BlockSpec(memory_space=pl.ANY)] * aliased,
            out_specs=[block(2 * half, start)] * 3,
        ),
        out_shape=[shape] * 3,
        input_output_aliases={count + 2 + i: i for i in range(aliased)},
        name="finish_gradients",
    )(own_side(), *summed, crossed, *(before or ()))


def scatter_gy(grad):
    many = lax.axis_size("gt")
    t, w, k = lax.axis_index("gt"), lax.axis_index("gw"), lax.axis_index("co")
    cols = grad.shape[1]
    grad = grad.reshape(many * 2, 2, -1, cols)
    total = pick(grad, k, 1).astype(f32) + swap(pick(grad, 1 - k, 1), "co", 1).astype(f32)
    total = total.astype(bf16).reshape(many, 2, -1, cols)
    own = pick(total, w, 1).astype(f32) + swap(pick(total, 1 - w, 1), "gw", 1).astype(f32)
    own = own.astype(bf16)
    total = pick(own, t, 0).astype(f32)
    for s in range(1, many):
        total = total + swap(pick(own, t ^ s, 0), "gt", s).astype(f32)
    return total


def sum_everywhere(value):
    for axis in ("co", "gw", "gt", "gx"):
        step = 1
        while step < lax.axis_size(axis):
            value = value + swap(value, axis, step)
            step = step * 2
    return value


def slot_mask(slot_row):
    wanted = lax.broadcasted_iota(jnp.int32, (CAP, slot_row.shape[1]), 0).astype(f32)
    return slot_row == wanted


def gather_slots(sources, order, slots):
    blocks, experts, tokens = slots.shape
    listed = isinstance(sources, list)
    width = sources[0].shape[1] if listed else order[1]

    def find(slots_ref, rows, out_ref):
        mask = jnp.concatenate([slot_mask(slots_ref[0, e : e + 1, :]) for e in range(experts)], axis=0)
        found = jnp.dot(mask.astype(f32).astype(bf16), rows, preferred_element_type=f32)
        out_ref[...] = found.astype(bf16).reshape(experts, 1, CAP, width)

    def kernel_list(order_ref, slots_ref, *refs):
        for i in range(blocks):

            @pl.when(pl.program_id(0) == i)
            def _(i=i):
                refs[blocks + 1][...] = refs[i][...]

        find(slots_ref, refs[blocks + 1][...], refs[blocks])

    def kernel_array(order_ref, slots_ref, rows_ref, out_ref):
        find(slots_ref, rows_ref[0], out_ref)

    if listed:
        specs = [pl.BlockSpec((tokens, width), lambda b, *_: (0, 0))] * blocks
        scratch = [pltpu.VMEM((tokens, width), bf16)]
        prefetch = jnp.zeros((1,), jnp.int32)
    else:
        specs = [pl.BlockSpec((1, tokens, width), lambda b, order_ref: (order_ref[b], 0, 0))]
        scratch = []
        prefetch = order[0]
        sources = [sources]
    return pl.pallas_call(
        kernel_list if listed else kernel_array,
        grid_spec=pltpu.PrefetchScalarGridSpec(
            num_scalar_prefetch=1,
            grid=(blocks,),
            in_specs=[pl.BlockSpec((1, experts, tokens), lambda b, *_: (b, 0, 0))] + specs,
            out_specs=pl.BlockSpec((experts, 1, CAP, width), lambda b, *_: (0, b, 0, 0)),
            scratch_shapes=scratch,
        ),
        out_shape=jax.ShapeDtypeStruct((experts, blocks, CAP, width), bf16),
        compiler_params=pltpu.CompilerParams(vmem_limit_bytes=40 * 2**20),
        cost_estimate=pl.CostEstimate(
            flops=2 * blocks * tokens * experts * CAP * width,
            bytes_accessed=2 * blocks * (tokens + experts * CAP) * width,
            transcendentals=0,
        ),
        name="gather_slots",
    )(prefetch, slots, *sources)


def sum_slots(slot_rows, slots, order):
    blocks, experts, tokens = slots.shape
    width = slot_rows[0].shape[3]

    def kernel(order_ref, slots_ref, *refs):
        total, first = None, 0
        for ref in refs[:-1]:
            mine = ref.shape[0]
            mask = jnp.concatenate(
                [slot_mask(slots_ref[0, e : e + 1, :]) for e in range(first, first + mine)], axis=0
            )
            first = first + mine
            part = contract_rows(mask.astype(f32).astype(bf16), ref[...].reshape(mine * CAP, width))
            total = part if total is None else total + part
        refs[-1][0] = total.astype(bf16)

    return pl.pallas_call(
        kernel,
        grid_spec=pltpu.PrefetchScalarGridSpec(
            num_scalar_prefetch=1,
            grid=(blocks,),
            in_specs=[pl.BlockSpec((1, experts, tokens), lambda b, *_: (b, 0, 0))]
            + [pl.BlockSpec((r.shape[0], 1, CAP, width), lambda b, *_: (0, b, 0, 0)) for r in slot_rows],
            out_specs=pl.BlockSpec((1, tokens, width), lambda b, order_ref: (order_ref[b], 0, 0)),
        ),
        out_shape=jax.ShapeDtypeStruct((blocks, tokens, width), bf16),
        compiler_params=pltpu.CompilerParams(vmem_limit_bytes=40 * 2**20),
        cost_estimate=pl.CostEstimate(
            flops=2 * blocks * tokens * experts * CAP * width,
            bytes_accessed=2 * blocks * (tokens + experts * CAP) * width,
            transcendentals=0,
        ),
        name="sum_slots",
    )(order, slots, *slot_rows)


def run_experts(rows_in, back_in, weights, start, slots, chances):
    blocks, _, width = rows_in.shape[1:]
    experts = weights[0].shape[0]
    places = part_places()
    tokens = slots.shape[2]
    cut, half = weights[0].shape[1], weights[0].shape[2] // 3
    count = len(places)
    total_slots = blocks * CAP

    def kernel(me_ref, rows_ref, back_ref, slots_ref, chances_ref, *refs):
        rows_out, mixed_out, chance_out = refs[count : count + 3]
        grads = refs[count + 3 : 2 * count + 3]
        gu_full, d_full, gu_total, d_total = refs[2 * count + 3 :]
        spots = [pl.ds(pl.multiple_of((me_ref[0] ^ place) * cut, cut), cut) for place in places]
        for spot, part in zip(spots, refs[:count]):
            gu_full[spot, :] = part[0, :, : 2 * half]
            d_full[spot, :] = part[0, :, 2 * half :]
        rows = rows_ref[0].reshape(total_slots, width)
        back = back_ref[0].reshape(total_slots, width)
        masks = [slot_mask(slots_ref[0, b : b + 1, :]) for b in range(blocks)]
        chance = jnp.concatenate(
            [
                jnp.sum(jnp.where(masks[b], chances_ref[0, b : b + 1, :], 0.0), axis=1, keepdims=True)
                for b in range(blocks)
            ],
            axis=0,
        )
        both = jnp.dot(rows, gu_full[...], preferred_element_type=f32)
        active_back = jnp.dot(back, d_full[...], preferred_element_type=f32) * residual_factor
        gate, upper = both[:, :half], both[:, half:]
        sigma = jax.nn.sigmoid(gate)
        silu = gate * sigma
        active = silu * upper
        chance_back = jnp.sum(active * active_back, axis=1, keepdims=True)
        for b in range(blocks):
            column = chance_back[b * CAP : (b + 1) * CAP]
            chance_out[0, b : b + 1, :] = jnp.sum(jnp.where(masks[b], column, 0.0), axis=0, keepdims=True)
        scaled = (active * chance).astype(bf16)
        active_back = active_back * chance
        gate_back = active_back * upper * (sigma * (1.0 + gate * (1.0 - sigma)))
        upper_back = active_back * silu
        both_back = jnp.concatenate([gate_back.astype(bf16), upper_back.astype(bf16)], axis=1)
        rows_out[0] = contract_cols(both_back, gu_full[...]).astype(bf16).reshape(blocks, CAP, width)
        mixed_out[0] = contract_cols(scaled, d_full[...]).astype(bf16).reshape(blocks, CAP, width)
        gu_total[...] = contract_rows(rows, both_back).astype(bf16)
        d_total[...] = (contract_rows(back, scaled) * residual_factor).astype(bf16)
        for spot, grad in zip(spots, grads):
            grad[0, :, : 2 * half] = gu_total[spot, :]
            grad[0, :, 2 * half :] = d_total[spot, :]

    def block(shape, first=0):
        zeros = (0,) * len(shape)
        return pl.BlockSpec((1,) + shape, lambda e, *_: (e + first,) + zeros)

    flops = 2 * experts * total_slots * width * half * 9
    grad_shape = jax.ShapeDtypeStruct((experts, cut, 3 * half), bf16)
    slot_shape = jax.ShapeDtypeStruct((experts, blocks, CAP, width), bf16)
    out = pl.pallas_call(
        kernel,
        grid_spec=pltpu.PrefetchScalarGridSpec(
            num_scalar_prefetch=1,
            grid=(experts,),
            in_specs=[
                block((blocks, CAP, width), start),
                block((blocks, CAP, width), start),
                block((blocks, tokens), start),
                block((blocks, tokens), start),
            ]
            + [block((cut, 3 * half))] * count,
            out_specs=[block((blocks, CAP, width)), block((blocks, CAP, width)), block((blocks, tokens))]
            + [block((cut, 3 * half))] * count,
            scratch_shapes=[
                pltpu.VMEM((width, 2 * half), bf16),
                pltpu.VMEM((width, half), bf16),
                pltpu.VMEM((width, 2 * half), bf16),
                pltpu.VMEM((width, half), bf16),
            ],
        ),
        out_shape=[slot_shape, slot_shape, jax.ShapeDtypeStruct((experts, blocks, tokens), f32)]
        + [grad_shape] * count,
        compiler_params=pltpu.CompilerParams(vmem_limit_bytes=60 * 2**20),
        cost_estimate=pl.CostEstimate(
            flops=flops,
            bytes_accessed=2 * experts * (4 * total_slots * width + 6 * half * width),
            transcendentals=experts * total_slots * half,
        ),
        name="run_experts",
    )(own_place(), rows_in, back_in, slots, chances, *weights)
    gradients = {(p // 4, (p // 2) % 2, p % 2): g for p, g in zip(places, out[3:])}
    return out[0], out[1], out[2], gradients


def block_scores(query_rows, key_rows, positions):
    raw = jnp.einsum("qhgd,khd->hgqk", query_rows, key_rows, preferred_element_type=f32)
    return jnp.where(positions[None, :] <= positions[:, None], raw * score_factor, masked_value)


def attend_forward(query_rows, key_rows, value_rows, positions):
    scores = block_scores(query_rows, key_rows, positions)
    top = jnp.max(scores, axis=-1, keepdims=True)
    weights = jnp.exp(scores - top)
    total = jnp.sum(weights, axis=-1, keepdims=True)
    probs = (weights / total).astype(bf16)
    mixed = jnp.einsum("hgqk,khd->qhgd", probs, value_rows, preferred_element_type=f32)
    return (mixed.astype(bf16).reshape(query_rows.shape[0], -1), top + jnp.log(total))


def attend_backward(query_rows, key_rows, value_rows, heads_back, spread, positions):
    scores = block_scores(query_rows, key_rows, positions)
    probs = jnp.exp(scores - spread)
    prob_back = jnp.einsum("qhgd,khd->hgqk", heads_back, value_rows, preferred_element_type=f32)
    inner = jnp.sum(probs * prob_back, axis=-1, keepdims=True)
    score_back = (probs * (prob_back - inner)).astype(bf16)
    query_back = jnp.einsum("hgqk,khd->qhgd", score_back, key_rows, preferred_element_type=f32)
    key_back = jnp.einsum("hgqk,qhgd->khd", score_back, query_rows, preferred_element_type=f32)
    value_back = jnp.einsum(
        "hgqk,qhgd->khd", probs.astype(bf16), heads_back, preferred_element_type=f32
    )
    return (query_back * score_factor, key_back * score_factor, value_back)


def local(
    tokens,
    first_gain,
    query_weight,
    key_matrix,
    value_matrix,
    out_weight,
    second_gain,
    gate_weight,
    up_weight,
    down_weight,
    routes,
    route_logits,
    cotangent,
):
    groups, many = lax.axis_size("gx"), lax.axis_size("gt")
    me_x, me_w = lax.axis_index("gx"), lax.axis_index("gw")
    own_tokens = tokens[0]
    rows, width = own_tokens.shape
    query_cols = query_weight.shape[1]
    key_cols = key_matrix.shape[1]
    query_heads = query_cols // HEAD_SIZE
    pair_heads = key_cols // HEAD_SIZE
    ratio = query_heads // pair_heads
    experts = gate_weight.shape[0]
    some = (experts + 1) // 2
    spans = ((0, some), (some, experts - some))

    token_blocks = gather_gx(own_tokens)
    attention = jnp.concatenate(
        [query_weight, key_matrix, value_matrix, out_weight.T], axis=1
    )
    down_turned = jnp.swapaxes(down_weight, 1, 2)
    (keep_0, give_0), (keep_1, give_1) = [
        halve_weights(gate_weight, up_weight, down_turned, *span) for span in spans
    ]
    across = swap(attention, "gw", 1)
    along = over_y(attention)
    both = over_y(across)
    across, give_0 = tie(across, give_0)
    both, keep_0, keep_1 = tie(both, keep_0, keep_1)
    attention_parts = [attention, across] + along + both
    attention_full = place_parts(attention_parts + [swap(p, "co", 1) for p in attention_parts])
    attention_full = attention_full.reshape(width, -1)
    joined = attention_full[:, : query_cols + 2 * key_cols]
    out_full = attention_full[:, query_cols + 2 * key_cols :]

    across_0, along_0 = swap(give_0, "gw", 1), over_y(keep_0)
    mirror_keep = [swap(keep_0, "co", 1), swap(keep_1, "co", 1)]

    logits = route_logits[0].T
    weights = jnp.exp(logits - jnp.max(logits, axis=0, keepdims=True))
    chance = weights / jnp.sum(weights, axis=0, keepdims=True)
    chance_high = lax.reduce_precision(chance, 8, 7)
    routing = jnp.concatenate([routes[0].T.astype(f32), chance_high, chance - chance_high], axis=0)
    routing = jnp.pad(routing.astype(bf16).T, ((0, 0), (0, 128 - 3 * TOPK)))
    payload = jnp.concatenate([cotangent[0], routing], axis=1)
    payload, token_blocks = tie(payload, token_blocks)
    turned = jnp.stack([((me_x ^ s) * 2 + (me_w ^ w)) for w in range(2) for s in range(groups)])
    gathered = lax.all_gather(payload, ("gx", "gw"), axis=0)

    sequence = jnp.concatenate(token_blocks, axis=0).astype(f32)
    length = sequence.shape[0]
    factor_all = rms_factor(sequence)
    sequence_rows = (sequence * factor_all * first_gain).astype(bf16)
    projected = jnp.dot(sequence_rows, joined, preferred_element_type=f32)
    positions = jnp.concatenate(
        [(me_x ^ s) * rows + jnp.arange(rows, dtype=jnp.int32) for s in range(groups)]
    )
    freq = rope_base ** (-(jnp.arange(HEAD_SIZE // 2, dtype=f32) * 2.0 / HEAD_SIZE))
    angle = positions.astype(f32)[:, None] * freq[None, :]
    cosine = jnp.cos(angle)[:, None, :]
    sine = jnp.sin(angle)[:, None, :]
    query_rows = rotary(projected[:, :query_cols].reshape(length, query_heads, HEAD_SIZE), cosine, sine)
    query_rows = query_rows.astype(bf16).reshape(length, pair_heads, ratio, HEAD_SIZE)
    key_rows = rotary(
        projected[:, query_cols : query_cols + key_cols].reshape(length, pair_heads, HEAD_SIZE),
        cosine,
        sine,
    ).astype(bf16)
    value_rows = (
        projected[:, query_cols + key_cols :].reshape(length, pair_heads, HEAD_SIZE).astype(bf16)
    )
    heads, spread = attend_forward(query_rows, key_rows, value_rows, positions)
    branch_parts = contract_cols(heads, out_full).astype(bf16)

    branch_parts, across_0, along_0, mirror_keep, keep_1, give_1 = tie(
        branch_parts, across_0, along_0, mirror_keep, keep_1, give_1
    )
    branch_got = [
        swap(branch_parts[s * rows : (s + 1) * rows], "gx", s) for s in range(1, groups)
    ]
    across_1, along_1 = swap(give_1, "gw", 1), over_y(keep_1)
    branch_got[0], branch_got[-1], across_0, along_0 = tie(
        branch_got[0], branch_got[-1], across_0, along_0
    )
    mirror_across = [swap(across_0, "co", 1)]
    mirror_along = [[swap(p, "co", 1) for p in along_0]]
    branch = branch_parts[:rows].astype(f32)
    for value in branch_got:
        branch = branch + value.astype(f32)

    routing_rows = jnp.swapaxes(gathered[:, :, width : width + 3 * TOPK].astype(f32), 1, 2)
    routing_rows = jnp.stack([pick(routing_rows, turned[b], 0) for b in range(2 * groups)])
    ids = (me_x * experts + jnp.arange(experts, dtype=jnp.int32)).astype(f32)
    same = routing_rows[:, None, :TOPK, :] == ids[None, :, None, None]
    chances = routing_rows[:, TOPK : 2 * TOPK] + routing_rows[:, 2 * TOPK :]
    hits = jnp.sum(same.astype(f32), axis=2)
    before = jnp.triu(jnp.ones((rows, rows), f32), 1)
    slots = jnp.where(hits > 0.0, jnp.einsum("beu,ut->bet", hits, before), -1.0)
    chosen = jnp.sum(jnp.where(same, chances[:, None], 0.0), axis=2)
    back_in = gather_slots(gathered, (turned, width), slots)

    hidden = own_tokens.astype(f32)
    middle = hidden + residual_factor * branch
    factor_two = rms_factor(middle)
    normed_two = (middle * factor_two * second_gain).astype(bf16)

    normed_two, back_in, across_0, across_1, along_1, mirror_across, mirror_along = tie(
        normed_two, back_in, across_0, across_1, along_1, mirror_across, mirror_along
    )
    normed_parts = gather_gx(normed_two)
    both_0 = over_y(across_0)
    normed_rows = normed_parts + [swap(p, "gw", 1) for p in normed_parts]

    normed_rows[:groups], both_0, across_1, along_1 = tie(normed_rows[:groups], both_0, across_1, along_1)
    both_1 = over_y(across_1)
    mirror_both = [[swap(p, "co", 1) for p in both_0]]
    mirror_across.append(swap(across_1, "co", 1))
    mirror_along.append([swap(p, "co", 1) for p in along_1])
    mirror_both.append([swap(p, "co", 1) for p in both_1])
    rows_in = gather_slots(normed_rows, None, slots)
    by_expert = (jnp.swapaxes(slots, 0, 1), jnp.swapaxes(chosen, 0, 1))
    rows_back, mixed_parts, chance_parts, gradients = [], [], [], []
    for i, own in enumerate(
        ([keep_0, across_0] + along_0 + both_0, [keep_1, across_1] + along_1 + both_1)
    ):
        mirrors = [mirror_keep[i], mirror_across[i]] + mirror_along[i] + mirror_both[i]
        result = run_experts(rows_in, back_in, own + mirrors, spans[i][0], *by_expert)
        for lot, value in zip((rows_back, mixed_parts, chance_parts, gradients), result):
            lot.append(value)

    got = [{}, {}]

    def joint(i, t, w):
        return gradients[i][t, w, 0].astype(f32) + got[i][t, w].astype(f32)

    others = range(1, many)
    got[0] = {(t, w): swap(gradients[0][t, w, 1], "co", 1) for t in range(many) for w in (0, 1)}
    got[0], rows_back = tie(got[0], rows_back)
    got[1] = {(t, 1): swap(gradients[1][t, 1, 1], "co", 1) for t in others}
    plain = jnp.arange(2 * groups, dtype=jnp.int32)
    summed = sum_slots(rows_back, slots, plain)
    order = [s for s in (2, 3, 1) if s < groups] + list(range(4, groups)) + [0]
    crossed = {s: swap(summed[groups + s], "gw", 1) for s in order}
    far = [joint(0, t, 1).astype(bf16) for t in others]
    crossed[order[0]], far, got[1], mixed_parts = tie(crossed[order[0]], far, got[1], mixed_parts)
    along_one_0 = spread_y(far)
    mixed_rows = sum_slots(mixed_parts, slots, turned)
    chance_part = jnp.swapaxes(jnp.concatenate(chance_parts, axis=0), 0, 1)
    chance_rows = jnp.sum(jnp.where(same, chance_part[:, :, None, :], 0.0), axis=1)
    normed_got = [
        swap((summed[s].astype(f32) + crossed[s].astype(f32)).astype(bf16), "gx", s)
        for s in range(1, groups)
    ]
    near_gradient = gradients[1][0, 1, 1]
    crossed[0], mixed_rows, near_gradient, chance_rows = tie(crossed[0], mixed_rows, near_gradient, chance_rows)
    got[1][0, 1] = swap(near_gradient, "co", 1)
    chance_crossed = swap(chance_rows[groups:], "gw", 1)
    far = [joint(1, t, 1).astype(bf16) for t in others]
    mixed = lax.psum_scatter(mixed_rows, ("gx", "gw"), scatter_dimension=0).astype(f32)
    output = (middle + residual_factor * mixed).astype(bf16)
    normed_two_back = summed[0].astype(f32) + crossed[0].astype(f32)
    for value in normed_got:
        normed_two_back = normed_two_back + value.astype(f32)

    upstream = cotangent[0].astype(f32)
    middle_back = upstream + norm_back(middle, factor_two, second_gain, normed_two_back)
    second_part = jnp.sum(normed_two_back * middle * factor_two, axis=0)
    branch_back = (residual_factor * middle_back).astype(bf16)
    branch_back, along_one_0, got[1], far, chance_crossed = tie(
        branch_back, along_one_0, got[1], far, chance_crossed
    )
    branch_back_blocks = gather_gx(branch_back)
    along_one_1 = spread_y(far)

    def near(i, along):
        total = joint(i, 0, 1)
        for value in along:
            total = total + value.astype(f32)
        return total.astype(bf16)

    crossed_0 = swap(near(0, along_one_0), "gw", 1)
    far = [joint(0, t, 0).astype(bf16) for t in others]
    last = {(t, 0): gradients[1][t, 0, 1] for t in range(many)}
    branch_back_blocks, along_one_1, crossed_0, far, last = tie(
        branch_back_blocks, along_one_1, crossed_0, far, last
    )
    along_zero_0 = spread_y(far)
    crossed_1 = swap(near(1, along_one_1), "gw", 1)
    got[1].update({p: swap(v, "co", 1) for p, v in last.items()})

    piece = jnp.concatenate(branch_back_blocks, axis=0)
    heads_back = jnp.dot(piece, out_full, preferred_element_type=f32)
    out_grad = contract_rows(piece, heads)
    heads_back = heads_back.astype(bf16).reshape(length, pair_heads, ratio, HEAD_SIZE)
    query_back, key_back, value_back = attend_backward(
        query_rows, key_rows, value_rows, heads_back, spread, positions
    )
    query_back = rotary(query_back.reshape(length, query_heads, HEAD_SIZE), cosine, -sine)
    key_back = rotary(key_back, cosine, -sine)
    projected_back = jnp.concatenate(
        [
            query_back.reshape(length, query_cols),
            key_back.reshape(length, key_cols),
            value_back.reshape(length, key_cols),
        ],
        axis=1,
    ).astype(bf16)
    normed_one_parts = contract_cols(projected_back, joined)
    first_part = jnp.sum(normed_one_parts * (sequence * factor_all), axis=0)
    normed_one_parts = normed_one_parts.astype(bf16)
    normed_one_parts, got[1] = tie(normed_one_parts, got[1])
    normed_got = [
        swap(normed_one_parts[s * rows : (s + 1) * rows], "gx", s) for s in range(1, groups)
    ]
    far = [joint(1, t, 0).astype(bf16) for t in others]
    along_zero_0, far = tie(along_zero_0, far)
    along_zero_1 = spread_y(far)
    joined_grad = contract_rows(sequence_rows, projected_back)
    attention_sum = scatter_gy(jnp.concatenate([joined_grad, out_grad], axis=1).astype(bf16))
    gains = jnp.stack([first_part, second_part])
    gains, normed_got, chance_rows = tie(gains, normed_got, chance_rows)
    gains = sum_everywhere(gains)
    normed_one_back = normed_one_parts[:rows].astype(f32)
    for value in normed_got:
        normed_one_back = normed_one_back + value.astype(f32)
    tokens_back = middle_back + norm_back(hidden, factor_all[:rows], first_gain, normed_one_back)
    chance_rows = chance_rows[:groups] + chance_crossed
    chance_back = chance_rows[0]
    for s in range(1, groups):
        chance_back = chance_back + swap(chance_rows[s], "gx", s)
    logit_back = chance * (chance_back - jnp.sum(chance * chance_back, axis=0, keepdims=True))
    sums = finish_gradients(
        [gradients[0][0, 0, 0], got[0][0, 0]] + along_zero_0, crossed_0, 0, None, experts
    )
    gate_sum, up_sum, down_sum = finish_gradients(
        [gradients[1][0, 0, 0], got[1][0, 0]] + along_zero_1, crossed_1, some, sums, experts
    )
    return (
        output[None],
        tokens_back[None],
        gains[0],
        attention_sum[:, :query_cols],
        attention_sum[:, query_cols : query_cols + key_cols],
        attention_sum[:, query_cols + key_cols : query_cols + 2 * key_cols],
        attention_sum[:, query_cols + 2 * key_cols :].T,
        gains[1],
        gate_sum,
        up_sum,
        jnp.swapaxes(down_sum, 1, 2),
        logit_back.T[None],
    )


def solution(mesh):
    groups, others = mesh.shape["gx"], mesh.shape["gy"]
    split = Mesh(mesh.devices.reshape(groups, others // 4, 2, 2), ("gx", "gt", "gw", "co"))
    gy = ("gt", "gw", "co")
    in_specs = (
        P(gy, "gx", None),
        P(),
        P(gy, "gx"),
        P(gy, "gx"),
        P(gy, "gx"),
        P("gx", gy),
        P(),
        P("gx", gy, None),
        P("gx", gy, None),
        P("gx", None, gy),
        P(gy, "gx", None),
        P(gy, "gx", None),
        P(gy, "gx", None),
    )
    out_specs = (
        P(gy, "gx", None),
        P(gy, "gx", None),
        P(),
        P(gy, "gx"),
        P(gy, "gx"),
        P(gy, "gx"),
        P("gx", gy),
        P(),
        P("gx", gy, None),
        P("gx", gy, None),
        P("gx", None, gy),
        P(gy, "gx", None),
    )
    return jax.shard_map(local, mesh=split, in_specs=in_specs, out_specs=out_specs, check_vma=False)
```

time: 735 us -> 607 us (0.83)
  blocking collectives: 122 us -> 0 us
  starting transfers between devices: 45.9 us -> 72 us
  Pallas kernels: 87.2 us -> 108 us
  local copies, waits for them, and re-layouts: 58.6 us -> 40.1 us
  other arithmetic: 68.2 us -> 50.3 us
  waiting for transfers between devices: 303 us -> 286 us
    unnamed x1 -> x0, blocking collectives: 89.5 us -> none
    all_gather x1 -> x0, blocking collectives: 32.2 us -> none  [gather_early(): whole = lax.all_gather(after(block, last_token), ('gx', 'gw'), axis=0)]
    ppermute x62 -> x73, starting transfers between devices: 45.8 us -> 71.9 us  [swap(): return lax.ppermute(value, axis, [(i, i ^ step) for i in range(count)])]
    ppermute x62 -> x73, waiting for transfers between devices: 303 us -> 286 us  [swap(): return lax.ppermute(value, axis, [(i, i ^ step) for i in range(count)])]
    pallas_call x5 -> x7, Pallas kernels: 30.7 us -> 46.9 us  [the longest x2 16.4 us: sum_slots(): pl.pallas_call(kernel, grid_spec=pltpu.PrefetchScalarGridSpec(num_scalar_...]
    unnamed x216 -> x212, local copies, waits for them, and re-layouts: 36.2 us -> 21.9 us
    pallas_call x1 -> x2, Pallas kernels: 46.9 us -> 50.5 us  [run_experts(): pl.pallas_call(kernel, grid_spec=pltpu.PrefetchScalarGridSpec(num_scalar_...]
    convert_element_type x6 -> x10, other arithmetic: 17.9 us -> 20.5 us  [the longest x2 6.42 us: near(): return total.astype(bf16)]
  transfers between devices with their start and end apart: 64 -> 75, of which waited for: 24 -> 29; matrix products, arithmetic and copies ran while one was open for 16% -> 15% of each run, Pallas kernels for 3% -> 18%
where the time goes in v3:
time: 607 us; the launch traced here: 596 us
  waiting for transfers between devices  286 us (47%)
  Pallas kernels  108 us (18%)
  starting transfers between devices  72 us (12%)
  other arithmetic  50.3 us (8%)
  local copies, waits for them, and re-layouts  40.1 us (7%)
  matrix products  23.3 us (4%)
  between operations  16 us (3%)
    ppermute x73, waiting for transfers between devices, swap(): return lax.ppermute(value, axis, [(i, i ^ step) for i in range(count)])  286 us
    ppermute x73, starting transfers between devices, swap(): return lax.ppermute(value, axis, [(i, i ^ step) for i in range(count)])  71.9 us
    pallas_call x2, Pallas kernels, run_experts(): pl.pallas_call(kernel, grid_spec=pltpu.PrefetchScalarGridSpec(num_scalar_...  50.5 us
    unnamed x212, local copies, waits for them, and re-layouts  21.9 us
    pallas_call x2, Pallas kernels, sum_slots(): pl.pallas_call(kernel, grid_spec=pltpu.PrefetchScalarGridSpec(num_scalar_...  16.4 us
    pallas_call x2, Pallas kernels, gather_slots(): pl.pallas_call(kernel_list if listed else kernel_array, grid_spec=pltpu.P...  15.5 us
    pallas_call x2, Pallas kernels, finish_gradients(): pl.pallas_call(kernel, grid_spec=pltpu.PrefetchScalarGridSpec(num_scalar_...  14.8 us
  transfers between devices with their start and end apart: 75, of which 29 were waited for; matrix products, arithmetic and copies ran while one was open for 15% of the time, Pallas kernels for 18%

profile of v3, /device:TPU:0, one launch (start us, length us, event | category | flops | bytes accessed | tf_op | source)
XLA Modules:
  0.0 595.7 jit_solution(3377470945369030244)
XLA Ops:
  27.0 22.1 %collective-permute-done.1 = bf16[128,1536]{1,0:T(8,128)(2,1)S(1)} collective-permute-done((bf16[128,1536]{1,0:T(8,128)(2,1)}, bf16[128,1536]{1,0:T(8,128)(2,1)S(1)}, u32[]{:S(2)}, u32[]{:S(2)}) %collective-permute-start.1) | collective-permute-done | bytes 393248 | tf_op jit(solution)/shard_map/ppermute | solution.py:27
  95.5 19.7 %collective-permute-done.10.refs_1_ = bf16[5,192,768]{2,1,0:T(8,128)(2,1)} collective-permute-done((bf16[5,192,768]{2,1,0:T(8,128)(2,1)}, bf16[5,192,768]{2,1,0:T(8,128)(2,1)}, u32[]{:S(2)}, u32[]{:S(2)}) %collective-permute-start.10) | collective-permute-done | bytes 1474592 | tf_op jit(solution)/shard_map/ppermute | solution.py:27
  120.5 16.5 %collective-permute-done.15 = bf16[128,1536]{1,0:T(8,128)(2,1)S(1)} collective-permute-done((bf16[128,1536]{1,0:T(8,128)(2,1)S(1)}, bf16[128,1536]{1,0:T(8,128)(2,1)S(1)}, u32[]{:S(2)}, u32[]{:S(2)}) %collective-permute-start.15) | collective-permute-done | bytes 393248 | tf_op jit(solution)/shard_map/ppermute | solution.py:27
  137.0 10.6 %collective-permute-done.14 = bf16[128,1536]{1,0:T(8,128)(2,1)S(1)} collective-permute-done((bf16[128,1536]{1,0:T(8,128)(2,1)S(1)}, bf16[128,1536]{1,0:T(8,128)(2,1)S(1)}, u32[]{:S(2)}, u32[]{:S(2)}) %collective-permute-start.14) | collective-permute-done | bytes 393248 | tf_op jit(solution)/shard_map/ppermute | solution.py:27
  148.1 9.2 %collective-permute-done.16 = bf16[128,1536]{1,0:T(8,128)(2,1)S(1)} collective-permute-done((bf16[128,1536]{1,0:T(8,128)(2,1)S(1)}, bf16[128,1536]{1,0:T(8,128)(2,1)S(1)}, u32[]{:S(2)}, u32[]{:S(2)}) %collective-permute-start.16) | collective-permute-done | bytes 393248 | tf_op jit(solution)/shard_map/ppermute | solution.py:27
  163.9 7.9 %gather_slots.2.back_ref = bf16[10,8,48,1536]{3,2,1,0:T(8,128)(2,1)} custom-call(s32[8]{0:T(128)S(1)} %stack.56.order_ref, f32[8,10,128]{2,1,0:T(8,128)S(1)} %convolution_select_fusion.slots_ref, bf16[8,128,1664]{2,1,0:T(8,128)(2,1)S(1)} %bitcast.234), custom_call_target="tpu_custom_call" | custom-call | flops 1509949440 | bytes 14942208 | tf_op jit(solution)/shard_map/gather_slots/pallas_call | solution.py:251
  177.8 9.6 %collective-permute-done.23.refs_3_ = bf16[128,1536]{1,0:T(8,128)(2,1)S(1)} collective-permute-done((bf16[128,1536]{1,0:T(8,128)(2,1)S(1)}, bf16[128,1536]{1,0:T(8,128)(2,1)S(1)}, u32[]{:S(2)}, u32[]{:S(2)}) %collective-permute-start.23) | collective-permute-done | bytes 393248 | tf_op jit(solution)/shard_map/ppermute | solution.py:27
  187.3 19.7 %collective-permute-done.22.refs_2_ = bf16[128,1536]{1,0:T(8,128)(2,1)S(1)} collective-permute-done((bf16[128,1536]{1,0:T(8,128)(2,1)S(1)}, bf16[128,1536]{1,0:T(8,128)(2,1)S(1)}, u32[]{:S(2)}, u32[]{:S(2)}) %collective-permute-start.22) | collective-permute-done | bytes 393248 | tf_op jit(solution)/shard_map/ppermute | solution.py:27
  210.2 9.3 %collective-permute-done.25.refs_4_ = bf16[128,1536]{1,0:T(8,128)(2,1)S(1)} collective-permute-done((bf16[128,1536]{1,0:T(8,128)(2,1)S(1)}, bf16[128,1536]{1,0:T(8,128)(2,1)S(1)}, u32[]{:S(2)}, u32[]{:S(2)}) %collective-permute-start.25) | collective-permute-done | bytes 393248 | tf_op jit(solution)/shard_map/ppermute | solution.py:27
  220.1 7.8 %collective-permute-done.28.refs_7_ = bf16[128,1536]{1,0:T(8,128)(2,1)S(1)} collective-permute-done((bf16[128,1536]{1,0:T(8,128)(2,1)S(1)}, bf16[128,1536]{1,0:T(8,128)(2,1)S(1)}, u32[]{:S(2)}, u32[]{:S(2)}) %collective-permute-start.28) | collective-permute-done | bytes 393248 | tf_op jit(solution)/shard_map/ppermute | solution.py:27
  227.9 8.4 %collective-permute-done.27.refs_6_ = bf16[128,1536]{1,0:T(8,128)(2,1)S(1)} collective-permute-done((bf16[128,1536]{1,0:T(8,128)(2,1)S(1)}, bf16[128,1536]{1,0:T(8,128)(2,1)S(1)}, u32[]{:S(2)}, u32[]{:S(2)}) %collective-permute-start.27) | collective-permute-done | bytes 393248 | tf_op jit(solution)/shard_map/ppermute | solution.py:27
  244.4 7.6 %gather_slots.3.rows_ref = bf16[10,8,48,1536]{3,2,1,0:T(8,128)(2,1)} custom-call(s32[1]{0:T(128)} %constant.104.clone.1.order_ref, f32[8,10,128]{2,1,0:T(8,128)S(1)} %convolution_select_fusion.slots_ref, bf16[128,1536]{1,0:T(8,128)(2,1)S(1)} %multiply_convert_fusion.1.refs_0_, bf16[128,1536]{1,0:T(8,128)(2,1)S(1)} %collective-permute-done.21.refs_1_, ...), custom_call_target="tpu_custom_call" | custom-call | flops 1509949440 | bytes 14942208 | tf_op jit(solution)/shard_map/gather_slots/pallas_call | solution.py:251
  253.2 25.2 %run_experts.2 = (bf16[5,8,48,1536]{3,2,1,0:T(8,128)(2,1)}, bf16[5,8,48,1536]{3,2,1,0:T(8,128)(2,1)}, f32[5,8,128]{2,1,0:T(8,128)}, bf16[5,192,768]{2,1,0:T(8,12...) custom-call(s32[1]{0:T(128)} %bitcast.7.me_ref, ...), custom_call_target="tpu_custom_call" | custom-call | flops 13589544960 | bytes 47185920 | tf_op jit(solution)/shard_map/run_experts/pallas_call | solution.py:364
  279.5 25.3 %run_experts.3 = (bf16[5,8,48,1536]{3,2,1,0:T(8,128)(2,1)}, bf16[5,8,48,1536]{3,2,1,0:T(8,128)(2,1)}, f32[5,8,128]{2,1,0:T(8,128)}, bf16[5,192,768]{2,1,0:T(8,12...) custom-call(s32[1]{0:T(128)} %bitcast.7.me_ref, ...), custom_call_target="tpu_custom_call" | custom-call | flops 13589544960 | bytes 47185920 | tf_op jit(solution)/shard_map/run_experts/pallas_call | solution.py:364
  309.9 7.5 %sum_slots.2 = bf16[8,128,1536]{2,1,0:T(8,128)(2,1)S(1)} custom-call(s32[8]{0:T(128)S(1)} %iota.44.order_ref, f32[8,10,128]{2,1,0:T(8,128)S(1)} %convolution_select_fusion.slots_ref, bf16[5,8,48,1536]{3,2,1,0:T(8,128)(2,1)S(1)} %copy-done.1, bf16[5,8,48,1536]{3,2,1,0:T(8,128)(2,1)} %get-tuple-element.164.refs_1_), custom_call_target="tpu_custom_call" | custom-call | flops 1509949440 | bytes 14942208 | tf_op jit(solution)/shard_map/sum_slots/pallas_call | solution.py:287
  330.5 8.9 %sum_slots.3 = bf16[8,128,1536]{2,1,0:T(8,128)(2,1)} custom-call(s32[8]{0:T(128)S(1)} %stack.56.order_ref, f32[8,10,128]{2,1,0:T(8,128)S(1)} %convolution_select_fusion.slots_ref, bf16[5,8,48,1536]{3,2,1,0:T(8,128)(2,1)S(1)} %copy-done, bf16[5,8,48,1536]{3,2,1,0:T(8,128)(2,1)} %get-tuple-element.171.refs_1_), custom_call_target="tpu_custom_call" | custom-call | flops 1509949440 | bytes 14942208 | tf_op jit(solution)/shard_map/sum_slots/pallas_call | solution.py:287
  339.4 15.9 %collective-permute-done.38 = bf16[128,1536]{1,0:T(8,128)(2,1)} collective-permute-done((bf16[128,1536]{1,0:T(8,128)(2,1)}, bf16[128,1536]{1,0:T(8,128)(2,1)}, u32[]{:S(2)}, u32[]{:S(2)}) %collective-permute-start.38) | collective-permute-done | bytes 393248 | tf_op jit(solution)/shard_map/ppermute | solution.py:27
  370.3 9.2 %collective-permute-done.45 = bf16[128,1536]{1,0:T(8,128)(2,1)S(1)} collective-permute-done((bf16[128,1536]{1,0:T(8,128)(2,1)S(1)}, bf16[128,1536]{1,0:T(8,128)(2,1)S(1)}, u32[]{:S(2)}, u32[]{:S(2)}) %collective-permute-start.45) | collective-permute-done | bytes 393248 | tf_op jit(solution)/shard_map/ppermute | solution.py:27
  379.5 16.6 %collective-permute-done.43 = bf16[128,1536]{1,0:T(8,128)(2,1)S(1)} collective-permute-done((bf16[128,1536]{1,0:T(8,128)(2,1)S(1)}, bf16[128,1536]{1,0:T(8,128)(2,1)S(1)}, u32[]{:S(2)}, u32[]{:S(2)}) %collective-permute-start.43) | collective-permute-done | bytes 393248 | tf_op jit(solution)/shard_map/ppermute | solution.py:27
  419.2 45.3 %collective-permute-done.50 = bf16[128,1536]{1,0:T(8,128)(2,1)} collective-permute-done((bf16[128,1536]{1,0:T(8,128)(2,1)}, bf16[128,1536]{1,0:T(8,128)(2,1)}, u32[]{:S(2)}, u32[]{:S(2)}) %collective-permute-start.50) | collective-permute-done | bytes 393248 | tf_op jit(solution)/shard_map/ppermute | solution.py:27
  505.3 9.9 %collective-permute-done.67.refs_2_ = bf16[5,192,768]{2,1,0:T(8,128)(2,1)} collective-permute-done((bf16[5,192,768]{2,1,0:T(8,128)(2,1)}, bf16[5,192,768]{2,1,0:T(8,128)(2,1)}, u32[]{:S(2)}, u32[]{:S(2)}) %collective-permute-start.67) | collective-permute-done | bytes 1474592 | tf_op jit(solution)/shard_map/ppermute | solution.py:27
  520.7 7.4 %finish_gradients.2 = (f32[10,192,512]{2,1,0:T(8,128)}, f32[10,192,512]{2,1,0:T(8,128)}, f32[10,192,512]{2,1,0:T(8,128)}) custom-call(s32[1]{0:T(128)} %bitcast.9.side_ref, bf16[5,192,768]{2,1,0:T(8,128)(2,1)} %get-tuple-element.212.refs_0_, bf16[5,192,768]{2,1,0:T(8,128)(2,1)} %copy-done.34, bf16[5,192,768]{2,1,0:T(8,128)(2,1)} %collective-permute-done.67.refs_2_, ...), custom_call_target="tpu_custom_call" | custom-call | tf_op jit(solution)/shard_map/finish_gradients/pallas_call | solution.py:177
  533.3 16.8 %collective-permute-done.57 = bf16[128,1536]{1,0:T(8,128)(2,1)} collective-permute-done((bf16[128,1536]{1,0:T(8,128)(2,1)}, bf16[128,1536]{1,0:T(8,128)(2,1)}, u32[]{:S(2)}, u32[]{:S(2)}) %collective-permute-start.57) | collective-permute-done | bytes 393248 | tf_op jit(solution)/shard_map/ppermute | solution.py:27
  577.8 7.4 %finish_gradients.3 = (f32[10,192,512]{2,1,0:T(8,128)}, f32[10,192,512]{2,1,0:T(8,128)}, f32[10,192,512]{2,1,0:T(8,128)}) custom-call(s32[1]{0:T(128)} %bitcast.9.side_ref, bf16[5,192,768]{2,1,0:T(8,128)(2,1)} %get-tuple-element.204.refs_0_, ...), custom_call_target="tpu_custom_call", output_to_operand_aliasing={{0}: (5, {}), {1}: (6, {}), {2}: (7, {})} | custom-call | tf_op jit(solution)/shard_map/finish_gradients/pallas_call | solution.py:177
  (462 shorter events, 235.9 us)
Async XLA Ops:
  7.2 152.6 %all-gather.3.cloned.1.call-start = ((), (), s32[]{:S(2)}) async-start(), calls=%async_computation.2 | async-start | bytes 3833856 | tf_op jit(solution)/shard_map/all_gather | solution.py:487
  8.3 62.0 %collective-permute-start.6 = (bf16[192,1024]{1,0:T(8,128)(2,1)S(1)}, bf16[192,1024]{1,0:T(8,128)(2,1)S(1)}, u32[]{:S(2)}, u32[]{:S(2)}) collective-permute-start(bf16[192,1024]{1,0:T(8,128)(2,1)S(1)} %pad_maximum_fusion.2.refs_0_), channel_id=1, source_target_pairs={{0,1},{1,0},{2,3},{3,2},{4,5},{5,4},{6,7},{7,6},{8,9},{9,8},{10,11... | collective-permute-start | bytes 1179656 | tf_op jit(solution)/shard_map/ppermute | solution.py:27
  8.8 50.6 %collective-permute-start.3 = (bf16[192,1024]{1,0:T(8,128)(2,1)S(1)}, bf16[192,1024]{1,0:T(8,128)(2,1)S(1)}, u32[]{:S(2)}, u32[]{:S(2)}) collective-permute-start(bf16[192,1024]{1,0:T(8,128)(2,1)S(1)} %pad_maximum_fusion.2.refs_0_), channel_id=1, source_target_pairs={{0,2},{2,0},{1,3},{3,1},{4,6},{6,4},{5,7},{7,5},{8,10},{10,8},{9,1... | collective-permute-start | bytes 1179656 | tf_op jit(solution)/shard_map/ppermute | solution.py:27
  25.5 37.9 %collective-permute-start.4 = (bf16[192,1024]{1,0:T(8,128)(2,1)S(1)}, bf16[192,1024]{1,0:T(8,128)(2,1)S(1)}, u32[]{:S(2)}, u32[]{:S(2)}) collective-permute-start(bf16[192,1024]{1,0:T(8,128)(2,1)S(1)} %pad_maximum_fusion.2.refs_0_), channel_id=1, source_target_pairs={{0,4},{4,0},{1,5},{5,1},{2,6},{6,2},{3,7},{7,3},{8,12},{12,8},{9,1... | collective-permute-start | bytes 1179656 | tf_op jit(solution)/shard_map/ppermute | solution.py:27
  49.1 536.1 %reduce-scatter.2.cloned.1.call-start = ((), (), s32[]{:S(2)}) async-start(), calls=%async_computation.1 | async-start | bytes 3538944 | tf_op jit(solution)/shard_map/reduce_scatter | solution.py:598
  63.0 52.2 %collective-permute-start.10 = (bf16[5,192,768]{2,1,0:T(8,128)(2,1)}, bf16[5,192,768]{2,1,0:T(8,128)(2,1)}, u32[]{:S(2)}, u32[]{:S(2)}) collective-permute-start(bf16[5,192,768]{2,1,0:T(8,128)(2,1)} %get-tuple-element.127), channel_id=1, source_target_pairs={{0,2},{2,0},{1,3},{3,1},{4,6},{6,4},{5,7},{7,5},{8,10},{10,8},{9,1... | collective-permute-start | bytes 4423688 | tf_op jit(solution)/shard_map/ppermute | solution.py:27
  71.0 44.2 %collective-permute-start.12 = (bf16[5,192,768]{2,1,0:T(8,128)(2,1)}, bf16[5,192,768]{2,1,0:T(8,128)(2,1)}, u32[]{:S(2)}, u32[]{:S(2)}) collective-permute-start(bf16[5,192,768]{2,1,0:T(8,128)(2,1)} %get-tuple-element.128.refs_0_), channel_id=1, source_target_pairs={{0,1},{1,0},{2,3},{3,2},{4,5},{5,4},{6,7},{7,6},{8,9},{9,8},{10,11... | collective-permute-start | bytes 4423688 | tf_op jit(solution)/shard_map/ppermute | solution.py:27
  71.5 43.7 %collective-permute-start.11 = (bf16[5,192,768]{2,1,0:T(8,128)(2,1)}, bf16[5,192,768]{2,1,0:T(8,128)(2,1)}, u32[]{:S(2)}, u32[]{:S(2)}) collective-permute-start(bf16[5,192,768]{2,1,0:T(8,128)(2,1)} %get-tuple-element.128.refs_0_), channel_id=1, source_target_pairs={{0,4},{4,0},{1,5},{5,1},{2,6},{6,2},{3,7},{7,3},{8,12},{12,8},{9,1... | collective-permute-start | bytes 4423688 | tf_op jit(solution)/shard_map/ppermute | solution.py:27
  73.0 42.2 %collective-permute-start.13 = (bf16[5,192,768]{2,1,0:T(8,128)(2,1)}, bf16[5,192,768]{2,1,0:T(8,128)(2,1)}, u32[]{:S(2)}, u32[]{:S(2)}) collective-permute-start(bf16[5,192,768]{2,1,0:T(8,128)(2,1)} %get-tuple-element.139.refs_0_), channel_id=1, source_target_pairs={{0,1},{1,0},{2,3},{3,2},{4,5},{5,4},{6,7},{7,6},{8,9},{9,8},{10,11... | collective-permute-start | bytes 4423688 | tf_op jit(solution)/shard_map/ppermute | solution.py:27
  116.8 40.5 %collective-permute-start.16 = (bf16[128,1536]{1,0:T(8,128)(2,1)S(1)}, bf16[128,1536]{1,0:T(8,128)(2,1)S(1)}, u32[]{:S(2)}, u32[]{:S(2)}) collective-permute-start(bf16[128,1536]{1,0:T(8,128)(2,1)S(1)} %get-tuple-element.271), channel_id=1, source_target_pairs={{0,16},{8,24},{16,0},{24,8},{1,17},{9,25},{17,1},{25,9},{2,18},{10... | collective-permute-start | bytes 1179656 | tf_op jit(solution)/shard_map/ppermute | solution.py:27
  119.9 51.9 %collective-permute-start.17 = (bf16[5,192,768]{2,1,0:T(8,128)(2,1)}, bf16[5,192,768]{2,1,0:T(8,128)(2,1)}, u32[]{:S(2)}, u32[]{:S(2)}) collective-permute-start(bf16[5,192,768]{2,1,0:T(8,128)(2,1)} %get-tuple-element.138), channel_id=1, source_target_pairs={{0,2},{2,0},{1,3},{3,1},{4,6},{6,4},{5,7},{7,5},{8,10},{10,8},{9,1... | collective-permute-start | bytes 4423688 | tf_op jit(solution)/shard_map/ppermute | solution.py:27
  120.5 51.3 %collective-permute-start.18 = (bf16[5,192,768]{2,1,0:T(8,128)(2,1)}, bf16[5,192,768]{2,1,0:T(8,128)(2,1)}, u32[]{:S(2)}, u32[]{:S(2)}) collective-permute-start(bf16[5,192,768]{2,1,0:T(8,128)(2,1)} %get-tuple-element.139.refs_0_), channel_id=1, source_target_pairs={{0,4},{4,0},{1,5},{5,1},{2,6},{6,2},{3,7},{7,3},{8,12},{12,8},{9,1... | collective-permute-start | bytes 4423688 | tf_op jit(solution)/shard_map/ppermute | solution.py:27
  207.6 44.4 %collective-permute-start.29 = (bf16[5,192,768]{2,1,0:T(8,128)(2,1)S(1)}, bf16[5,192,768]{2,1,0:T(8,128)(2,1)S(1)}, u32[]{:S(2)}, u32[]{:S(2)}) collective-permute-start(bf16[5,192,768]{2,1,0:T(8,128)(2,1)S(1)} %collective-permute-done.24.refs_3_), channel_id=1, source_target_pairs={{0,1},{1,0},{2,3},{3,2},{4,5},{5,4},{6,7},{7,6},{8,9},{9,8},{10,11... | collective-permute-start | bytes 4423688 | tf_op jit(solution)/shard_map/ppermute | solution.py:27
  227.9 51.0 %collective-permute-start.36 = (bf16[5,192,768]{2,1,0:T(8,128)(2,1)}, bf16[5,192,768]{2,1,0:T(8,128)(2,1)}, u32[]{:S(2)}, u32[]{:S(2)}) collective-permute-start(bf16[5,192,768]{2,1,0:T(8,128)(2,1)} %collective-permute-done.18.refs_2_), channel_id=1, source_target_pairs={{0,1},{1,0},{2,3},{3,2},{4,5},{5,4},{6,7},{7,6},{8,9},{9,8},{10,11... | collective-permute-start | bytes 4423688 | tf_op jit(solution)/shard_map/ppermute | solution.py:27
  236.4 42.7 %collective-permute-start.35 = (bf16[5,192,768]{2,1,0:T(8,128)(2,1)}, bf16[5,192,768]{2,1,0:T(8,128)(2,1)}, u32[]{:S(2)}, u32[]{:S(2)}) collective-permute-start(bf16[5,192,768]{2,1,0:T(8,128)(2,1)} %collective-permute-done.17.refs_1_), channel_id=1, source_target_pairs={{0,1},{1,0},{2,3},{3,2},{4,5},{5,4},{6,7},{7,6},{8,9},{9,8},{10,11... | collective-permute-start | bytes 4423688 | tf_op jit(solution)/shard_map/ppermute | solution.py:27
  240.0 39.5 %collective-permute-start.37 = (bf16[5,192,768]{2,1,0:T(8,128)(2,1)}, bf16[5,192,768]{2,1,0:T(8,128)(2,1)}, u32[]{:S(2)}, u32[]{:S(2)}) collective-permute-start(bf16[5,192,768]{2,1,0:T(8,128)(2,1)} %collective-permute-done.34.refs_3_), channel_id=1, source_target_pairs={{0,1},{1,0},{2,3},{3,2},{4,5},{5,4},{6,7},{7,6},{8,9},{9,8},{10,11... | collective-permute-start | bytes 4423688 | tf_op jit(solution)/shard_map/ppermute | solution.py:27
  355.3 44.1 %collective-permute-start.47 = (bf16[5,192,768]{2,1,0:T(8,128)(2,1)}, bf16[5,192,768]{2,1,0:T(8,128)(2,1)S(1)}, u32[]{:S(2)}, u32[]{:S(2)}) collective-permute-start(bf16[5,192,768]{2,1,0:T(8,128)(2,1)} %get-tuple-element.179), channel_id=1, source_target_pairs={{0,1},{1,0},{2,3},{3,2},{4,5},{5,4},{6,7},{7,6},{8,9},{9,8},{10,11... | collective-permute-start | bytes 4423688 | tf_op jit(solution)/shard_map/ppermute | solution.py:27
  355.3 44.1 %collective-permute-start.46 = (bf16[5,192,768]{2,1,0:T(8,128)(2,1)}, bf16[5,192,768]{2,1,0:T(8,128)(2,1)S(1)}, u32[]{:S(2)}, u32[]{:S(2)}) collective-permute-start(bf16[5,192,768]{2,1,0:T(8,128)(2,1)} %add_convert_fusion.5), channel_id=1, source_target_pairs={{0,4},{4,0},{1,5},{5,1},{2,6},{6,2},{3,7},{7,3},{8,12},{12,8},{9,1... | collective-permute-start | bytes 4423688 | tf_op jit(solution)/shard_map/ppermute | solution.py:27
  403.8 60.7 %collective-permute-start.53 = (bf16[5,192,768]{2,1,0:T(8,128)(2,1)}, bf16[5,192,768]{2,1,0:T(8,128)(2,1)}, u32[]{:S(2)}, u32[]{:S(2)}) collective-permute-start(bf16[5,192,768]{2,1,0:T(8,128)(2,1)} %add_convert_fusion.3), channel_id=1, source_target_pairs={{0,2},{2,0},{1,3},{3,1},{4,6},{6,4},{5,7},{7,5},{8,10},{10,8},{9,1... | collective-permute-start | bytes 4423688 | tf_op jit(solution)/shard_map/ppermute | solution.py:27
  404.4 60.1 %collective-permute-start.52 = (bf16[5,192,768]{2,1,0:T(8,128)(2,1)}, bf16[5,192,768]{2,1,0:T(8,128)(2,1)}, u32[]{:S(2)}, u32[]{:S(2)}) collective-permute-start(bf16[5,192,768]{2,1,0:T(8,128)(2,1)} %add_convert_fusion.4), channel_id=1, source_target_pairs={{0,4},{4,0},{1,5},{5,1},{2,6},{6,2},{3,7},{7,3},{8,12},{12,8},{9,1... | collective-permute-start | bytes 4423688 | tf_op jit(solution)/shard_map/ppermute | solution.py:27
  407.4 57.0 %collective-permute-start.50 = (bf16[128,1536]{1,0:T(8,128)(2,1)}, bf16[128,1536]{1,0:T(8,128)(2,1)}, u32[]{:S(2)}, u32[]{:S(2)}) collective-permute-start(bf16[128,1536]{1,0:T(8,128)(2,1)} %multiply_convert_fusion), channel_id=1, source_target_pairs={{0,16},{8,24},{16,0},{24,8},{1,17},{9,25},{17,1},{25,9},{2,18},{10... | collective-permute-start | bytes 1179656 | tf_op jit(solution)/shard_map/ppermute | solution.py:27
  407.4 57.0 %collective-permute-start.49 = (bf16[128,1536]{1,0:T(8,128)(2,1)}, bf16[128,1536]{1,0:T(8,128)(2,1)}, u32[]{:S(2)}, u32[]{:S(2)}) collective-permute-start(bf16[128,1536]{1,0:T(8,128)(2,1)} %multiply_convert_fusion), channel_id=1, source_target_pairs={{0,8},{8,0},{16,24},{24,16},{1,9},{9,1},{17,25},{25,17},{2,10},{10... | collective-permute-start | bytes 1179656 | tf_op jit(solution)/shard_map/ppermute | solution.py:27
  485.6 91.0 %collective-permute-start.69 = (bf16[5,192,768]{2,1,0:T(8,128)(2,1)}, bf16[5,192,768]{2,1,0:T(8,128)(2,1)}, u32[]{:S(2)}, u32[]{:S(2)}) collective-permute-start(bf16[5,192,768]{2,1,0:T(8,128)(2,1)} %add_convert_fusion), channel_id=1, source_target_pairs={{0,2},{2,0},{1,3},{3,1},{4,6},{6,4},{5,7},{7,5},{8,10},{10,8},{9,1... | collective-permute-start | bytes 4423688 | tf_op jit(solution)/shard_map/ppermute | solution.py:27
  528.1 48.5 %collective-permute-start.68 = (bf16[5,192,768]{2,1,0:T(8,128)(2,1)}, bf16[5,192,768]{2,1,0:T(8,128)(2,1)S(1)}, u32[]{:S(2)}, u32[]{:S(2)}) collective-permute-start(bf16[5,192,768]{2,1,0:T(8,128)(2,1)} %add_convert_fusion.1), channel_id=1, source_target_pairs={{0,4},{4,0},{1,5},{5,1},{2,6},{6,2},{3,7},{7,3},{8,12},{12,8},{9,1... | collective-permute-start | bytes 4423688 | tf_op jit(solution)/shard_map/ppermute | solution.py:27
  (153 other events, 2310.9 us)
Sparse Core Ops, SparseCore 0:
  49.2 90.7 all-gather.2
  411.0 94.9 reduce-scatter.1

commit v4 on v3

v4 whole, which is shorter than its diff:
```python
import functools

import jax
import jax.numpy as jnp
from jax import lax
from jax.experimental import pallas as pl
from jax.experimental.pallas import tpu as pltpu
from jax.sharding import Mesh, PartitionSpec as P

HEAD_SIZE = 64
EXPERTS = 40
TOPK = 8
CAP = 48

epsilon = 1e-06
rope_base = 10000.0
residual_factor = 0.22
score_factor = 0.015625
masked_value = -1e30

SMALL_COST = pl.CostEstimate(flops=1, bytes_accessed=1, transcendentals=0)
LARGE_COST = pl.CostEstimate(flops=10**10, bytes_accessed=10**8, transcendentals=0)

f32 = jnp.float32
bf16 = jnp.bfloat16


def swap(value, axis, step):
    count = lax.axis_size(axis)
    return lax.ppermute(value, axis, [(i, i ^ step) for i in range(count)])


def tie(*values):
    return lax.optimization_barrier(values)


def pick(array, index, dim):
    return lax.dynamic_index_in_dim(array, index, dim, keepdims=False)


def rms_factor(rows):
    return lax.rsqrt(jnp.mean(rows * rows, axis=-1, keepdims=True) + epsilon)


def norm_back(rows, factor, gain, upstream):
    scaled = upstream * gain
    inner = jnp.mean(scaled * rows, axis=-1, keepdims=True)
    return factor * scaled - rows * factor * factor * factor * inner


def contract_rows(left, right):
    return lax.dot_general(left, right, (((0,), (0,)), ((), ())), preferred_element_type=f32)


def contract_cols(left, right):
    return lax.dot_general(left, right, (((1,), (1,)), ((), ())), preferred_element_type=f32)


def gather_gx(block):
    return [block] + [swap(block, "gx", s) for s in range(1, lax.axis_size("gx"))]


def over_y(value):
    return [swap(value, "gt", s) for s in range(1, lax.axis_size("gt"))]


def spread_y(values):
    return [swap(value, "gt", s) for s, value in enumerate(values, 1)]


def part_places():
    many = lax.axis_size("gt")
    places = [0, 2] + [4 * s for s in range(1, many)] + [4 * s + 2 for s in range(1, many)]
    return places + [p + 1 for p in places]


def own_place():
    me = (lax.axis_index("gt") * 2 + lax.axis_index("gw")) * 2 + lax.axis_index("co")
    return jnp.full((1,), me, jnp.int32)


def own_side():
    return jnp.full((1,), lax.axis_index("gw"), jnp.int32)


def halve_weights(gate, up, down):
    experts, rows, full = gate.shape
    half = full // 2

    def kernel(side_ref, gate_ref, up_ref, down_ref, keep, give):
        def put(low, out):
            for i, ref in enumerate((gate_ref, up_ref, down_ref)):
                out[0, :, i * half : (i + 1) * half] = ref[0, :, low : low + half]

        @pl.when(side_ref[0] == 0)
        def _():
            put(0, keep)
            put(half, give)

        @pl.when(side_ref[0] != 0)
        def _():
            put(half, keep)
            put(0, give)

    def block(columns):
        return pl.BlockSpec((1, rows, columns), lambda e, *_: (e, 0, 0))

    shape = jax.ShapeDtypeStruct((experts, rows, 3 * half), bf16)
    return pl.pallas_call(
        kernel,
        grid_spec=pltpu.PrefetchScalarGridSpec(
            num_scalar_prefetch=1,
            grid=(experts,),
            in_specs=[block(full)] * 3,
            out_specs=[block(3 * half)] * 2,
        ),
        out_shape=[shape, shape],
        cost_estimate=LARGE_COST,
        name="halve_weights",
    )(own_side(), gate, up, down)


def finish_gradients(summed, crossed, start, before, total_experts):
    experts, rows, columns = crossed.shape
    half = columns // 3
    count = len(summed)
    aliased = 0 if before is None else 3

    def kernel(side_ref, *refs):
        total = 0.0
        for ref in refs[:count]:
            total = total + (ref[0, 0] if len(ref.shape) == 4 else ref[0]).astype(f32)
        other = refs[count][0].astype(f32)

        def put(low, value):
            for i, out in enumerate(refs[count + 1 + aliased :]):
                out[0, :, low : low + half] = value[:, i * half : (i + 1) * half]

        @pl.when(side_ref[0] == 0)
        def _():
            put(0, total)
            put(half, other)

        @pl.when(side_ref[0] != 0)
        def _():
            put(half, total)
            put(0, other)

    def block(columns, first):
        return pl.BlockSpec((1, rows, columns), lambda e, *_: (e + first, 0, 0))

    shape = jax.ShapeDtypeStruct((total_experts, rows, 2 * half), f32)
    return pl.pallas_call(
        kernel,
        grid_spec=pltpu.PrefetchScalarGridSpec(
            num_scalar_prefetch=1,
            grid=(experts,),
            in_specs=[
                pl.BlockSpec((1, 1, rows, columns), lambda e, *_: (0, e, 0, 0)) if v.ndim == 4 else block(columns, 0)
                for v in summed
            ]
            + [block(columns, 0)]
            + [pl.BlockSpec(memory_space=pl.ANY)] * aliased,
            out_specs=[block(2 * half, start)] * 3,
        ),
        out_shape=[shape] * 3,
        input_output_aliases={count + 2 + i: i for i in range(aliased)},
        cost_estimate=SMALL_COST,
        name="finish_gradients",
    )(own_side(), *summed, crossed, *(before or ()))


def scatter_gy(keep, got):
    many = lax.axis_size("gt")
    send = (keep[1::2].astype(f32) + got[1::2].astype(f32)).astype(bf16)
    got_w = swap(send, "gw", 1)
    total = keep[0::2].astype(f32) + got[0::2].astype(f32) + got_w.astype(f32)
    own = total[0]
    for value in spread_y([total[t].astype(bf16) for t in range(1, many)]):
        own = own + value.astype(f32)
    return own


def sum_everywhere(value):
    value = value + swap(value, "co", 1)
    for axes in (("gt", "gw"), ("gx",)):
        count = lax.axis_size(axes)
        sent = [lax.ppermute(value, axes, [(i, i ^ s) for i in range(count)]) for s in range(1, count)]
        for got in sent:
            value = value + got
    return value


def slot_mask(slot_row):
    wanted = lax.broadcasted_iota(jnp.int32, (CAP, slot_row.shape[1]), 0).astype(f32)
    return slot_row == wanted


def route_slots(gathered, order, first_expert, experts, width):
    blocks, tokens = gathered.shape[:2]

    def kernel(order_ref, first_ref, routing_ref, routes_out, slots_out, chances_out, slots_by, chances_by):
        earlier = lax.broadcasted_iota(jnp.int32, (tokens, tokens), 0)
        earlier = (earlier < lax.broadcasted_iota(jnp.int32, (tokens, tokens), 1)).astype(f32).astype(bf16)
        for b in range(blocks):
            routing = routing_ref[order_ref[b]].astype(f32).T
            routes = routing[:TOPK]
            chance = routing[TOPK : 2 * TOPK] + routing[2 * TOPK : 3 * TOPK]
            routes_out[b] = routes
            hits, chosen = [], []
            for e in range(experts):
                same = routes == (first_ref[0] + e).astype(f32)
                hits.append(jnp.sum(jnp.where(same, 1.0, 0.0), axis=0, keepdims=True))
                chosen.append(jnp.sum(jnp.where(same, chance, 0.0), axis=0, keepdims=True))
            hits, chosen = jnp.concatenate(hits, axis=0), jnp.concatenate(chosen, axis=0)
            rank = jnp.dot(hits.astype(bf16), earlier, preferred_element_type=f32)
            slots = jnp.where(hits > 0.0, rank, -1.0)
            slots_out[b] = slots
            chances_out[b] = chosen
            for e in range(experts):
                slots_by[e, b : b + 1, :] = slots[e : e + 1]
                chances_by[e, b : b + 1, :] = chosen[e : e + 1]

    def whole(*shape):
        zeros = (0,) * len(shape)
        return pl.BlockSpec(shape, lambda i, *_: zeros)

    shapes = [(blocks, TOPK, tokens)] + [(blocks, experts, tokens)] * 2 + [(experts, blocks, tokens)] * 2
    return pl.pallas_call(
        kernel,
        grid_spec=pltpu.PrefetchScalarGridSpec(
            num_scalar_prefetch=2,
            grid=(1,),
            in_specs=[pl.BlockSpec((blocks, tokens, 128), lambda i, *_: (0, 0, width // 128))],
            out_specs=[whole(*shape) for shape in shapes],
        ),
        out_shape=[jax.ShapeDtypeStruct(shape, f32) for shape in shapes],
        cost_estimate=SMALL_COST,
        name="route_slots",
    )(order, jnp.full((1,), first_expert, jnp.int32), gathered)


def gather_slots(sources, order, slots):
    blocks, experts, tokens = slots.shape
    listed = isinstance(sources, list)
    width = sources[0].shape[1] if listed else order[1]

    def find(slots_ref, rows, out_ref):
        mask = jnp.concatenate([slot_mask(slots_ref[0, e : e + 1, :]) for e in range(experts)], axis=0)
        found = jnp.dot(mask.astype(f32).astype(bf16), rows, preferred_element_type=f32)
        out_ref[...] = found.astype(bf16).reshape(experts, 1, CAP, width)

    def kernel_list(order_ref, slots_ref, *refs):
        for i in range(blocks):

            @pl.when(pl.program_id(0) == i)
            def _(i=i):
                refs[blocks + 1][...] = refs[i][...]

        find(slots_ref, refs[blocks + 1][...], refs[blocks])

    def kernel_array(order_ref, slots_ref, rows_ref, out_ref):
        find(slots_ref, rows_ref[0], out_ref)

    if listed:
        specs = [pl.BlockSpec((tokens, width), lambda b, *_: (0, 0))] * blocks
        scratch = [pltpu.VMEM((tokens, width), bf16)]
        prefetch = jnp.zeros((1,), jnp.int32)
    else:
        specs = [pl.BlockSpec((1, tokens, width), lambda b, order_ref: (order_ref[b], 0, 0))]
        scratch = []
        prefetch = order[0]
        sources = [sources]
    return pl.pallas_call(
        kernel_list if listed else kernel_array,
        grid_spec=pltpu.PrefetchScalarGridSpec(
            num_scalar_prefetch=1,
            grid=(blocks,),
            in_specs=[pl.BlockSpec((1, experts, tokens), lambda b, *_: (b, 0, 0))] + specs,
            out_specs=pl.BlockSpec((experts, 1, CAP, width), lambda b, *_: (0, b, 0, 0)),
            scratch_shapes=scratch,
        ),
        out_shape=jax.ShapeDtypeStruct((experts, blocks, CAP, width), bf16),
        compiler_params=pltpu.CompilerParams(vmem_limit_bytes=40 * 2**20),
        cost_estimate=SMALL_COST,
        name="gather_slots",
    )(prefetch, slots, *sources)


def sum_slots(slot_rows, slots, order):
    blocks, experts, tokens = slots.shape
    width = slot_rows[0].shape[3]

    def kernel(order_ref, slots_ref, *refs):
        total, first = None, 0
        for ref in refs[:-1]:
            mine = ref.shape[0]
            mask = jnp.concatenate(
                [slot_mask(slots_ref[0, e : e + 1, :]) for e in range(first, first + mine)], axis=0
            )
            first = first + mine
            part = contract_rows(mask.astype(f32).astype(bf16), ref[...].reshape(mine * CAP, width))
            total = part if total is None else total + part
        refs[-1][0] = total.astype(bf16)

    return pl.pallas_call(
        kernel,
        grid_spec=pltpu.PrefetchScalarGridSpec(
            num_scalar_prefetch=1,
            grid=(blocks,),
            in_specs=[pl.BlockSpec((1, experts, tokens), lambda b, *_: (b, 0, 0))]
            + [pl.BlockSpec((r.shape[0], 1, CAP, width), lambda b, *_: (0, b, 0, 0)) for r in slot_rows],
            out_specs=pl.BlockSpec((1, tokens, width), lambda b, order_ref: (order_ref[b], 0, 0)),
        ),
        out_shape=jax.ShapeDtypeStruct((blocks, tokens, width), bf16),
        compiler_params=pltpu.CompilerParams(vmem_limit_bytes=40 * 2**20),
        cost_estimate=LARGE_COST,
        name="sum_slots",
    )(order, slots, *slot_rows)


def run_experts(rows_in, back_in, weights, start, experts, slots, chances):
    blocks, _, width = rows_in.shape[1:]
    places = part_places()
    tokens = slots.shape[2]
    cut, half = weights[0][0].shape[1], weights[0][0].shape[2] // 3
    count = len(places)
    total_slots = blocks * CAP

    def kernel(me_ref, rows_ref, back_ref, slots_ref, chances_ref, *refs):
        rows_out, mixed_out, chance_out = refs[count : count + 3]
        grads = refs[count + 3 : count + 5]
        gu_full, d_full, gu_total, d_total = refs[count + 5 :]
        spots = [pl.ds(pl.multiple_of((me_ref[0] ^ place) * cut, cut), cut) for place in places]
        for spot, part in zip(spots, refs[:count]):
            gu_full[spot, :] = part[0, :, : 2 * half]
            d_full[spot, :] = part[0, :, 2 * half :]
        rows = rows_ref[0].reshape(total_slots, width)
        back = back_ref[0].reshape(total_slots, width)
        masks = [slot_mask(slots_ref[0, b : b + 1, :]) for b in range(blocks)]
        chance = jnp.concatenate(
            [
                jnp.sum(jnp.where(masks[b], chances_ref[0, b : b + 1, :], 0.0), axis=1, keepdims=True)
                for b in range(blocks)
            ],
            axis=0,
        )
        both = jnp.dot(rows, gu_full[...], preferred_element_type=f32)
        active_back = jnp.dot(back, d_full[...], preferred_element_type=f32) * residual_factor
        gate, upper = both[:, :half], both[:, half:]
        sigma = jax.nn.sigmoid(gate)
        silu = gate * sigma
        active = silu * upper
        chance_back = jnp.sum(active * active_back, axis=1, keepdims=True)
        for b in range(blocks):
            column = chance_back[b * CAP : (b + 1) * CAP]
            chance_out[0, b : b + 1, :] = jnp.sum(jnp.where(masks[b], column, 0.0), axis=0, keepdims=True)
        scaled = (active * chance).astype(bf16)
        active_back = active_back * chance
        gate_back = active_back * upper * (sigma * (1.0 + gate * (1.0 - sigma)))
        upper_back = active_back * silu
        both_back = jnp.concatenate([gate_back.astype(bf16), upper_back.astype(bf16)], axis=1)
        rows_out[0] = contract_cols(both_back, gu_full[...]).astype(bf16).reshape(blocks, CAP, width)
        mixed_out[0] = contract_cols(scaled, d_full[...]).astype(bf16).reshape(blocks, CAP, width)
        gu_total[...] = contract_rows(rows, both_back).astype(bf16)
        d_total[...] = (contract_rows(back, scaled) * residual_factor).astype(bf16)
        for spot, place in zip(spots, places):
            grads[place % 2][place // 2, 0, :, : 2 * half] = gu_total[spot, :]
            grads[place % 2][place // 2, 0, :, 2 * half :] = d_total[spot, :]

    def block(shape, first=0):
        zeros = (0,) * len(shape)
        return pl.BlockSpec((1,) + shape, lambda e, *_: (e + first,) + zeros)

    grad_shape = jax.ShapeDtypeStruct((count // 2, experts, cut, 3 * half), bf16)
    slot_shape = jax.ShapeDtypeStruct((experts, blocks, CAP, width), bf16)
    out = pl.pallas_call(
        kernel,
        grid_spec=pltpu.PrefetchScalarGridSpec(
            num_scalar_prefetch=1,
            grid=(experts,),
            in_specs=[
                block((blocks, CAP, width), start),
                block((blocks, CAP, width), start),
                block((blocks, tokens), start),
                block((blocks, tokens), start),
            ]
            + [block((cut, 3 * half), first) for _, first in weights],
            out_specs=[block((blocks, CAP, width)), block((blocks, CAP, width)), block((blocks, tokens))]
            + [pl.BlockSpec((count // 2, 1, cut, 3 * half), lambda e, *_: (0, e, 0, 0))] * 2,
            scratch_shapes=[
                pltpu.VMEM((width, 2 * half), bf16),
                pltpu.VMEM((width, half), bf16),
                pltpu.VMEM((width, 2 * half), bf16),
                pltpu.VMEM((width, half), bf16),
            ],
        ),
        out_shape=[slot_shape, slot_shape, jax.ShapeDtypeStruct((experts, blocks, tokens), f32)]
        + [grad_shape] * 2,
        compiler_params=pltpu.CompilerParams(vmem_limit_bytes=60 * 2**20),
        cost_estimate=LARGE_COST,
        name="run_experts",
    )(own_place(), rows_in, back_in, slots, chances, *[w for w, _ in weights])
    return out


ATTENTION_PARAMS = pltpu.CompilerParams(vmem_limit_bytes=60 * 2**20)


def turned_half(x):
    lanes = lax.broadcasted_iota(jnp.int32, x.shape, 1) % HEAD_SIZE
    half = HEAD_SIZE // 2
    return jnp.where(lanes < half, -pltpu.roll(x, 128 - half, 1), pltpu.roll(x, half, 1))


def head(x, h):
    return x[:, h * HEAD_SIZE : (h + 1) * HEAD_SIZE]


def attention_forward(token_blocks, gain, parts, tables, query_cols, key_cols):
    blocks = len(token_blocks)
    rows, width = token_blocks[0].shape
    length = rows * blocks
    count = len(parts)
    places = part_places()
    columns = query_cols + 2 * key_cols
    heads = query_cols // HEAD_SIZE
    ratio = query_cols // key_cols
    step = 256

    def kernel(me_ref, gain_ref, cosine_ref, sine_ref, down_ref, along_ref, *refs):
        token_refs, part_refs = refs[:blocks], refs[blocks : blocks + count]
        full, normed, factors, qkv, heads_out, spread, branch = refs[blocks + count :]
        for place, ref in zip(places, part_refs):
            full[me_ref[0] ^ place] = ref[...]
        for s in range(blocks):
            x = token_refs[s][...].astype(f32)
            factor = rms_factor(x)
            span = slice(s * rows, (s + 1) * rows)
            factors[span, :] = factor
            normed[span, :] = (x * factor * gain_ref[...]).astype(bf16)
        weights = full[...].reshape(width, full.shape[2])
        projected = jnp.dot(normed[...], weights[:, :columns], preferred_element_type=f32)
        for g in range((query_cols + key_cols) // 128):
            span = slice(g * 128, (g + 1) * 128)
            x = projected[:, span]
            qkv[:, span] = (x * cosine_ref[...] + turned_half(x) * sine_ref[...]).astype(bf16)
        qkv[:, query_cols + key_cols :] = projected[:, query_cols + key_cols :].astype(bf16)
        for q in range(0, length, step):
            span = slice(q, q + step)
            mixed = []
            mask = along_ref[...] <= down_ref[span, :]
            query = qkv[span, :query_cols]
            for h in range(heads):
                key = head(qkv[:, query_cols : query_cols + key_cols], h // ratio)
                value = head(qkv[:, query_cols + key_cols :], h // ratio)
                scores = jnp.where(mask, contract_cols(head(query, h), key) * score_factor, masked_value)
                top = jnp.max(scores, axis=1, keepdims=True)
                exps = jnp.exp(scores - top)
                total = jnp.sum(exps, axis=1, keepdims=True)
                probs = (exps * (1.0 / total)).astype(bf16)
                mixed.append(jnp.dot(probs, value, preferred_element_type=f32).astype(bf16))
                spread[span, h : h + 1] = top + jnp.log(total)
            heads_out[span, :] = jnp.concatenate(mixed, axis=1)
        branch[...] = contract_cols(heads_out[...], weights[:, columns:]).astype(bf16)

    vmem = pl.BlockSpec(memory_space=pltpu.VMEM)
    return pl.pallas_call(
        kernel,
        out_shape=[
            jax.ShapeDtypeStruct((count,) + parts[0].shape, bf16),
            jax.ShapeDtypeStruct((length, width), bf16),
            jax.ShapeDtypeStruct((length, 1), f32),
            jax.ShapeDtypeStruct((length, columns), bf16),
            jax.ShapeDtypeStruct((length, query_cols), bf16),
            jax.ShapeDtypeStruct((length, heads), f32),
            jax.ShapeDtypeStruct((length, width), bf16),
        ],
        in_specs=[pl.BlockSpec(memory_space=pltpu.SMEM)] + [vmem] * (5 + blocks + count),
        out_specs=[vmem] * 7,
        compiler_params=ATTENTION_PARAMS,
        cost_estimate=SMALL_COST,
        name="attention_forward",
    )(own_place(), gain[None], *tables, *token_blocks, *parts)


def attention_backward(pieces, token_blocks, tables, full, factors, qkv, spread, query_cols, key_cols):
    blocks = len(pieces)
    rows, width = pieces[0].shape
    length = rows * blocks
    columns = query_cols + 2 * key_cols
    heads = query_cols // HEAD_SIZE
    pairs = key_cols // HEAD_SIZE
    ratio = heads // pairs
    step = 256

    def kernel(cosine_ref, sine_ref, down_ref, along_ref, full_ref, factors_ref, qkv_ref, spread_ref, *refs):
        piece_refs, token_refs = refs[:blocks], refs[blocks : 2 * blocks]
        back, normed_back, gain_back, heads_back, turned = refs[2 * blocks :]
        weights = full_ref[...].reshape(width, full_ref.shape[2])
        for s in range(blocks):
            part = jnp.dot(piece_refs[s][...], weights[:, columns:], preferred_element_type=f32)
            heads_back[s * rows : (s + 1) * rows, :] = part.astype(bf16)
        key_back, value_back = [None] * pairs, [None] * pairs

        def add(total, value):
            return value if total is None else total + value

        for q in range(0, length, step):
            span = slice(q, q + step)
            mask = along_ref[...] <= down_ref[span, :]
            query = qkv_ref[span, :query_cols]
            upper = heads_back[span, :]
            query_back = []
            for h in range(heads):
                g = h // ratio
                key = head(qkv_ref[:, query_cols : query_cols + key_cols], g)
                value = head(qkv_ref[:, query_cols + key_cols :], g)
                query_h, upper_h = head(query, h), head(upper, h)
                scores = jnp.where(mask, contract_cols(query_h, key) * score_factor, masked_value)
                probs = jnp.exp(scores - spread_ref[span, h : h + 1])
                prob_back = contract_cols(upper_h, value)
                inner = jnp.sum(probs * prob_back, axis=1, keepdims=True)
                score_back = (probs * (prob_back - inner)).astype(bf16)
                query_back.append(jnp.dot(score_back, key, preferred_element_type=f32) * score_factor)
                key_back[g] = add(key_back[g], contract_rows(score_back, query_h))
                value_back[g] = add(value_back[g], contract_rows(probs.astype(bf16), upper_h))
            turned[span, :query_cols] = jnp.concatenate(query_back, axis=1)
        turned[:, query_cols:] = jnp.concatenate(
            [k * score_factor for k in key_back] + value_back, axis=1
        )
        for g in range((query_cols + key_cols) // 128):
            span = slice(g * 128, (g + 1) * 128)
            x = turned[:, span]
            back[:, span] = (x * cosine_ref[...] - turned_half(x) * sine_ref[...]).astype(bf16)
        back[:, query_cols + key_cols :] = turned[:, query_cols + key_cols :].astype(bf16)
        total = None
        for s in range(blocks):
            span = slice(s * rows, (s + 1) * rows)
            part = contract_cols(back[span, :], weights[:, :columns])
            normed_back[s] = part.astype(bf16)
            scaled = part * (token_refs[s][...].astype(f32) * factors_ref[span, :])
            total = add(total, jnp.sum(scaled, axis=0, keepdims=True))
        gain_back[...] = total

    vmem = pl.BlockSpec(memory_space=pltpu.VMEM)
    return pl.pallas_call(
        kernel,
        out_shape=[
            jax.ShapeDtypeStruct((length, columns), bf16),
            jax.ShapeDtypeStruct((blocks, rows, width), bf16),
            jax.ShapeDtypeStruct((1, width), f32),
        ],
        in_specs=[vmem] * (8 + 2 * blocks),
        out_specs=[vmem] * 3,
        scratch_shapes=[pltpu.VMEM((length, query_cols), bf16), pltpu.VMEM((length, columns), f32)],
        compiler_params=ATTENTION_PARAMS,
        cost_estimate=LARGE_COST,
        name="attention_backward",
    )(*tables, full, factors, qkv, spread, *pieces, *token_blocks)


def attention_gradients(normed, back, pieces, heads):
    blocks = len(pieces)
    rows, width = pieces[0].shape
    columns = back.shape[1]
    both = columns + heads.shape[1]
    places = part_places()
    count = len(places)
    cut = width // count

    def kernel(me_ref, normed_ref, back_ref, heads_ref, *refs):
        keep, give, total = refs[blocks:]
        total[:, :columns] = contract_rows(normed_ref[...], back_ref[...]).astype(bf16)
        piece = jnp.concatenate([ref[...] for ref in refs[:blocks]], axis=0)
        total[:, columns:] = contract_rows(piece, heads_ref[...]).astype(bf16)
        for place in places:
            spot = pl.ds(pl.multiple_of((me_ref[0] ^ place) * cut, cut), cut)
            (give if place % 2 else keep)[place // 2] = total[spot, :]

    vmem = pl.BlockSpec(memory_space=pltpu.VMEM)
    shape = jax.ShapeDtypeStruct((count // 2, cut, both), bf16)
    return pl.pallas_call(
        kernel,
        out_shape=[shape, shape],
        in_specs=[pl.BlockSpec(memory_space=pltpu.SMEM)] + [vmem] * (3 + blocks),
        out_specs=[vmem] * 2,
        scratch_shapes=[pltpu.VMEM((width, both), bf16)],
        compiler_params=ATTENTION_PARAMS,
        cost_estimate=LARGE_COST,
        name="attention_gradients",
    )(own_place(), normed, back, heads, *pieces)


def local(
    tokens,
    first_gain,
    query_weight,
    key_matrix,
    value_matrix,
    out_weight,
    second_gain,
    gate_weight,
    up_weight,
    down_weight,
    routes,
    route_logits,
    cotangent,
):
    groups, many = lax.axis_size("gx"), lax.axis_size("gt")
    me_x, me_w = lax.axis_index("gx"), lax.axis_index("gw")
    own_tokens = tokens[0]
    rows, width = own_tokens.shape
    query_cols = query_weight.shape[1]
    key_cols = key_matrix.shape[1]
    query_heads = query_cols // HEAD_SIZE
    pair_heads = key_cols // HEAD_SIZE
    ratio = query_heads // pair_heads
    experts = gate_weight.shape[0]
    some = experts * 2 // 5
    spans = ((0, some), (some, experts - some))

    token_blocks = gather_gx(own_tokens)
    attention = jnp.concatenate(
        [query_weight, key_matrix, value_matrix, out_weight.T], axis=1
    )
    across = swap(attention, "gw", 1)
    along = over_y(attention)
    both = over_y(across)
    down_turned = jnp.swapaxes(down_weight, 1, 2)
    keep, give = halve_weights(gate_weight, up_weight, down_turned)
    across, give = tie(across, give)
    attention_parts = [attention, across] + along + both
    attention_parts, keep = tie(attention_parts, keep)
    token_blocks, attention_parts, keep_sent = tie(token_blocks, attention_parts, keep)
    attention_parts = attention_parts + [swap(p, "co", 1) for p in attention_parts]

    given_across, given_along = swap(give, "gw", 1), over_y(keep)
    mirror_keep = swap(keep_sent, "co", 1)

    logits = route_logits[0].T
    weights = jnp.exp(logits - jnp.max(logits, axis=0, keepdims=True))
    chance = weights / jnp.sum(weights, axis=0, keepdims=True)
    chance_high = lax.reduce_precision(chance, 8, 7)
    routing = jnp.concatenate([routes[0].T.astype(f32), chance_high, chance - chance_high], axis=0)
    routing = jnp.pad(routing.astype(bf16).T, ((0, 0), (0, 128 - 3 * TOPK)))
    payload = jnp.concatenate([cotangent[0], routing], axis=1)
    payload, token_blocks = tie(payload, token_blocks)
    turned = jnp.stack([w * groups + (me_x ^ s) for w in range(2) for s in range(groups)])
    gathered = lax.all_gather(payload, "gx", axis=0)

    positions = jnp.concatenate(
        [(me_x ^ s) * rows + jnp.arange(rows, dtype=jnp.int32) for s in range(groups)]
    ).astype(f32)
    half = HEAD_SIZE // 2
    freq = rope_base ** (-(jnp.arange(half, dtype=f32) * 2.0 / HEAD_SIZE))
    angle = positions[:, None] * jnp.tile(freq, 128 // half)[None, :]
    tables = (jnp.cos(angle), jnp.sin(angle), positions[:, None], positions[None, :])
    attention_full, normed_one, factor_all, qkv, heads, spread, branch_parts = attention_forward(
        token_blocks, first_gain, attention_parts, tables, query_cols, key_cols
    )

    branch_parts, mirror_keep = tie(branch_parts, mirror_keep)
    branch_got = [
        swap(branch_parts[s * rows : (s + 1) * rows], "gx", s) for s in range(1, groups)
    ]
    given_across, gathered, branch_got[0] = tie(given_across, gathered, branch_got[0])
    gathered_across = swap(gathered, "gw", 1)
    branch = branch_parts[:rows].astype(f32)
    for value in branch_got:
        branch = branch + value.astype(f32)

    hidden = own_tokens.astype(f32)
    middle = hidden + residual_factor * branch
    factor_two = rms_factor(middle)
    normed_two = (middle * factor_two * second_gain).astype(bf16)

    normed_two, given_across, given_along = tie(normed_two, given_across, given_along)
    normed_parts = gather_gx(normed_two)
    both_0 = over_y(given_across[:some])
    turned_parts = {s: swap(normed_parts[s], "gw", 1) for s in (0, 1)}

    gathered = jnp.concatenate([gathered, gathered_across])
    routes_of, slots, _, slots_by, chances_by = route_slots(gathered, turned, me_x * experts, experts, width)
    back_in = gather_slots(gathered, (turned, width), slots)
    normed_parts, turned_parts[0], turned_parts[1], both_0, given_across, given_along, back_in = tie(
        normed_parts, turned_parts[0], turned_parts[1], both_0, given_across, given_along, back_in
    )

    rest = [s for s in range(groups) if s not in (0, 1)]
    turned_rest = swap(jnp.stack([normed_parts[s] for s in rest]), "gw", 1)
    both_1 = over_y(given_across[some:])
    mirror_given = [swap(v, "co", 1) for v in [given_across] + given_along]
    mirror_both_0 = [swap(v, "co", 1) for v in both_0]
    normed_rows = normed_parts + [turned_parts[0], turned_parts[1]]
    normed_rows = normed_rows + [turned_rest[i] for i in range(len(rest))]
    rows_in = gather_slots(normed_rows, None, slots)
    rows_back, mixed_parts, chance_parts, gradients, given = [], [], [], [], []
    for i, (start, size) in enumerate(spans):
        if i == 0:
            both, mirror_both = both_0, mirror_both_0
        else:
            rows_in, rows_back[0], both_1 = tie(rows_in, rows_back[0], both_1)
            both, mirror_both = both_1, [swap(v, "co", 1) for v in both_1]
        parts = [(v, start) for v in [keep, given_across] + given_along] + [(v, 0) for v in both]
        parts = parts + [(v, start) for v in [mirror_keep] + mirror_given] + [(v, 0) for v in mirror_both]
        result = run_experts(rows_in, back_in, parts, start, size, slots_by, chances_by)
        for lot, value in zip((rows_back, mixed_parts, chance_parts, gradients, given), result):
            lot.append(value)

    got = [None, None]

    def joint(i, t, w):
        return gradients[i][2 * t + w].astype(f32) + got[i][2 * t + w].astype(f32)

    others = range(1, many)
    got[0] = swap(given[0], "co", 1)
    got[0], rows_back = tie(got[0], rows_back)
    got[1] = swap(given[1], "co", 1)
    far = [joint(0, t, 1).astype(bf16) for t in others]
    far, rows_back = tie(far, rows_back)
    along_one_0 = spread_y(far)
    plain = jnp.arange(2 * groups, dtype=jnp.int32)
    summed = sum_slots(rows_back, slots, plain)
    pieces = ((2, groups), (0, 2))
    crossed = [swap(summed[groups + a : groups + b], "gw", 1) for a, b in pieces]
    far = [joint(1, t, 1).astype(bf16) for t in others]
    crossed[1], along_one_0, far, got[1] = tie(crossed[1], along_one_0, far, got[1])
    along_one_1 = spread_y(far)

    def half_sum(s):
        a, b = pieces[0] if s >= 2 else pieces[1]
        value = crossed[0] if s >= 2 else crossed[1]
        return summed[s].astype(f32) + value[s - a].astype(f32)

    normed_got = {s: swap(half_sum(s).astype(bf16), "gx", s) for s in range(2, groups)}
    normed_got[1] = swap(half_sum(1).astype(bf16), "gx", 1)
    normed_got[3], mixed_parts = tie(normed_got[3], mixed_parts)
    mixed_rows = sum_slots(mixed_parts, slots, plain)
    chance_part = jnp.swapaxes(jnp.concatenate(chance_parts, axis=0), 0, 1)
    ids = (me_x * experts + jnp.arange(experts, dtype=jnp.int32)).astype(f32)
    same = routes_of[:, None, :, :] == ids[None, :, None, None]
    chance_rows = jnp.sum(jnp.where(same, chance_part[:, :, None, :], 0.0), axis=1)
    normed_two_back = half_sum(0)
    for value in normed_got.values():
        normed_two_back = normed_two_back + value.astype(f32)

    upstream = cotangent[0].astype(f32)
    middle_back = upstream + norm_back(middle, factor_two, second_gain, normed_two_back)
    second_part = jnp.sum(normed_two_back * middle * factor_two, axis=0)
    branch_back = (residual_factor * middle_back).astype(bf16)
    far = [joint(0, t, 0).astype(bf16) for t in others]
    branch_back, far = tie(branch_back, far)
    branch_back_blocks = gather_gx(branch_back)
    far, along_one_1 = tie(far, along_one_1)
    along_zero_0 = spread_y(far)

    def near(i, along):
        total = joint(i, 0, 1)
        for value in along:
            total = total + value.astype(f32)
        return total.astype(bf16)

    crossed_0 = swap(near(0, along_one_0), "gw", 1)
    crossed_0, mixed_rows = tie(crossed_0, mixed_rows)
    mixed_crossed = swap(mixed_rows[groups:], "gw", 1)
    branch_back_blocks[1], got[1] = tie(branch_back_blocks[1], got[1])
    near_1 = near(1, along_one_1)
    far = [joint(1, t, 0).astype(bf16) for t in others]
    mixed_rows = mixed_rows[:groups].astype(f32) + mixed_crossed.astype(f32)
    mixed_send = mixed_rows.astype(bf16)
    branch_back_blocks, near_1, far, mixed_send, chance_rows = tie(
        branch_back_blocks, near_1, far, mixed_send, chance_rows
    )
    mixed_got = [swap(mixed_send[s], "gx", s) for s in range(1, groups)]
    along_zero_0, far = tie(along_zero_0, far)
    along_zero_1 = spread_y(far)
    crossed_1 = swap(near_1, "gw", 1)

    back, normed_one_parts, first_part = attention_backward(
        branch_back_blocks, token_blocks, tables, attention_full, factor_all, qkv, spread, query_cols, key_cols
    )
    keep_gradient, give_gradient = attention_gradients(normed_one, back, branch_back_blocks, heads)
    got_gradient = swap(give_gradient, "co", 1)
    normed_one_parts, mixed_got, got_gradient = tie(normed_one_parts, mixed_got, got_gradient)
    mixed = mixed_rows[0]
    for value in mixed_got:
        mixed = mixed + value.astype(f32)
    output = (middle + residual_factor * mixed).astype(bf16)
    normed_got = [swap(normed_one_parts[s], "gx", s) for s in range(1, groups)]
    attention_sum = scatter_gy(keep_gradient, got_gradient)
    gains = jnp.stack([first_part[0], second_part])
    gains, along_zero_1, crossed_1, chance_rows = tie(gains, along_zero_1, crossed_1, chance_rows)
    chance_crossed = swap(chance_rows[groups:], "gw", 1)
    normed_got, chance_rows, chance_crossed = tie(normed_got, chance_rows, chance_crossed)
    gains = sum_everywhere(gains)
    normed_one_back = normed_one_parts[0].astype(f32)
    for value in normed_got:
        normed_one_back = normed_one_back + value.astype(f32)
    tokens_back = middle_back + norm_back(hidden, factor_all[:rows], first_gain, normed_one_back)
    chance_rows = chance_rows[:groups] + chance_crossed
    chance_back = chance_rows[0]
    for s in range(1, groups):
        chance_back = chance_back + swap(chance_rows[s], "gx", s)
    logit_back = chance * (chance_back - jnp.sum(chance * chance_back, axis=0, keepdims=True))
    sums = finish_gradients(
        [gradients[0], got[0]] + along_zero_0, crossed_0, 0, None, experts
    )
    gate_sum, up_sum, down_sum = finish_gradients(
        [gradients[1], got[1]] + along_zero_1, crossed_1, some, sums, experts
    )
    return (
        output[None],
        tokens_back[None],
        gains[0],
        attention_sum[:, :query_cols],
        attention_sum[:, query_cols : query_cols + key_cols],
        attention_sum[:, query_cols + key_cols : query_cols + 2 * key_cols],
        attention_sum[:, query_cols + 2 * key_cols :].T,
        gains[1],
        gate_sum,
        up_sum,
        jnp.swapaxes(down_sum, 1, 2),
        logit_back.T[None],
    )


def solution(mesh):
    groups, others = mesh.shape["gx"], mesh.shape["gy"]
    split = Mesh(mesh.devices.reshape(groups, others // 4, 2, 2), ("gx", "gt", "gw", "co"))
    gy = ("gt", "gw", "co")
    in_specs = (
        P(gy, "gx", None),
        P(),
        P(gy, "gx"),
        P(gy, "gx"),
        P(gy, "gx"),
        P("gx", gy),
        P(),
        P("gx", gy, None),
        P("gx", gy, None),
        P("gx", None, gy),
        P(gy, "gx", None),
        P(gy, "gx", None),
        P(gy, "gx", None),
    )
    out_specs = (
        P(gy, "gx", None),
        P(gy, "gx", None),
        P(),
        P(gy, "gx"),
        P(gy, "gx"),
        P(gy, "gx"),
        P("gx", gy),
        P(),
        P("gx", gy, None),
        P("gx", gy, None),
        P("gx", None, gy),
        P(gy, "gx", None),
    )
    return jax.shard_map(local, mesh=split, in_specs=in_specs, out_specs=out_specs, check_vma=False)
```

time: 607 us -> 557 us (0.918)
  waiting for transfers between devices: 286 us -> 217 us
  Pallas kernels: 108 us -> 144 us
  starting transfers between devices: 72 us -> 99.4 us
  matrix products: 23.3 us -> 0 us
  local copies, waits for them, and re-layouts: 40.1 us -> 28.6 us
  other arithmetic: 50.3 us -> 41.7 us
    ppermute x73 -> x60, waiting for transfers between devices: 286 us -> 188 us  [swap(): return lax.ppermute(value, axis, [(i, i ^ step) for i in range(count)])]
    pallas_call x1 -> x4, Pallas kernels: 0.21 us -> 36.5 us  [the longest x1 15.7 us: attention_backward(): pl.pallas_call(kernel, out_shape=[jax.ShapeDtypeStruct((length, columns),...]
    all_gather x1, waiting for transfers between devices: 0.02 us -> 24.1 us  [local(): gathered = lax.all_gather(payload, 'gx', axis=0)]
    dot_general x13 -> x0, matrix products: 23.3 us -> none  [the longest x1 4.46 us: attend_backward(): jnp.einsum('qhgd,khd->hgqk', heads_back, value_rows, preferred_element_ty...]
    ppermute x73 -> x60, starting transfers between devices: 71.9 us -> 91.5 us  [swap(): return lax.ppermute(value, axis, [(i, i ^ step) for i in range(count)])]
    ppermute x0 -> x6, starting transfers between devices: none -> 7.87 us  [sum_everywhere(): lax.ppermute(value, axes, [(i, i ^ s) for i in range(count)])]
    unnamed x212 -> x135, local copies, waits for them, and re-layouts: 21.9 us -> 14.1 us
  transfers between devices with their start and end apart: 75 -> 67, of which waited for: 29 -> 25; matrix products, arithmetic and copies ran while one was open for 15% -> 10% of each run, Pallas kernels for 18% -> 21%
where the time goes in v4:
time: 557 us; the launch traced here: 546 us
  waiting for transfers between devices  217 us (39%)
  Pallas kernels  144 us (26%)
  starting transfers between devices  99.4 us (18%)
  other arithmetic  41.7 us (7%)
  local copies, waits for them, and re-layouts  28.6 us (5%)
  between operations  15.1 us (3%)
    ppermute x60, waiting for transfers between devices, swap(): return lax.ppermute(value, axis, [(i, i ^ step) for i in range(count)])  188 us
    ppermute x60, starting transfers between devices, swap(): return lax.ppermute(value, axis, [(i, i ^ step) for i in range(count)])  91.5 us
    pallas_call x2, Pallas kernels, run_experts(): pl.pallas_call(kernel, grid_spec=pltpu.PrefetchScalarGridSpec(num_scalar_...  51.9 us
    all_gather x1, waiting for transfers between devices, local(): gathered = lax.all_gather(payload, 'gx', axis=0)  24.1 us
    pallas_call x2, Pallas kernels, gather_slots(): pl.pallas_call(kernel_list if listed else kernel_array, grid_spec=pltpu.P...  17.4 us
    pallas_call x2, Pallas kernels, sum_slots(): pl.pallas_call(kernel, grid_spec=pltpu.PrefetchScalarGridSpec(num_scalar_...  17.1 us
    pallas_call x1, Pallas kernels, attention_backward(): pl.pallas_call(kernel, out_shape=[jax.ShapeDtypeStruct((length, columns),...  15.7 us
    unnamed x135, local copies, waits for them, and re-layouts  14.1 us
  transfers between devices with their start and end apart: 67, of which 25 were waited for; matrix products, arithmetic and copies ran while one was open for 10% of the time, Pallas kernels for 21%

profile of v4, /device:TPU:0, one launch (start us, length us, event | category | flops | bytes accessed | tf_op | source)
XLA Modules:
  0.0 546.5 jit_solution(1999205058111837137)
XLA Ops:
  22.2 8.3 %halve_weights.1 = (bf16[10,192,768]{2,1,0:T(8,128)(2,1)}, bf16[10,192,768]{2,1,0:T(8,128)(2,1)}) custom-call(s32[1]{0:T(128)} %bitcast.17.side_ref, bf16[10,192,512]{2,1,0:T(8,128)(2,1)} %gate_ref.1, bf16[10,192,512]{2,1,0:T(8,128)(2,1)} %up_ref.1, bf16[10,192,512]{2,1,0:T(8,128)(2,1)} %bitcast.190), custom_call_target="tpu_custom_call" | custom-call | flops 10000000000 | bytes 100000000 | tf_op jit(solution)/shard_map/halve_weights/pallas_call | solution.py:109
  30.7 13.7 %collective-permute-done.1.refs_2_.refs_6_ = bf16[128,1536]{1,0:T(8,128)(2,1)S(1)} collective-permute-done((bf16[128,1536]{1,0:T(8,128)(2,1)}, bf16[128,1536]{1,0:T(8,128)(2,1)S(1)}, u32[]{:S(2)}, u32[]{:S(2)}) %collective-permute-start.1) | collective-permute-done | bytes 393248 | tf_op jit(solution)/shard_map/ppermute | solution.py:30
  55.5 12.1 %attention_forward.1 = (bf16[8,192,1024]{2,1,0:T(8,128)(2,1)}, bf16[512,1536]{1,0:T(8,128)(2,1)}, f32[512,1]{1,0:T(8,128)}, bf16[512,640]{1,0:T(8,128)(2,1)}, bf...) custom-call(s32[1]{0:T(128)} %bitcast.1.me_ref, f32[1,1536]{1,0:T(1,128)} %broadcast_in_dim.27.gain_ref, ...), custom_call_target="tpu_custom_call" | custom-call | flops 1 | bytes 1 | tf_op jit(solution)/shard_map/attention_forward/pallas_call | solution.py:468
  79.3 24.1 %all-gather.3.cloned.1.call-done = bf16[512,1664]{1,0:T(8,128)(2,1)} async-done(((bf16[128,1664]{1,0:T(8,128)(2,1)}), bf16[512,1664]{1,0:T(8,128)(2,1)}) %all-gather.3.cloned.1.call-update) | async-done | bytes 1703952 | tf_op jit(solution)/shard_map/all_gather | solution.py:650
  103.4 7.8 %collective-permute-done.11.refs_1_ = bf16[10,192,768]{2,1,0:T(8,128)(2,1)S(1)} collective-permute-done((bf16[10,192,768]{2,1,0:T(8,128)(2,1)}, bf16[10,192,768]{2,1,0:T(8,128)(2,1)S(1)}, u32[]{:S(2)}, u32[]{:S(2)}) %collective-permute-start.11) | collective-permute-done | bytes 2949152 | tf_op jit(solution)/shard_map/ppermute | solution.py:30
  122.8 8.2 %collective-permute-start.17 = (bf16[128,1536]{1,0:T(8,128)(2,1)}, bf16[128,1536]{1,0:T(8,128)(2,1)}, u32[]{:S(2)}, u32[]{:S(2)}) collective-permute-start(bf16[128,1536]{1,0:T(8,128)(2,1)} %multiply_convert_fusion.1.refs_0_), channel_id=1, source_target_pairs={{0,8},{8,0},{16,24},{24,16},{1,9},{9,1},{17,25},{25,17},{2,10},{10... | collective-permute-start | bytes 1179656 | tf_op jit(solution)/shard_map/ppermute | solution.py:30
  134.0 12.6 %collective-permute-done.17.refs_1_ = bf16[128,1536]{1,0:T(8,128)(2,1)} collective-permute-done((bf16[128,1536]{1,0:T(8,128)(2,1)}, bf16[128,1536]{1,0:T(8,128)(2,1)}, u32[]{:S(2)}, u32[]{:S(2)}) %collective-permute-start.17) | collective-permute-done | bytes 393248 | tf_op jit(solution)/shard_map/ppermute | solution.py:30
  161.2 8.3 %gather_slots.2.back_ref = bf16[10,8,48,1536]{3,2,1,0:T(8,128)(2,1)} custom-call(s32[8]{0:T(128)S(1)} %copy-done.4, f32[8,10,128]{2,1,0:T(8,128)S(1)} %copy-done.2, bf16[8,128,1664]{2,1,0:T(8,128)(2,1)S(1)} %copy-done.1), custom_call_target="tpu_custom_call" | custom-call | flops 1 | bytes 1 | tf_op jit(solution)/shard_map/gather_slots/pallas_call | solution.py:274
  174.9 16.3 %collective-permute-done.23 = bf16[2,128,1536]{2,1,0:T(8,128)(2,1)S(1)} collective-permute-done((bf16[2,128,1536]{2,1,0:T(8,128)(2,1)S(1)}, bf16[2,128,1536]{2,1,0:T(8,128)(2,1)S(1)}, u32[]{:S(2)}, u32[]{:S(2)}) %collective-permute-start.23) | collective-permute-done | bytes 786464 | tf_op jit(solution)/shard_map/ppermute | solution.py:30
  191.3 9.1 %gather_slots.3.rows_ref = bf16[10,8,48,1536]{3,2,1,0:T(8,128)(2,1)} custom-call(s32[1]{0:T(128)} %constant.46.clone.1.order_ref, f32[8,10,128]{2,1,0:T(8,128)S(1)} %copy-done.2, bf16[128,1536]{1,0:T(8,128)(2,1)} %multiply_convert_fusion.1.refs_0_, bf16[128,1536]{1,0:T(8,128)(2,1)} %collective-permute-done.17.refs_1_, ...), custom_call_target="tpu_custom_call" | custom-call | flops 1 | bytes 1 | tf_op jit(solution)/shard_map/gather_slots/pallas_call | solution.py:274
  202.4 21.6 %run_experts.2 = (bf16[4,8,48,1536]{3,2,1,0:T(8,128)(2,1)}, bf16[4,8,48,1536]{3,2,1,0:T(8,128)(2,1)}, f32[4,8,128]{2,1,0:T(8,128)}, bf16[4,4,192,768]{3,2,1,0:T(8,128)(2,1)}, bf16[4,4,192,768]{3,2,1,0:T(8,128)(2,1)}) custom-call(s32[1]{0:T(128)} %bitcast.1.me_ref, bf16[10,8,48,1536]{3,2,1,0:T(8,128)(2,1)} %gather_slots.3.rows_ref, ...), custom_call_target="tpu_custom_call" | custom-call | flops 10000000000 | bytes 100000000 | tf_op jit(solution)/shard_map/run_experts/pallas_call | solution.py:377
  229.2 30.3 %run_experts.3 = (bf16[6,8,48,1536]{3,2,1,0:T(8,128)(2,1)}, bf16[6,8,48,1536]{3,2,1,0:T(8,128)(2,1)}, f32[6,8,128]{2,1,0:T(8,128)}, bf16[4,6,192,768]{3,2,1,0:T(8,128)(2,1)}, bf16[4,6,192,768]{3,2,1,0:T(8,128)(2,1)}) custom-call(s32[1]{0:T(128)} %bitcast.1.me_ref, bf16[10,8,48,1536]{3,2,1,0:T(8,128)(2,1)} %gather_slots.3.rows_ref, ...), custom_call_target="tpu_custom_call" | custom-call | flops 10000000000 | bytes 100000000 | tf_op jit(solution)/shard_map/run_experts/pallas_call | solution.py:377
  260.0 17.5 %collective-permute-done.27.refs_1_ = bf16[4,4,192,768]{3,2,1,0:T(8,128)(2,1)S(1)} collective-permute-done((bf16[4,4,192,768]{3,2,1,0:T(8,128)(2,1)}, bf16[4,4,192,768]{3,2,1,0:T(8,128)(2,1)S(1)}, u32[]{:S(2)}, u32[]{:S(2)}) %collective-permute-start.27) | collective-permute-done | bytes 4718624 | tf_op jit(solution)/shard_map/ppermute | solution.py:30
  282.7 8.7 %sum_slots.2 = bf16[8,128,1536]{2,1,0:T(8,128)(2,1)S(1)} custom-call(s32[8]{0:T(128)S(1)} %iota.32.order_ref, f32[8,10,128]{2,1,0:T(8,128)S(1)} %copy-done.3, bf16[4,8,48,1536]{3,2,1,0:T(8,128)(2,1)S(1)} %copy-done.5, bf16[6,8,48,1536]{3,2,1,0:T(8,128)(2,1)} %get-tuple-element.189.refs_1_), custom_call_target="tpu_custom_call" | custom-call | flops 10000000000 | bytes 100000000 | tf_op jit(solution)/shard_map/sum_slots/pallas_call | solution.py:306
  296.9 15.1 %collective-permute-done.30 = bf16[2,128,1536]{2,1,0:T(8,128)(2,1)S(1)} collective-permute-done((bf16[2,128,1536]{2,1,0:T(8,128)(2,1)S(1)}, bf16[2,128,1536]{2,1,0:T(8,128)(2,1)S(1)}, u32[]{:S(2)}, u32[]{:S(2)}) %collective-permute-start.30) | collective-permute-done | bytes 786464 | tf_op jit(solution)/shard_map/ppermute | solution.py:30
  312.0 16.3 %collective-permute-done.34 = bf16[2,128,1536]{2,1,0:T(8,128)(2,1)S(1)} collective-permute-done((bf16[2,128,1536]{2,1,0:T(8,128)(2,1)S(1)}, bf16[2,128,1536]{2,1,0:T(8,128)(2,1)S(1)}, u32[]{:S(2)}, u32[]{:S(2)}) %collective-permute-start.34) | collective-permute-done | bytes 786464 | tf_op jit(solution)/shard_map/ppermute | solution.py:30
  343.0 8.3 %sum_slots.3 = bf16[8,128,1536]{2,1,0:T(8,128)(2,1)S(1)} custom-call(s32[8]{0:T(128)S(1)} %iota.33.order_ref, f32[8,10,128]{2,1,0:T(8,128)S(1)} %copy-done.3, bf16[4,8,48,1536]{3,2,1,0:T(8,128)(2,1)S(1)} %bitcast.176, bf16[6,8,48,1536]{3,2,1,0:T(8,128)(2,1)} %get-tuple-element.197.refs_1_), custom_call_target="tpu_custom_call" | custom-call | flops 10000000000 | bytes 100000000 | tf_op jit(solution)/shard_map/sum_slots/pallas_call | solution.py:306
  351.3 15.1 %collective-permute-done.37 = bf16[128,1536]{1,0:T(8,128)(2,1)} collective-permute-done((bf16[128,1536]{1,0:T(8,128)(2,1)S(1)}, bf16[128,1536]{1,0:T(8,128)(2,1)}, u32[]{:S(2)}, u32[]{:S(2)}) %collective-permute-start.37) | collective-permute-done | bytes 393248 | tf_op jit(solution)/shard_map/ppermute | solution.py:30
  375.7 13.0 %collective-permute-done.39.refs_1_ = bf16[128,1536]{1,0:T(8,128)(2,1)S(1)} collective-permute-done((bf16[128,1536]{1,0:T(8,128)(2,1)S(1)}, bf16[128,1536]{1,0:T(8,128)(2,1)S(1)}, u32[]{:S(2)}, u32[]{:S(2)}) %collective-permute-start.39) | collective-permute-done | bytes 393248 | tf_op jit(solution)/shard_map/ppermute | solution.py:30
  396.4 8.3 %collective-permute-done.36 = bf16[4,128,1536]{2,1,0:T(8,128)(2,1)S(1)} collective-permute-done((bf16[4,128,1536]{2,1,0:T(8,128)(2,1)S(1)}, bf16[4,128,1536]{2,1,0:T(8,128)(2,1)S(1)}, u32[]{:S(2)}, u32[]{:S(2)}) %collective-permute-start.36) | collective-permute-done | bytes 1572896 | tf_op jit(solution)/shard_map/ppermute | solution.py:30
  408.4 15.7 %attention_backward.1 = (bf16[512,640]{1,0:T(8,128)(2,1)}, bf16[4,128,1536]{2,1,0:T(8,128)(2,1)}, f32[1,1536]{1,0:T(1,128)}) custom-call(f32[512,128]{1,0:T(8,128)} %get-tuple-element.319.cosine_ref, f32[512,128]{1,0:T(8,128)} %get-tuple-element.318.sine_ref, f32[512,1]{1,0:T(8,128)} %convert_element_type.271.down_ref, ...), custom_call_target="tpu_custom_call" | custom-call | flops 10000000000 | bytes 100000000 | tf_op jit(solution)/shard_map/attention_backward/pallas_call | solution.py:547
  436.8 15.7 %collective-permute-done.43 = bf16[128,1536]{1,0:T(8,128)(2,1)S(1)} collective-permute-done((bf16[128,1536]{1,0:T(8,128)(2,1)S(1)}, bf16[128,1536]{1,0:T(8,128)(2,1)S(1)}, u32[]{:S(2)}, u32[]{:S(2)}) %collective-permute-start.43) | collective-permute-done | bytes 393248 | tf_op jit(solution)/shard_map/ppermute | solution.py:30
  456.4 8.8 %collective-permute-done.45 = bf16[128,1536]{1,0:T(8,128)(2,1)S(1)} collective-permute-done((bf16[128,1536]{1,0:T(8,128)(2,1)S(1)}, bf16[128,1536]{1,0:T(8,128)(2,1)S(1)}, u32[]{:S(2)}, u32[]{:S(2)}) %collective-permute-start.45) | collective-permute-done | bytes 393248 | tf_op jit(solution)/shard_map/ppermute | solution.py:30
  486.8 7.8 %finish_gradients.3 = (f32[10,192,512]{2,1,0:T(8,128)}, f32[10,192,512]{2,1,0:T(8,128)}, f32[10,192,512]{2,1,0:T(8,128)}) custom-call(s32[1]{0:T(128)} %bitcast.17.side_ref, bf16[4,6,192,768]{3,2,1,0:T(8,128)(2,1)} %get-tuple-element.191.refs_0_, ...), custom_call_target="tpu_custom_call", output_to_operand_aliasing={{0}: (5, {}), {1}: (6, {}), {2}: (7, {})} | custom-call | flops 1 | bytes 1 | tf_op jit(solution)/shard_map/finish_gradients/pallas_call | solution.py:153
  (336 shorter events, 208.7 us)
Async XLA Ops:
  7.2 96.2 %all-gather.3.cloned.1.call-start = ((), (), s32[]{:S(2)}) async-start(), calls=%async_computation | async-start | bytes 2129920 | tf_op jit(solution)/shard_map/all_gather | solution.py:650
  45.3 65.9 %collective-permute-start.11 = (bf16[10,192,768]{2,1,0:T(8,128)(2,1)}, bf16[10,192,768]{2,1,0:T(8,128)(2,1)S(1)}, u32[]{:S(2)}, u32[]{:S(2)}) collective-permute-start(bf16[10,192,768]{2,1,0:T(8,128)(2,1)} %get-tuple-element.156), channel_id=1, source_target_pairs={{0,2},{2,0},{1,3},{3,1},{4,6},{6,4},{5,7},{7,5},{8,10},{10,8},{9,1... | collective-permute-start | bytes 8847368 | tf_op jit(solution)/shard_map/ppermute | solution.py:30
  47.0 73.2 %collective-permute-start.16 = (bf16[10,192,768]{2,1,0:T(8,128)(2,1)}, bf16[10,192,768]{2,1,0:T(8,128)(2,1)}, u32[]{:S(2)}, u32[]{:S(2)}) collective-permute-start(bf16[10,192,768]{2,1,0:T(8,128)(2,1)} %get-tuple-element.154.refs_0_), channel_id=1, source_target_pairs={{0,4},{4,0},{1,5},{5,1},{2,6},{6,2},{3,7},{7,3},{8,12},{12,8},{9,1... | collective-permute-start | bytes 8847368 | tf_op jit(solution)/shard_map/ppermute | solution.py:30
  69.9 41.3 %collective-permute-start.12 = (bf16[128,1536]{1,0:T(8,128)(2,1)}, bf16[128,1536]{1,0:T(8,128)(2,1)}, u32[]{:S(2)}, u32[]{:S(2)}) collective-permute-start(bf16[128,1536]{1,0:T(8,128)(2,1)} %get-tuple-element.302), channel_id=1, source_target_pairs={{0,8},{8,0},{16,24},{24,16},{1,9},{9,1},{17,25},{25,17},{2,10},{10... | collective-permute-start | bytes 1179656 | tf_op jit(solution)/shard_map/ppermute | solution.py:30
  76.9 34.9 %collective-permute-start.13 = (bf16[128,1536]{1,0:T(8,128)(2,1)}, bf16[128,1536]{1,0:T(8,128)(2,1)}, u32[]{:S(2)}, u32[]{:S(2)}) collective-permute-start(bf16[128,1536]{1,0:T(8,128)(2,1)} %get-tuple-element.304), channel_id=1, source_target_pairs={{0,16},{8,24},{16,0},{24,8},{1,17},{9,25},{17,1},{25,9},{2,18},{10... | collective-permute-start | bytes 1179656 | tf_op jit(solution)/shard_map/ppermute | solution.py:30
  77.8 38.8 %collective-permute-start.14 = (bf16[128,1536]{1,0:T(8,128)(2,1)}, bf16[128,1536]{1,0:T(8,128)(2,1)}, u32[]{:S(2)}, u32[]{:S(2)}) collective-permute-start(bf16[128,1536]{1,0:T(8,128)(2,1)} %get-tuple-element.303), channel_id=1, source_target_pairs={{0,24},{8,16},{16,8},{24,0},{1,25},{9,17},{17,9},{25,1},{2,26},{10... | collective-permute-start | bytes 1179656 | tf_op jit(solution)/shard_map/ppermute | solution.py:30
  111.2 39.5 %collective-permute-start.15 = (bf16[4,128,1664]{2,1,0:T(8,128)(2,1)}, bf16[4,128,1664]{2,1,0:T(8,128)(2,1)}, u32[]{:S(2)}, u32[]{:S(2)}) collective-permute-start(bf16[4,128,1664]{2,1,0:T(8,128)(2,1)} %bitcast.186), channel_id=1, source_target_pairs={{0,2},{2,0},{1,3},{3,1},{4,6},{6,4},{5,7},{7,5},{8,10},{10,8},{9,1... | collective-permute-start | bytes 5111816 | tf_op jit(solution)/shard_map/ppermute | solution.py:30
  121.3 48.3 %collective-permute-start.22 = (bf16[4,192,768]{2,1,0:T(8,128)(2,1)}, bf16[4,192,768]{2,1,0:T(8,128)(2,1)}, u32[]{:S(2)}, u32[]{:S(2)}) collective-permute-start(bf16[4,192,768]{2,1,0:T(8,128)(2,1)} %slice.182), channel_id=1, source_target_pairs={{0,4},{4,0},{1,5},{5,1},{2,6},{6,2},{3,7},{7,3},{8,12},{12,8},{9,1... | collective-permute-start | bytes 3538952 | tf_op jit(solution)/shard_map/ppermute | solution.py:30
  131.6 37.9 %collective-permute-start.18 = (bf16[128,1536]{1,0:T(8,128)(2,1)}, bf16[128,1536]{1,0:T(8,128)(2,1)}, u32[]{:S(2)}, u32[]{:S(2)}) collective-permute-start(bf16[128,1536]{1,0:T(8,128)(2,1)} %multiply_convert_fusion.1.refs_0_), channel_id=1, source_target_pairs={{0,16},{8,24},{16,0},{24,8},{1,17},{9,25},{17,1},{25,9},{2,18},{10... | collective-permute-start | bytes 1179656 | tf_op jit(solution)/shard_map/ppermute | solution.py:30
  131.6 37.9 %collective-permute-start.19 = (bf16[128,1536]{1,0:T(8,128)(2,1)}, bf16[128,1536]{1,0:T(8,128)(2,1)}, u32[]{:S(2)}, u32[]{:S(2)}) collective-permute-start(bf16[128,1536]{1,0:T(8,128)(2,1)} %multiply_convert_fusion.1.refs_0_), channel_id=1, source_target_pairs={{0,24},{8,16},{16,8},{24,0},{1,25},{9,17},{17,9},{25,1},{2,26},{10... | collective-permute-start | bytes 1179656 | tf_op jit(solution)/shard_map/ppermute | solution.py:30
  174.8 49.2 %collective-permute-start.28 = (bf16[6,192,768]{2,1,0:T(8,128)(2,1)}, bf16[6,192,768]{2,1,0:T(8,128)(2,1)}, u32[]{:S(2)}, u32[]{:S(2)}) collective-permute-start(bf16[6,192,768]{2,1,0:T(8,128)(2,1)} %slice.186), channel_id=1, source_target_pairs={{0,4},{4,0},{1,5},{5,1},{2,6},{6,2},{3,7},{7,3},{8,12},{12,8},{9,1... | collective-permute-start | bytes 5308424 | tf_op jit(solution)/shard_map/ppermute | solution.py:30
  259.4 34.2 %collective-permute-start.32 = (bf16[4,6,192,768]{3,2,1,0:T(8,128)(2,1)}, bf16[4,6,192,768]{3,2,1,0:T(8,128)(2,1)}, u32[]{:S(2)}, u32[]{:S(2)}) collective-permute-start(bf16[4,6,192,768]{3,2,1,0:T(8,128)(2,1)} %get-tuple-element.192), channel_id=1, source_target_pairs={{0,1},{1,0},{2,3},{3,2},{4,5},{5,4},{6,7},{7,6},{8,9},{9,8},{10,11... | collective-permute-start | bytes 21233672 | tf_op jit(solution)/shard_map/ppermute | solution.py:30
  293.4 34.9 %collective-permute-start.34 = (bf16[2,128,1536]{2,1,0:T(8,128)(2,1)S(1)}, bf16[2,128,1536]{2,1,0:T(8,128)(2,1)S(1)}, u32[]{:S(2)}, u32[]{:S(2)}) collective-permute-start(bf16[2,128,1536]{2,1,0:T(8,128)(2,1)S(1)} %get-tuple-element.294), channel_id=1, source_target_pairs={{0,2},{2,0},{1,3},{3,1},{4,6},{6,4},{5,7},{7,5},{8,10},{10,8},{9,1... | collective-permute-start | bytes 2359304 | tf_op jit(solution)/shard_map/ppermute | solution.py:30
  333.4 34.8 %collective-permute-start.33 = (bf16[4,192,768]{2,1,0:T(8,128)(2,1)S(1)}, bf16[4,192,768]{2,1,0:T(8,128)(2,1)S(1)}, u32[]{:S(2)}, u32[]{:S(2)}) collective-permute-start(bf16[4,192,768]{2,1,0:T(8,128)(2,1)S(1)} %fusion.1), channel_id=1, source_target_pairs={{0,2},{2,0},{1,3},{3,1},{4,6},{6,4},{5,7},{7,5},{8,10},{10,8},{9,1... | collective-permute-start | bytes 3538952 | tf_op jit(solution)/shard_map/ppermute | solution.py:30
  335.2 31.2 %collective-permute-start.37 = (bf16[128,1536]{1,0:T(8,128)(2,1)S(1)}, bf16[128,1536]{1,0:T(8,128)(2,1)}, u32[]{:S(2)}, u32[]{:S(2)}) collective-permute-start(bf16[128,1536]{1,0:T(8,128)(2,1)S(1)} %get-tuple-element.291), channel_id=1, source_target_pairs={{0,16},{8,24},{16,0},{24,8},{1,17},{9,25},{17,1},{25,9},{2,18},{10... | collective-permute-start | bytes 1179656 | tf_op jit(solution)/shard_map/ppermute | solution.py:30
  341.7 50.4 %collective-permute-start.42 = (bf16[6,192,768]{2,1,0:T(8,128)(2,1)}, bf16[6,192,768]{2,1,0:T(8,128)(2,1)S(1)}, u32[]{:S(2)}, u32[]{:S(2)}) collective-permute-start(bf16[6,192,768]{2,1,0:T(8,128)(2,1)} %fusion.2), channel_id=1, source_target_pairs={{0,4},{4,0},{1,5},{5,1},{2,6},{6,2},{3,7},{7,3},{8,12},{12,8},{9,1... | collective-permute-start | bytes 5308424 | tf_op jit(solution)/shard_map/ppermute | solution.py:30
  368.3 36.4 %collective-permute-start.36 = (bf16[4,128,1536]{2,1,0:T(8,128)(2,1)S(1)}, bf16[4,128,1536]{2,1,0:T(8,128)(2,1)S(1)}, u32[]{:S(2)}, u32[]{:S(2)}) collective-permute-start(bf16[4,128,1536]{2,1,0:T(8,128)(2,1)S(1)} %slice.197), channel_id=1, source_target_pairs={{0,2},{2,0},{1,3},{3,1},{4,6},{6,4},{5,7},{7,5},{8,10},{10,8},{9,1... | collective-permute-start | bytes 4718600 | tf_op jit(solution)/shard_map/ppermute | solution.py:30
  371.9 35.0 %collective-permute-start.40 = (bf16[128,1536]{1,0:T(8,128)(2,1)S(1)}, bf16[128,1536]{1,0:T(8,128)(2,1)S(1)}, u32[]{:S(2)}, u32[]{:S(2)}) collective-permute-start(bf16[128,1536]{1,0:T(8,128)(2,1)S(1)} %multiply_convert_fusion.refs_0_), channel_id=1, source_target_pairs={{0,16},{8,24},{16,0},{24,8},{1,17},{9,25},{17,1},{25,9},{2,18},{10... | collective-permute-start | bytes 1179656 | tf_op jit(solution)/shard_map/ppermute | solution.py:30
  374.9 32.0 %collective-permute-start.41 = (bf16[128,1536]{1,0:T(8,128)(2,1)S(1)}, bf16[128,1536]{1,0:T(8,128)(2,1)S(1)}, u32[]{:S(2)}, u32[]{:S(2)}) collective-permute-start(bf16[128,1536]{1,0:T(8,128)(2,1)S(1)} %multiply_convert_fusion.refs_0_), channel_id=1, source_target_pairs={{0,24},{8,16},{16,8},{24,0},{1,25},{9,17},{17,9},{25,1},{2,26},{10... | collective-permute-start | bytes 1179656 | tf_op jit(solution)/shard_map/ppermute | solution.py:30
  392.0 40.0 %collective-permute-start.50 = (bf16[4,192,768]{2,1,0:T(8,128)(2,1)}, bf16[4,192,768]{2,1,0:T(8,128)(2,1)}, u32[]{:S(2)}, u32[]{:S(2)}) collective-permute-start(bf16[4,192,768]{2,1,0:T(8,128)(2,1)} %get-tuple-element.230), channel_id=1, source_target_pairs={{0,4},{4,0},{1,5},{5,1},{2,6},{6,2},{3,7},{7,3},{8,12},{12,8},{9,1... | collective-permute-start | bytes 3538952 | tf_op jit(solution)/shard_map/ppermute | solution.py:30
  430.2 35.1 %collective-permute-start.46 = (bf16[4,192,1024]{2,1,0:T(8,128)(2,1)}, bf16[4,192,1024]{2,1,0:T(8,128)(2,1)S(1)}, u32[]{:S(2)}, u32[]{:S(2)}) collective-permute-start(bf16[4,192,1024]{2,1,0:T(8,128)(2,1)} %get-tuple-element.224), channel_id=1, source_target_pairs={{0,1},{1,0},{2,3},{3,2},{4,5},{5,4},{6,7},{7,6},{8,9},{9,8},{10,11... | collective-permute-start | bytes 4718600 | tf_op jit(solution)/shard_map/ppermute | solution.py:30
  430.2 52.1 %collective-permute-start.52 = (bf16[6,192,768]{2,1,0:T(8,128)(2,1)}, bf16[6,192,768]{2,1,0:T(8,128)(2,1)}, u32[]{:S(2)}, u32[]{:S(2)}) collective-permute-start(bf16[6,192,768]{2,1,0:T(8,128)(2,1)} %fusion), channel_id=1, source_target_pairs={{0,2},{2,0},{1,3},{3,1},{4,6},{6,4},{5,7},{7,5},{8,10},{10,8},{9,1... | collective-permute-start | bytes 5308424 | tf_op jit(solution)/shard_map/ppermute | solution.py:30
  432.0 50.3 %collective-permute-start.51 = (bf16[6,192,768]{2,1,0:T(8,128)(2,1)}, bf16[6,192,768]{2,1,0:T(8,128)(2,1)}, u32[]{:S(2)}, u32[]{:S(2)}) collective-permute-start(bf16[6,192,768]{2,1,0:T(8,128)(2,1)} %fusion.3), channel_id=1, source_target_pairs={{0,4},{4,0},{1,5},{5,1},{2,6},{6,2},{3,7},{7,3},{8,12},{12,8},{9,1... | collective-permute-start | bytes 5308424 | tf_op jit(solution)/shard_map/ppermute | solution.py:30
  494.6 34.8 %collective-permute-start.61 = (bf16[2,192,1024]{2,1,0:T(8,128)(2,1)S(1)}, bf16[2,192,1024]{2,1,0:T(8,128)(2,1)S(1)}, u32[]{:S(2)}, u32[]{:S(2)}) collective-permute-start(bf16[2,192,1024]{2,1,0:T(8,128)(2,1)S(1)} %copy-done.25), channel_id=1, source_target_pairs={{0,2},{2,0},{1,3},{3,1},{4,6},{6,4},{5,7},{7,5},{8,10},{10,8},{9,1... | collective-permute-start | bytes 2359304 | tf_op jit(solution)/shard_map/ppermute | solution.py:30
  (110 other events, 1701.8 us)
Sparse Core Ops, SparseCore 0:
  47.0 56.2 all-gather.2

commit v5 on v4

--- a/solution.py
+++ b/solution.py
@@ -170,25 +170,9 @@
     )(own_side(), *summed, crossed, *(before or ()))
 
 
-def scatter_gy(keep, got):
-    many = lax.axis_size("gt")
-    send = (keep[1::2].astype(f32) + got[1::2].astype(f32)).astype(bf16)
-    got_w = swap(send, "gw", 1)
-    total = keep[0::2].astype(f32) + got[0::2].astype(f32) + got_w.astype(f32)
-    own = total[0]
-    for value in spread_y([total[t].astype(bf16) for t in range(1, many)]):
-        own = own + value.astype(f32)
-    return own
-
-
-def sum_everywhere(value):
-    value = value + swap(value, "co", 1)
-    for axes in (("gt", "gw"), ("gx",)):
-        count = lax.axis_size(axes)
-        sent = [lax.ppermute(value, axes, [(i, i ^ s) for i in range(count)]) for s in range(1, count)]
-        for got in sent:
-            value = value + got
-    return value
+def others_of(value, axes):
+    count = lax.axis_size(axes)
+    return [lax.ppermute(value, axes, [(i, i ^ s) for i in range(count)]) for s in range(1, count)]
 
 
 def slot_mask(slot_row):
@@ -282,7 +266,7 @@
         ),
         out_shape=jax.ShapeDtypeStruct((experts, blocks, CAP, width), bf16),
         compiler_params=pltpu.CompilerParams(vmem_limit_bytes=40 * 2**20),
-        cost_estimate=SMALL_COST,
+        cost_estimate=LARGE_COST,
         name="gather_slots",
     )(prefetch, slots, *sources)
 
@@ -323,18 +307,34 @@
     blocks, _, width = rows_in.shape[1:]
     places = part_places()
     tokens = slots.shape[2]
-    cut, half = weights[0][0].shape[1], weights[0][0].shape[2] // 3
+    weights = [
+        [(w, first) for w, first in part if first < start + experts and first + w.shape[0] > start]
+        for part in weights
+    ]
+    flat = [piece for part in weights for piece in part]
+    cut, half = flat[0][0].shape[1], flat[0][0].shape[2] // 3
     count = len(places)
     total_slots = blocks * CAP
 
     def kernel(me_ref, rows_ref, back_ref, slots_ref, chances_ref, *refs):
-        rows_out, mixed_out, chance_out = refs[count : count + 3]
-        grads = refs[count + 3 : count + 5]
-        gu_full, d_full, gu_total, d_total = refs[count + 5 :]
+        rows_out, mixed_out, chance_out = refs[len(flat) : len(flat) + 3]
+        grads = refs[len(flat) + 3 : len(flat) + 5]
+        gu_full, d_full, gu_total, d_total = refs[len(flat) + 5 :]
         spots = [pl.ds(pl.multiple_of((me_ref[0] ^ place) * cut, cut), cut) for place in places]
-        for spot, part in zip(spots, refs[:count]):
-            gu_full[spot, :] = part[0, :, : 2 * half]
-            d_full[spot, :] = part[0, :, 2 * half :]
+        expert = start + pl.program_id(0)
+        part_refs = iter(refs[: len(flat)])
+        for spot, part in zip(spots, weights):
+            for w, first in part:
+                ref = next(part_refs)
+
+                def put(spot=spot, ref=ref):
+                    gu_full[spot, :] = ref[0, :, : 2 * half]
+                    d_full[spot, :] = ref[0, :, 2 * half :]
+
+                if len(part) == 1:
+                    put()
+                else:
+                    pl.when((expert >= first) & (expert < first + w.shape[0]))(put)
         rows = rows_ref[0].reshape(total_slots, width)
         back = back_ref[0].reshape(total_slots, width)
         masks = [slot_mask(slots_ref[0, b : b + 1, :]) for b in range(blocks)]
@@ -373,6 +373,11 @@
         return pl.BlockSpec((1,) + shape, lambda e, *_: (e + first,) + zeros)
 
     grad_shape = jax.ShapeDtypeStruct((count // 2, experts, cut, 3 * half), bf16)
+    def held(size, first):
+        return pl.BlockSpec(
+            (1, cut, 3 * half), lambda e, *_: (jnp.clip(e + start - first, 0, size - 1), 0, 0)
+        )
+
     slot_shape = jax.ShapeDtypeStruct((experts, blocks, CAP, width), bf16)
     out = pl.pallas_call(
         kernel,
@@ -385,7 +390,7 @@
                 block((blocks, tokens), start),
                 block((blocks, tokens), start),
             ]
-            + [block((cut, 3 * half), first) for _, first in weights],
+            + [held(w.shape[0], first) for w, first in flat],
             out_specs=[block((blocks, CAP, width)), block((blocks, CAP, width)), block((blocks, tokens))]
             + [pl.BlockSpec((count // 2, 1, cut, 3 * half), lambda e, *_: (0, e, 0, 0))] * 2,
             scratch_shapes=[
@@ -400,7 +405,7 @@
         compiler_params=pltpu.CompilerParams(vmem_limit_bytes=60 * 2**20),
         cost_estimate=LARGE_COST,
         name="run_experts",
-    )(own_place(), rows_in, back_in, slots, chances, *[w for w, _ in weights])
+    )(own_place(), rows_in, back_in, slots, chances, *[w for w, _ in flat])
     return out
 
 
@@ -417,7 +422,7 @@
     return x[:, h * HEAD_SIZE : (h + 1) * HEAD_SIZE]
 
 
-def attention_forward(token_blocks, gain, parts, tables, query_cols, key_cols):
+def attention_forward(token_blocks, gain, parts, mirrors, tables, query_cols, key_cols):
     blocks = len(token_blocks)
     rows, width = token_blocks[0].shape
     length = rows * blocks
@@ -429,10 +434,12 @@
     step = 256
 
     def kernel(me_ref, gain_ref, cosine_ref, sine_ref, down_ref, along_ref, *refs):
-        token_refs, part_refs = refs[:blocks], refs[blocks : blocks + count]
-        full, normed, factors, qkv, heads_out, spread, branch = refs[blocks + count :]
-        for place, ref in zip(places, part_refs):
-            full[me_ref[0] ^ place] = ref[...]
+        token_refs, part_refs = refs[:blocks], refs[blocks : blocks + count + 1]
+        full, normed, factors, qkv, heads_out, spread = refs[blocks + count + 1 : blocks + count + 7]
+        branch = refs[blocks + count + 7 :]
+        for i, ref in enumerate(part_refs[:count]):
+            full[me_ref[0] ^ places[i]] = ref[...]
+            full[me_ref[0] ^ places[count + i]] = part_refs[count][i]
         for s in range(blocks):
             x = token_refs[s][...].astype(f32)
             factor = rms_factor(x)
@@ -462,26 +469,28 @@
                 mixed.append(jnp.dot(probs, value, preferred_element_type=f32).astype(bf16))
                 spread[span, h : h + 1] = top + jnp.log(total)
             heads_out[span, :] = jnp.concatenate(mixed, axis=1)
-        branch[...] = contract_cols(heads_out[...], weights[:, columns:]).astype(bf16)
+        for s in range(blocks):
+            part = contract_cols(heads_out[s * rows : (s + 1) * rows, :], weights[:, columns:])
+            branch[s][...] = part.astype(bf16)
 
     vmem = pl.BlockSpec(memory_space=pltpu.VMEM)
     return pl.pallas_call(
         kernel,
         out_shape=[
-            jax.ShapeDtypeStruct((count,) + parts[0].shape, bf16),
+            jax.ShapeDtypeStruct((2 * count,) + parts[0].shape, bf16),
             jax.ShapeDtypeStruct((length, width), bf16),
             jax.ShapeDtypeStruct((length, 1), f32),
             jax.ShapeDtypeStruct((length, columns), bf16),
             jax.ShapeDtypeStruct((length, query_cols), bf16),
             jax.ShapeDtypeStruct((length, heads), f32),
-            jax.ShapeDtypeStruct((length, width), bf16),
-        ],
-        in_specs=[pl.BlockSpec(memory_space=pltpu.SMEM)] + [vmem] * (5 + blocks + count),
-        out_specs=[vmem] * 7,
+        ]
+        + [jax.ShapeDtypeStruct((rows, width), bf16)] * blocks,
+        in_specs=[pl.BlockSpec(memory_space=pltpu.SMEM)] + [vmem] * (6 + blocks + count),
+        out_specs=[vmem] * (6 + blocks),
         compiler_params=ATTENTION_PARAMS,
         cost_estimate=SMALL_COST,
         name="attention_forward",
-    )(own_place(), gain[None], *tables, *token_blocks, *parts)
+    )(own_place(), gain[None], *tables, *token_blocks, *parts, mirrors)
 
 
 def attention_backward(pieces, token_blocks, tables, full, factors, qkv, spread, query_cols, key_cols):
@@ -496,7 +505,9 @@
 
     def kernel(cosine_ref, sine_ref, down_ref, along_ref, full_ref, factors_ref, qkv_ref, spread_ref, *refs):
         piece_refs, token_refs = refs[:blocks], refs[blocks : 2 * blocks]
-        back, normed_back, gain_back, heads_back, turned = refs[2 * blocks :]
+        back, gain_back = refs[2 * blocks : 2 * blocks + 2]
+        normed_back = refs[2 * blocks + 2 : 3 * blocks + 2]
+        heads_back, turned = refs[3 * blocks + 2 :]
         weights = full_ref[...].reshape(width, full_ref.shape[2])
         for s in range(blocks):
             part = jnp.dot(piece_refs[s][...], weights[:, columns:], preferred_element_type=f32)
@@ -538,7 +549,7 @@
         for s in range(blocks):
             span = slice(s * rows, (s + 1) * rows)
             part = contract_cols(back[span, :], weights[:, :columns])
-            normed_back[s] = part.astype(bf16)
+            normed_back[s][...] = part.astype(bf16)
             scaled = part * (token_refs[s][...].astype(f32) * factors_ref[span, :])
             total = add(total, jnp.sum(scaled, axis=0, keepdims=True))
         gain_back[...] = total
@@ -548,11 +559,11 @@
         kernel,
         out_shape=[
             jax.ShapeDtypeStruct((length, columns), bf16),
-            jax.ShapeDtypeStruct((blocks, rows, width), bf16),
             jax.ShapeDtypeStruct((1, width), f32),
-        ],
+        ]
+        + [jax.ShapeDtypeStruct((rows, width), bf16)] * blocks,
         in_specs=[vmem] * (8 + 2 * blocks),
-        out_specs=[vmem] * 3,
+        out_specs=[vmem] * (2 + blocks),
         scratch_shapes=[pltpu.VMEM((length, query_cols), bf16), pltpu.VMEM((length, columns), f32)],
         compiler_params=ATTENTION_PARAMS,
         cost_estimate=LARGE_COST,
@@ -617,7 +628,7 @@
     pair_heads = key_cols // HEAD_SIZE
     ratio = query_heads // pair_heads
     experts = gate_weight.shape[0]
-    some = experts * 2 // 5
+    some = experts // 2
     spans = ((0, some), (some, experts - some))
 
     token_blocks = gather_gx(own_tokens)
@@ -629,14 +640,20 @@
     both = over_y(across)
     down_turned = jnp.swapaxes(down_weight, 1, 2)
     keep, give = halve_weights(gate_weight, up_weight, down_turned)
-    across, give = tie(across, give)
     attention_parts = [attention, across] + along + both
-    attention_parts, keep = tie(attention_parts, keep)
-    token_blocks, attention_parts, keep_sent = tie(token_blocks, attention_parts, keep)
-    attention_parts = attention_parts + [swap(p, "co", 1) for p in attention_parts]
-
-    given_across, given_along = swap(give, "gw", 1), over_y(keep)
-    mirror_keep = swap(keep_sent, "co", 1)
+    attention_mirrors = swap(jnp.stack(attention_parts), "co", 1)
+    positions = jnp.concatenate(
+        [(me_x ^ s) * rows + jnp.arange(rows, dtype=jnp.int32) for s in range(groups)]
+    ).astype(f32)
+    half = HEAD_SIZE // 2
+    freq = rope_base ** (-(jnp.arange(half, dtype=f32) * 2.0 / HEAD_SIZE))
+    angle = positions[:, None] * jnp.tile(freq, 128 // half)[None, :]
+    tables = (jnp.cos(angle), jnp.sin(angle), positions[:, None], positions[None, :])
+    token_blocks, tables, attention_mirrors, give, keep = tie(
+        token_blocks, tables, attention_mirrors, give, keep
+    )
+    across_w, along_w = swap(give, "gw", 1), over_y(keep)
+    mirror_keep = swap(keep, "co", 1)
 
     logits = route_logits[0].T
     weights = jnp.exp(logits - jnp.max(logits, axis=0, keepdims=True))
@@ -645,28 +662,18 @@
     routing = jnp.concatenate([routes[0].T.astype(f32), chance_high, chance - chance_high], axis=0)
     routing = jnp.pad(routing.astype(bf16).T, ((0, 0), (0, 128 - 3 * TOPK)))
     payload = jnp.concatenate([cotangent[0], routing], axis=1)
-    payload, token_blocks = tie(payload, token_blocks)
     turned = jnp.stack([w * groups + (me_x ^ s) for w in range(2) for s in range(groups)])
     gathered = lax.all_gather(payload, "gx", axis=0)
 
-    positions = jnp.concatenate(
-        [(me_x ^ s) * rows + jnp.arange(rows, dtype=jnp.int32) for s in range(groups)]
-    ).astype(f32)
-    half = HEAD_SIZE // 2
-    freq = rope_base ** (-(jnp.arange(half, dtype=f32) * 2.0 / HEAD_SIZE))
-    angle = positions[:, None] * jnp.tile(freq, 128 // half)[None, :]
-    tables = (jnp.cos(angle), jnp.sin(angle), positions[:, None], positions[None, :])
-    attention_full, normed_one, factor_all, qkv, heads, spread, branch_parts = attention_forward(
-        token_blocks, first_gain, attention_parts, tables, query_cols, key_cols
+    attention_full, normed_one, factor_all, qkv, heads, spread, *branch_parts = attention_forward(
+        token_blocks, first_gain, attention_parts, attention_mirrors, tables, query_cols, key_cols
     )
 
     branch_parts, mirror_keep = tie(branch_parts, mirror_keep)
-    branch_got = [
-        swap(branch_parts[s * rows : (s + 1) * rows], "gx", s) for s in range(1, groups)
-    ]
-    given_across, gathered, branch_got[0] = tie(given_across, gathered, branch_got[0])
+    branch_got = [swap(branch_parts[s], "gx", s) for s in range(1, groups)]
+    across_w, gathered, branch_got[0] = tie(across_w, gathered, branch_got[0])
     gathered_across = swap(gathered, "gw", 1)
-    branch = branch_parts[:rows].astype(f32)
+    branch = branch_parts[0].astype(f32)
     for value in branch_got:
         branch = branch + value.astype(f32)
 
@@ -675,35 +682,40 @@
     factor_two = rms_factor(middle)
     normed_two = (middle * factor_two * second_gain).astype(bf16)
 
-    normed_two, given_across, given_along = tie(normed_two, given_across, given_along)
+    middle_part = experts * 7 // 10
+    normed_two, across_w, along_w = tie(normed_two, across_w, along_w)
     normed_parts = gather_gx(normed_two)
-    both_0 = over_y(given_across[:some])
+    both_0 = over_y(across_w[:middle_part])
     turned_parts = {s: swap(normed_parts[s], "gw", 1) for s in (0, 1)}
 
     gathered = jnp.concatenate([gathered, gathered_across])
     routes_of, slots, _, slots_by, chances_by = route_slots(gathered, turned, me_x * experts, experts, width)
     back_in = gather_slots(gathered, (turned, width), slots)
-    normed_parts, turned_parts[0], turned_parts[1], both_0, given_across, given_along, back_in = tie(
-        normed_parts, turned_parts[0], turned_parts[1], both_0, given_across, given_along, back_in
+    normed_parts, turned_parts[0], turned_parts[1], both_0, across_w, along_w, back_in = tie(
+        normed_parts, turned_parts[0], turned_parts[1], both_0, across_w, along_w, back_in
     )
 
     rest = [s for s in range(groups) if s not in (0, 1)]
     turned_rest = swap(jnp.stack([normed_parts[s] for s in rest]), "gw", 1)
-    both_1 = over_y(given_across[some:])
-    mirror_given = [swap(v, "co", 1) for v in [given_across] + given_along]
+    both_1 = over_y(across_w[middle_part:])
+    mirror_w = [swap(v, "co", 1) for v in [across_w] + along_w]
     mirror_both_0 = [swap(v, "co", 1) for v in both_0]
     normed_rows = normed_parts + [turned_parts[0], turned_parts[1]]
     normed_rows = normed_rows + [turned_rest[i] for i in range(len(rest))]
+    normed_rows, both_1 = tie(normed_rows, both_1)
     rows_in = gather_slots(normed_rows, None, slots)
+    mirror_both_1 = [swap(v, "co", 1) for v in both_1]
+    rows_in, mirror_w, mirror_both_0, mirror_both_1 = tie(rows_in, mirror_w, mirror_both_0, mirror_both_1)
+
+    def halved(boths):
+        return [[(first, 0), (second, middle_part)] for first, second in zip(*boths)]
+
+    parts = [[(v, 0)] for v in [keep, across_w] + along_w] + halved((both_0, both_1))
+    parts = parts + [[(v, 0)] for v in [mirror_keep] + mirror_w] + halved((mirror_both_0, mirror_both_1))
     rows_back, mixed_parts, chance_parts, gradients, given = [], [], [], [], []
     for i, (start, size) in enumerate(spans):
-        if i == 0:
-            both, mirror_both = both_0, mirror_both_0
-        else:
-            rows_in, rows_back[0], both_1 = tie(rows_in, rows_back[0], both_1)
-            both, mirror_both = both_1, [swap(v, "co", 1) for v in both_1]
-        parts = [(v, start) for v in [keep, given_across] + given_along] + [(v, 0) for v in both]
-        parts = parts + [(v, start) for v in [mirror_keep] + mirror_given] + [(v, 0) for v in mirror_both]
+        if i == 1:
+            rows_in, rows_back[0] = tie(rows_in, rows_back[0])
         result = run_experts(rows_in, back_in, parts, start, size, slots_by, chances_by)
         for lot, value in zip((rows_back, mixed_parts, chance_parts, gradients, given), result):
             lot.append(value)
@@ -716,17 +728,17 @@
     others = range(1, many)
     got[0] = swap(given[0], "co", 1)
     got[0], rows_back = tie(got[0], rows_back)
+    far = [joint(0, t, 1).astype(bf16) for t in others]
+    far, rows_back, given[1] = tie(far, rows_back, given[1])
     got[1] = swap(given[1], "co", 1)
-    far = [joint(0, t, 1).astype(bf16) for t in others]
-    far, rows_back = tie(far, rows_back)
     along_one_0 = spread_y(far)
     plain = jnp.arange(2 * groups, dtype=jnp.int32)
     summed = sum_slots(rows_back, slots, plain)
     pieces = ((2, groups), (0, 2))
     crossed = [swap(summed[groups + a : groups + b], "gw", 1) for a, b in pieces]
     far = [joint(1, t, 1).astype(bf16) for t in others]
-    crossed[1], along_one_0, far, got[1] = tie(crossed[1], along_one_0, far, got[1])
-    along_one_1 = spread_y(far)
+    mixed_rows = sum_slots(mixed_parts, slots, plain)
+    crossed[0], mixed_rows = tie(crossed[0], mixed_rows)
 
     def half_sum(s):
         a, b = pieces[0] if s >= 2 else pieces[1]
@@ -734,9 +746,10 @@
         return summed[s].astype(f32) + value[s - a].astype(f32)
 
     normed_got = {s: swap(half_sum(s).astype(bf16), "gx", s) for s in range(2, groups)}
+    along_one_0, far, got[1], crossed[1] = tie(along_one_0, far, got[1], crossed[1])
+    along_one_1 = spread_y(far)
+    crossed[1], normed_got[3] = tie(crossed[1], normed_got[3])
     normed_got[1] = swap(half_sum(1).astype(bf16), "gx", 1)
-    normed_got[3], mixed_parts = tie(normed_got[3], mixed_parts)
-    mixed_rows = sum_slots(mixed_parts, slots, plain)
     chance_part = jnp.swapaxes(jnp.concatenate(chance_parts, axis=0), 0, 1)
     ids = (me_x * experts + jnp.arange(experts, dtype=jnp.int32)).astype(f32)
     same = routes_of[:, None, :, :] == ids[None, :, None, None]
@@ -749,10 +762,13 @@
     middle_back = upstream + norm_back(middle, factor_two, second_gain, normed_two_back)
     second_part = jnp.sum(normed_two_back * middle * factor_two, axis=0)
     branch_back = (residual_factor * middle_back).astype(bf16)
+    branch_back_blocks = gather_gx(branch_back)
+    mixed_rows, crossed[1] = tie(mixed_rows, crossed[1])
+    mixed_crossed = swap(mixed_rows[groups:], "gw", 1)
+    branch_back_blocks[1], gradients[0], along_one_1, mixed_crossed = tie(
+        branch_back_blocks[1], gradients[0], along_one_1, mixed_crossed
+    )
     far = [joint(0, t, 0).astype(bf16) for t in others]
-    branch_back, far = tie(branch_back, far)
-    branch_back_blocks = gather_gx(branch_back)
-    far, along_one_1 = tie(far, along_one_1)
     along_zero_0 = spread_y(far)
 
     def near(i, along):
@@ -761,9 +777,8 @@
             total = total + value.astype(f32)
         return total.astype(bf16)
 
-    crossed_0 = swap(near(0, along_one_0), "gw", 1)
-    crossed_0, mixed_rows = tie(crossed_0, mixed_rows)
-    mixed_crossed = swap(mixed_rows[groups:], "gw", 1)
+    near_0, mixed_crossed = tie(near(0, along_one_0), mixed_crossed)
+    crossed_0 = swap(near_0, "gw", 1)
     branch_back_blocks[1], got[1] = tie(branch_back_blocks[1], got[1])
     near_1 = near(1, along_one_1)
     far = [joint(1, t, 0).astype(bf16) for t in others]
@@ -773,27 +788,42 @@
         branch_back_blocks, near_1, far, mixed_send, chance_rows
     )
     mixed_got = [swap(mixed_send[s], "gx", s) for s in range(1, groups)]
-    along_zero_0, far = tie(along_zero_0, far)
-    along_zero_1 = spread_y(far)
-    crossed_1 = swap(near_1, "gw", 1)
-
-    back, normed_one_parts, first_part = attention_backward(
+    far_last, near_last = far, near_1
+
+    back, first_part, *normed_one_parts = attention_backward(
         branch_back_blocks, token_blocks, tables, attention_full, factor_all, qkv, spread, query_cols, key_cols
     )
+    back, along_zero_0, crossed_0, far_last, near_last = tie(back, along_zero_0, crossed_0, far_last, near_last)
+    along_zero_1 = spread_y(far_last)
+    crossed_1 = swap(near_last, "gw", 1)
     keep_gradient, give_gradient = attention_gradients(normed_one, back, branch_back_blocks, heads)
+    normed_one_parts, mixed_got, give_gradient = tie(normed_one_parts, mixed_got, give_gradient)
     got_gradient = swap(give_gradient, "co", 1)
-    normed_one_parts, mixed_got, got_gradient = tie(normed_one_parts, mixed_got, got_gradient)
     mixed = mixed_rows[0]
     for value in mixed_got:
         mixed = mixed + value.astype(f32)
     output = (middle + residual_factor * mixed).astype(bf16)
     normed_got = [swap(normed_one_parts[s], "gx", s) for s in range(1, groups)]
-    attention_sum = scatter_gy(keep_gradient, got_gradient)
     gains = jnp.stack([first_part[0], second_part])
-    gains, along_zero_1, crossed_1, chance_rows = tie(gains, along_zero_1, crossed_1, chance_rows)
+    gains = gains + swap(gains, "co", 1)
+    normed_got, got_gradient, along_zero_1, gains, chance_rows = tie(
+        normed_got, got_gradient, along_zero_1, gains, chance_rows
+    )
     chance_crossed = swap(chance_rows[groups:], "gw", 1)
-    normed_got, chance_rows, chance_crossed = tie(normed_got, chance_rows, chance_crossed)
-    gains = sum_everywhere(gains)
+    gains_got = others_of(gains, ("gt", "gw"))
+    total = keep_gradient.astype(f32) + got_gradient.astype(f32)
+    far_attention = spread_y([total[2 * t : 2 * t + 2].astype(bf16) for t in others])
+    sums = finish_gradients([gradients[0], got[0]] + along_zero_0, crossed_0, 0, None, experts)
+    sums = finish_gradients([gradients[1], got[1]] + along_zero_1, crossed_1, some, sums, experts)
+    gate_sum, up_sum, down_sum = sums
+    for value in gains_got:
+        gains = gains + value
+    for value in others_of(gains, ("gx",)):
+        gains = gains + value
+    attention_sum = total[:2]
+    for value in far_attention:
+        attention_sum = attention_sum + value.astype(f32)
+    attention_sum = attention_sum[0] + swap(attention_sum[1].astype(bf16), "gw", 1).astype(f32)
     normed_one_back = normed_one_parts[0].astype(f32)
     for value in normed_got:
         normed_one_back = normed_one_back + value.astype(f32)
@@ -803,12 +833,6 @@
     for s in range(1, groups):
         chance_back = chance_back + swap(chance_rows[s], "gx", s)
     logit_back = chance * (chance_back - jnp.sum(chance * chance_back, axis=0, keepdims=True))
-    sums = finish_gradients(
-        [gradients[0], got[0]] + along_zero_0, crossed_0, 0, None, experts
-    )
-    gate_sum, up_sum, down_sum = finish_gradients(
-        [gradients[1], got[1]] + along_zero_1, crossed_1, some, sums, experts
-    )
     return (
         output[None],
         tokens_back[None],

time: 557 us -> 526 us (0.944)
  waiting for transfers between devices: 217 us -> 178 us
  starting transfers between devices: 99.4 us -> 110 us
    ppermute x60 -> x57, waiting for transfers between devices: 188 us -> 131 us  [swap(): return lax.ppermute(value, axis, [(i, i ^ step) for i in range(count)])]
    all_gather x1, waiting for transfers between devices: 24.1 us -> 47.6 us  [local(): gathered = lax.all_gather(payload, 'gx', axis=0)]
    ppermute x60 -> x57, starting transfers between devices: 91.5 us -> 102 us  [swap(): return lax.ppermute(value, axis, [(i, i ^ step) for i in range(count)])]
    unnamed x135 -> x107, local copies, waits for them, and re-layouts: 14.1 us -> 16 us
  transfers between devices with their start and end apart: 67 -> 64, of which waited for: 25 -> 22; matrix products, arithmetic and copies ran while one was open for 10% -> 9% of each run, Pallas kernels for 21% -> 23%
where the time goes in v5:
time: 526 us; the launch traced here: 516 us
  waiting for transfers between devices  178 us (34%)
  Pallas kernels  145 us (28%)
  starting transfers between devices  110 us (21%)
  other arithmetic  39.2 us (7%)
  local copies, waits for them, and re-layouts  28.2 us (5%)
  between operations  15.2 us (3%)
    ppermute x57, waiting for transfers between devices, swap(): return lax.ppermute(value, axis, [(i, i ^ step) for i in range(count)])  131 us
    ppermute x57, starting transfers between devices, swap(): return lax.ppermute(value, axis, [(i, i ^ step) for i in range(count)])  102 us
    pallas_call x2, Pallas kernels, run_experts(): pl.pallas_call(kernel, grid_spec=pltpu.PrefetchScalarGridSpec(num_scalar_...  52.5 us
    all_gather x1, waiting for transfers between devices, local(): gathered = lax.all_gather(payload, 'gx', axis=0)  47.6 us
    pallas_call x2, Pallas kernels, gather_slots(): pl.pallas_call(kernel_list if listed else kernel_array, grid_spec=pltpu.P...  17.4 us
    unnamed x107, local copies, waits for them, and re-layouts  16 us
    pallas_call x2, Pallas kernels, sum_slots(): pl.pallas_call(kernel, grid_spec=pltpu.PrefetchScalarGridSpec(num_scalar_...  15.5 us
    pallas_call x1, Pallas kernels, attention_backward(): pl.pallas_call(kernel, out_shape=[jax.ShapeDtypeStruct((length, columns),...  15.4 us
  transfers between devices with their start and end apart: 64, of which 22 were waited for; matrix products, arithmetic and copies ran while one was open for 9% of the time, Pallas kernels for 23%

profile of v5, /device:TPU:0, one launch (start us, length us, event | category | flops | bytes accessed | tf_op | source)
XLA Modules:
  0.0 515.6 jit_solution(8670810643806124854)
XLA Ops:
  22.3 8.6 %collective-permute-done.5.refs_7_ = bf16[192,1024]{1,0:T(8,128)(2,1)S(1)} collective-permute-done((bf16[192,1024]{1,0:T(8,128)(2,1)S(1)}, bf16[192,1024]{1,0:T(8,128)(2,1)S(1)}, u32[]{:S(2)}, u32[]{:S(2)}) %collective-permute-start.5) | collective-permute-done | bytes 393248 | tf_op jit(solution)/shard_map/ppermute | solution.py:30
  31.8 8.3 %halve_weights.1 = (bf16[10,192,768]{2,1,0:T(8,128)(2,1)}, bf16[10,192,768]{2,1,0:T(8,128)(2,1)}) custom-call(s32[1]{0:T(128)} %bitcast.15.side_ref, bf16[10,192,512]{2,1,0:T(8,128)(2,1)} %gate_ref.1, bf16[10,192,512]{2,1,0:T(8,128)(2,1)} %up_ref.1, bf16[10,192,512]{2,1,0:T(8,128)(2,1)} %bitcast.189), custom_call_target="tpu_custom_call" | custom-call | flops 10000000000 | bytes 100000000 | tf_op jit(solution)/shard_map/halve_weights/pallas_call | solution.py:109
  48.2 12.3 %attention_forward.1 = (bf16[8,192,1024]{2,1,0:T(8,128)(2,1)}, bf16[512,1536]{1,0:T(8,128)(2,1)}, f32[512,1]{1,0:T(8,128)}, bf16[512,640]{1,0:T(8,128)(2,1)}, bf...) custom-call(s32[1]{0:T(128)} %bitcast.1.me_ref, ...), custom_call_target="tpu_custom_call" | custom-call | flops 1 | bytes 1 | tf_op jit(solution)/shard_map/attention_forward/pallas_call | solution.py:477
  60.5 6.2 %collective-permute-start.9 = (bf16[128,1536]{1,0:T(8,128)(2,1)}, bf16[128,1536]{1,0:T(8,128)(2,1)}, u32[]{:S(2)}, u32[]{:S(2)}) collective-permute-start(bf16[128,1536]{1,0:T(8,128)(2,1)} %get-tuple-element.170), channel_id=1, source_target_pairs={{0,8},{8,0},{16,24},{24,16},{1,9},{9,1},{17,25},{25,17},{2,10},{10... | collective-permute-start | bytes 1179656 | tf_op jit(solution)/shard_map/ppermute | solution.py:30
  69.2 47.6 %all-gather.3.cloned.1.call-done = bf16[512,1664]{1,0:T(8,128)(2,1)} async-done(((bf16[128,1664]{1,0:T(8,128)(2,1)}), bf16[512,1664]{1,0:T(8,128)(2,1)}) %all-gather.3.cloned.1.call-update) | async-done | bytes 1703952 | tf_op jit(solution)/shard_map/all_gather | solution.py:666
  135.3 10.9 %collective-permute-done.14.refs_1_ = bf16[128,1536]{1,0:T(8,128)(2,1)} collective-permute-done((bf16[128,1536]{1,0:T(8,128)(2,1)}, bf16[128,1536]{1,0:T(8,128)(2,1)}, u32[]{:S(2)}, u32[]{:S(2)}) %collective-permute-start.14) | collective-permute-done | bytes 393248 | tf_op jit(solution)/shard_map/ppermute | solution.py:30
  163.5 8.1 %gather_slots.2.back_ref = bf16[10,8,48,1536]{3,2,1,0:T(8,128)(2,1)} custom-call(s32[8]{0:T(128)S(1)} %copy-done.2, f32[8,10,128]{2,1,0:T(8,128)S(1)} %copy-done.4, bf16[8,128,1664]{2,1,0:T(8,128)(2,1)S(1)} %copy-done.1), custom_call_target="tpu_custom_call" | custom-call | flops 10000000000 | bytes 100000000 | tf_op jit(solution)/shard_map/gather_slots/pallas_call | solution.py:258
  176.6 16.4 %collective-permute-done.20 = bf16[2,128,1536]{2,1,0:T(8,128)(2,1)S(1)} collective-permute-done((bf16[2,128,1536]{2,1,0:T(8,128)(2,1)S(1)}, bf16[2,128,1536]{2,1,0:T(8,128)(2,1)S(1)}, u32[]{:S(2)}, u32[]{:S(2)}) %collective-permute-start.20) | collective-permute-done | bytes 786464 | tf_op jit(solution)/shard_map/ppermute | solution.py:30
  196.9 9.3 %gather_slots.3.rows_ref = bf16[10,8,48,1536]{3,2,1,0:T(8,128)(2,1)} custom-call(s32[1]{0:T(128)} %constant.48.clone.1.order_ref, f32[8,10,128]{2,1,0:T(8,128)S(1)} %copy-done.4, bf16[128,1536]{1,0:T(8,128)(2,1)} %multiply_convert_fusion.1.refs_0_, bf16[128,1536]{1,0:T(8,128)(2,1)} %collective-permute-done.14.refs_1_, ...), custom_call_target="tpu_custom_call" | custom-call | flops 10000000000 | bytes 100000000 | tf_op jit(solution)/shard_map/gather_slots/pallas_call | solution.py:258
  209.2 26.0 %run_experts.2 = (bf16[5,8,48,1536]{3,2,1,0:T(8,128)(2,1)}, bf16[5,8,48,1536]{3,2,1,0:T(8,128)(2,1)}, f32[5,8,128]{2,1,0:T(8,128)}, bf16[4,5,192,768]{3,2,1,0:T(8,128)(2,1)}, bf16[4,5,192,768]{3,2,1,0:T(8,128)(2,1)}) custom-call(s32[1]{0:T(128)} %bitcast.1.me_ref, bf16[10,8,48,1536]{3,2,1,0:T(8,128)(2,1)} %gather_slots.3.rows_ref, ...), custom_call_target="tpu_custom_call" | custom-call | flops 10000000000 | bytes 100000000 | tf_op jit(solution)/shard_map/run_experts/pallas_call | solution.py:382
  235.5 26.5 %run_experts.3 = (bf16[5,8,48,1536]{3,2,1,0:T(8,128)(2,1)}, bf16[5,8,48,1536]{3,2,1,0:T(8,128)(2,1)}, f32[5,8,128]{2,1,0:T(8,128)}, bf16[4,5,192,768]{3,2,1,0:T(8,128)(2,1)}, bf16[4,5,192,768]{3,2,1,0:T(8,128)(2,1)}) custom-call(s32[1]{0:T(128)} %bitcast.1.me_ref, bf16[10,8,48,1536]{3,2,1,0:T(8,128)(2,1)} %gather_slots.3.rows_ref, ...), custom_call_target="tpu_custom_call" | custom-call | flops 10000000000 | bytes 100000000 | tf_op jit(solution)/shard_map/run_experts/pallas_call | solution.py:382
  268.4 7.5 %sum_slots.2 = bf16[8,128,1536]{2,1,0:T(8,128)(2,1)S(1)} custom-call(s32[8]{0:T(128)S(1)} %iota.32.order_ref, f32[8,10,128]{2,1,0:T(8,128)S(1)} %copy-done.5, bf16[5,8,48,1536]{3,2,1,0:T(8,128)(2,1)S(1)} %copy-done.3, bf16[5,8,48,1536]{3,2,1,0:T(8,128)(2,1)} %get-tuple-element.218.refs_1_), custom_call_target="tpu_custom_call" | custom-call | flops 10000000000 | bytes 100000000 | tf_op jit(solution)/shard_map/sum_slots/pallas_call | solution.py:290
  279.9 8.0 %sum_slots.3 = bf16[8,128,1536]{2,1,0:T(8,128)(2,1)S(1)} custom-call(s32[8]{0:T(128)S(1)} %iota.33.order_ref, f32[8,10,128]{2,1,0:T(8,128)S(1)} %copy-done.5, bf16[5,8,48,1536]{3,2,1,0:T(8,128)(2,1)S(1)} %bitcast.168, bf16[5,8,48,1536]{3,2,1,0:T(8,128)(2,1)} %get-tuple-element.220.refs_1_), custom_call_target="tpu_custom_call" | custom-call | flops 10000000000 | bytes 100000000 | tf_op jit(solution)/shard_map/sum_slots/pallas_call | solution.py:290
  288.8 8.8 %collective-permute-done.27 = bf16[2,128,1536]{2,1,0:T(8,128)(2,1)} collective-permute-done((bf16[2,128,1536]{2,1,0:T(8,128)(2,1)}, bf16[2,128,1536]{2,1,0:T(8,128)(2,1)}, u32[]{:S(2)}, u32[]{:S(2)}) %collective-permute-start.27) | collective-permute-done | bytes 786464 | tf_op jit(solution)/shard_map/ppermute | solution.py:30
  313.7 14.9 %collective-permute-start.33 = (bf16[128,1536]{1,0:T(8,128)(2,1)S(1)}, bf16[128,1536]{1,0:T(8,128)(2,1)S(1)}, u32[]{:S(2)}, u32[]{:S(2)}) collective-permute-start(bf16[128,1536]{1,0:T(8,128)(2,1)S(1)} %fusion.26), channel_id=1, source_target_pairs={{0,8},{8,0},{16,24},{24,16},{1,9},{9,1},{17,25},{25,17},{2,10},{10... | collective-permute-start | bytes 1179656 | tf_op jit(solution)/shard_map/ppermute | solution.py:30
  336.1 8.3 %collective-permute-done.33 = bf16[128,1536]{1,0:T(8,128)(2,1)S(1)} collective-permute-done((bf16[128,1536]{1,0:T(8,128)(2,1)S(1)}, bf16[128,1536]{1,0:T(8,128)(2,1)S(1)}, u32[]{:S(2)}, u32[]{:S(2)}) %collective-permute-start.33) | collective-permute-done | bytes 393248 | tf_op jit(solution)/shard_map/ppermute | solution.py:30
  350.5 13.3 %collective-permute-done.34.refs_1_ = bf16[128,1536]{1,0:T(8,128)(2,1)S(1)} collective-permute-done((bf16[128,1536]{1,0:T(8,128)(2,1)S(1)}, bf16[128,1536]{1,0:T(8,128)(2,1)S(1)}, u32[]{:S(2)}, u32[]{:S(2)}) %collective-permute-start.34) | collective-permute-done | bytes 393248 | tf_op jit(solution)/shard_map/ppermute | solution.py:30
  388.3 15.4 %attention_backward.1 = (bf16[512,640]{1,0:T(8,128)(2,1)}, f32[1,1536]{1,0:T(1,128)}, bf16[128,1536]{1,0:T(8,128)(2,1)}, bf16[128,1536]{1,0:T(8,128)(2,1)}, bf16...) custom-call(f32[512,128]{1,0:T(8,128)} %get-tuple-element.154.cosine_ref, f32[512,128]{1,0:T(8,128)} %get-tuple-element.155.sine_ref, ...), custom_call_target="tpu_custom_call" | custom-call | flops 10000000000 | bytes 100000000 | tf_op jit(solution)/shard_map/attention_backward/pallas_call | solution.py:558
  418.6 7.1 %collective-permute-start.44 = (bf16[128,1536]{1,0:T(8,128)(2,1)}, bf16[128,1536]{1,0:T(8,128)(2,1)S(1)}, u32[]{:S(2)}, u32[]{:S(2)}) collective-permute-start(bf16[128,1536]{1,0:T(8,128)(2,1)} %get-tuple-element.268), channel_id=1, source_target_pairs={{0,8},{8,0},{16,24},{24,16},{1,9},{9,1},{17,25},{25,17},{2,10},{10... | collective-permute-start | bytes 1179656 | tf_op jit(solution)/shard_map/ppermute | solution.py:30
  428.7 7.3 %finish_gradients.2 = (f32[10,192,512]{2,1,0:T(8,128)}, f32[10,192,512]{2,1,0:T(8,128)}, f32[10,192,512]{2,1,0:T(8,128)}) custom-call(s32[1]{0:T(128)} %bitcast.15.side_ref, bf16[4,5,192,768]{3,2,1,0:T(8,128)(2,1)} %get-tuple-element.231.refs_0_, bf16[4,5,192,768]{3,2,1,0:T(8,128)(2,1)} %collective-permute-done.26.refs_1_, ...), custom_call_target="tpu_custom_call" | custom-call | flops 1 | bytes 1 | tf_op jit(solution)/shard_map/finish_gradients/pallas_call | solution.py:153
  436.0 7.3 %collective-permute-done.44 = bf16[128,1536]{1,0:T(8,128)(2,1)S(1)} collective-permute-done((bf16[128,1536]{1,0:T(8,128)(2,1)}, bf16[128,1536]{1,0:T(8,128)(2,1)S(1)}, u32[]{:S(2)}, u32[]{:S(2)}) %collective-permute-start.44) | collective-permute-done | bytes 393248 | tf_op jit(solution)/shard_map/ppermute | solution.py:30
  443.5 12.2 %collective-permute-done.45 = bf16[128,1536]{1,0:T(8,128)(2,1)S(1)} collective-permute-done((bf16[128,1536]{1,0:T(8,128)(2,1)}, bf16[128,1536]{1,0:T(8,128)(2,1)S(1)}, u32[]{:S(2)}, u32[]{:S(2)}) %collective-permute-start.45) | collective-permute-done | bytes 393248 | tf_op jit(solution)/shard_map/ppermute | solution.py:30
  469.1 9.1 %collective-permute-done.58.refs_3_ = bf16[5,192,768]{2,1,0:T(8,128)(2,1)} collective-permute-done((bf16[5,192,768]{2,1,0:T(8,128)(2,1)}, bf16[5,192,768]{2,1,0:T(8,128)(2,1)}, u32[]{:S(2)}, u32[]{:S(2)}) %collective-permute-start.58) | collective-permute-done | bytes 1474592 | tf_op jit(solution)/shard_map/ppermute | solution.py:30
  478.6 7.3 %finish_gradients.3 = (f32[10,192,512]{2,1,0:T(8,128)}, f32[10,192,512]{2,1,0:T(8,128)}, f32[10,192,512]{2,1,0:T(8,128)}) custom-call(s32[1]{0:T(128)} %bitcast.15.side_ref, bf16[4,5,192,768]{3,2,1,0:T(8,128)(2,1)} %get-tuple-element.223.refs_0_, bf16[4,5,192,768]{3,2,1,0:T(8,128)(2,1)} %copy-done.10, ...), custom_call_target="tpu_custom_call", output_to_operand_aliasing={{0}: (5, {}), {1}: (6, {}), {2}: (7, {})} | custom-call | flops 1 | bytes 1 | tf_op jit(solution)/shard_map/finish_gradients/pallas_call | solution.py:153
  (306 shorter events, 193.8 us)
Async XLA Ops:
  7.2 109.6 %all-gather.3.cloned.1.call-start = ((), (), s32[]{:S(2)}) async-start(), calls=%async_computation | async-start | bytes 2129920 | tf_op jit(solution)/shard_map/all_gather | solution.py:666
  44.6 72.1 %collective-permute-start.8 = (bf16[10,192,768]{2,1,0:T(8,128)(2,1)}, bf16[10,192,768]{2,1,0:T(8,128)(2,1)S(1)}, u32[]{:S(2)}, u32[]{:S(2)}) collective-permute-start(bf16[10,192,768]{2,1,0:T(8,128)(2,1)} %get-tuple-element.169), channel_id=1, source_target_pairs={{0,2},{2,0},{1,3},{3,1},{4,6},{6,4},{5,7},{7,5},{8,10},{10,8},{9,1... | collective-permute-start | bytes 8847368 | tf_op jit(solution)/shard_map/ppermute | solution.py:30
  46.2 75.6 %collective-permute-start.13 = (bf16[10,192,768]{2,1,0:T(8,128)(2,1)}, bf16[10,192,768]{2,1,0:T(8,128)(2,1)}, u32[]{:S(2)}, u32[]{:S(2)}) collective-permute-start(bf16[10,192,768]{2,1,0:T(8,128)(2,1)} %get-tuple-element.167.refs_0_), channel_id=1, source_target_pairs={{0,4},{4,0},{1,5},{5,1},{2,6},{6,2},{3,7},{7,3},{8,12},{12,8},{9,1... | collective-permute-start | bytes 8847368 | tf_op jit(solution)/shard_map/ppermute | solution.py:30
  60.5 56.3 %collective-permute-start.9 = (bf16[128,1536]{1,0:T(8,128)(2,1)}, bf16[128,1536]{1,0:T(8,128)(2,1)}, u32[]{:S(2)}, u32[]{:S(2)}) collective-permute-start(bf16[128,1536]{1,0:T(8,128)(2,1)} %get-tuple-element.170), channel_id=1, source_target_pairs={{0,8},{8,0},{16,24},{24,16},{1,9},{9,1},{17,25},{25,17},{2,10},{10... | collective-permute-start | bytes 1179656 | tf_op jit(solution)/shard_map/ppermute | solution.py:30
  66.7 51.6 %collective-permute-start.10 = (bf16[128,1536]{1,0:T(8,128)(2,1)}, bf16[128,1536]{1,0:T(8,128)(2,1)}, u32[]{:S(2)}, u32[]{:S(2)}) collective-permute-start(bf16[128,1536]{1,0:T(8,128)(2,1)} %get-tuple-element.172), channel_id=1, source_target_pairs={{0,16},{8,24},{16,0},{24,8},{1,17},{9,25},{17,1},{25,9},{2,18},{10... | collective-permute-start | bytes 1179656 | tf_op jit(solution)/shard_map/ppermute | solution.py:30
  67.8 50.5 %collective-permute-start.11 = (bf16[128,1536]{1,0:T(8,128)(2,1)}, bf16[128,1536]{1,0:T(8,128)(2,1)}, u32[]{:S(2)}, u32[]{:S(2)}) collective-permute-start(bf16[128,1536]{1,0:T(8,128)(2,1)} %get-tuple-element.173), channel_id=1, source_target_pairs={{0,24},{8,16},{16,8},{24,0},{1,25},{9,17},{17,9},{25,1},{2,26},{10... | collective-permute-start | bytes 1179656 | tf_op jit(solution)/shard_map/ppermute | solution.py:30
  116.8 36.4 %collective-permute-start.12 = (bf16[4,128,1664]{2,1,0:T(8,128)(2,1)}, bf16[4,128,1664]{2,1,0:T(8,128)(2,1)}, u32[]{:S(2)}, u32[]{:S(2)}) collective-permute-start(bf16[4,128,1664]{2,1,0:T(8,128)(2,1)} %bitcast.182), channel_id=1, source_target_pairs={{0,2},{2,0},{1,3},{3,1},{4,6},{6,4},{5,7},{7,5},{8,10},{10,8},{9,1... | collective-permute-start | bytes 5111816 | tf_op jit(solution)/shard_map/ppermute | solution.py:30
  123.3 48.3 %collective-permute-start.19 = (bf16[7,192,768]{2,1,0:T(8,128)(2,1)}, bf16[7,192,768]{2,1,0:T(8,128)(2,1)}, u32[]{:S(2)}, u32[]{:S(2)}) collective-permute-start(bf16[7,192,768]{2,1,0:T(8,128)(2,1)} %slice.149), channel_id=1, source_target_pairs={{0,4},{4,0},{1,5},{5,1},{2,6},{6,2},{3,7},{7,3},{8,12},{12,8},{9,1... | collective-permute-start | bytes 6193160 | tf_op jit(solution)/shard_map/ppermute | solution.py:30
  131.4 40.2 %collective-permute-start.15 = (bf16[128,1536]{1,0:T(8,128)(2,1)}, bf16[128,1536]{1,0:T(8,128)(2,1)}, u32[]{:S(2)}, u32[]{:S(2)}) collective-permute-start(bf16[128,1536]{1,0:T(8,128)(2,1)} %multiply_convert_fusion.1.refs_0_), channel_id=1, source_target_pairs={{0,16},{8,24},{16,0},{24,8},{1,17},{9,25},{17,1},{25,9},{2,18},{10... | collective-permute-start | bytes 1179656 | tf_op jit(solution)/shard_map/ppermute | solution.py:30
  131.4 40.2 %collective-permute-start.16 = (bf16[128,1536]{1,0:T(8,128)(2,1)}, bf16[128,1536]{1,0:T(8,128)(2,1)}, u32[]{:S(2)}, u32[]{:S(2)}) collective-permute-start(bf16[128,1536]{1,0:T(8,128)(2,1)} %multiply_convert_fusion.1.refs_0_), channel_id=1, source_target_pairs={{0,24},{8,16},{16,8},{24,0},{1,25},{9,17},{17,9},{25,1},{2,26},{10... | collective-permute-start | bytes 1179656 | tf_op jit(solution)/shard_map/ppermute | solution.py:30
  171.6 34.7 %collective-permute-start.22 = (bf16[10,192,768]{2,1,0:T(8,128)(2,1)S(1)}, bf16[10,192,768]{2,1,0:T(8,128)(2,1)S(1)}, u32[]{:S(2)}, u32[]{:S(2)}) collective-permute-start(bf16[10,192,768]{2,1,0:T(8,128)(2,1)S(1)} %copy-done.7), channel_id=1, source_target_pairs={{0,1},{1,0},{2,3},{3,2},{4,5},{5,4},{6,7},{7,6},{8,9},{9,8},{10,11... | collective-permute-start | bytes 8847368 | tf_op jit(solution)/shard_map/ppermute | solution.py:30
  171.7 36.0 %collective-permute-start.23 = (bf16[10,192,768]{2,1,0:T(8,128)(2,1)}, bf16[10,192,768]{2,1,0:T(8,128)(2,1)}, u32[]{:S(2)}, u32[]{:S(2)}) collective-permute-start(bf16[10,192,768]{2,1,0:T(8,128)(2,1)} %collective-permute-done.13.refs_2_), channel_id=1, source_target_pairs={{0,1},{1,0},{2,3},{3,2},{4,5},{5,4},{6,7},{7,6},{8,9},{9,8},{10,11... | collective-permute-start | bytes 8847368 | tf_op jit(solution)/shard_map/ppermute | solution.py:30
  265.4 39.8 %collective-permute-start.29 = (bf16[4,5,192,768]{3,2,1,0:T(8,128)(2,1)}, bf16[4,5,192,768]{3,2,1,0:T(8,128)(2,1)S(1)}, u32[]{:S(2)}, u32[]{:S(2)}) collective-permute-start(bf16[4,5,192,768]{3,2,1,0:T(8,128)(2,1)} %get-tuple-element.224), channel_id=1, source_target_pairs={{0,1},{1,0},{2,3},{3,2},{4,5},{5,4},{6,7},{7,6},{8,9},{9,8},{10,11... | collective-permute-start | bytes 17694728 | tf_op jit(solution)/shard_map/ppermute | solution.py:30
  278.1 35.5 %collective-permute-start.28 = (bf16[5,192,768]{2,1,0:T(8,128)(2,1)}, bf16[5,192,768]{2,1,0:T(8,128)(2,1)}, u32[]{:S(2)}, u32[]{:S(2)}) collective-permute-start(bf16[5,192,768]{2,1,0:T(8,128)(2,1)} %fusion.2), channel_id=1, source_target_pairs={{0,4},{4,0},{1,5},{5,1},{2,6},{6,2},{3,7},{7,3},{8,12},{12,8},{9,1... | collective-permute-start | bytes 4423688 | tf_op jit(solution)/shard_map/ppermute | solution.py:30
  302.8 33.3 %collective-permute-start.32 = (bf16[128,1536]{1,0:T(8,128)(2,1)S(1)}, bf16[128,1536]{1,0:T(8,128)(2,1)S(1)}, u32[]{:S(2)}, u32[]{:S(2)}) collective-permute-start(bf16[128,1536]{1,0:T(8,128)(2,1)S(1)} %get-tuple-element.327), channel_id=1, source_target_pairs={{0,16},{8,24},{16,0},{24,8},{1,17},{9,25},{17,1},{25,9},{2,18},{10... | collective-permute-start | bytes 1179656 | tf_op jit(solution)/shard_map/ppermute | solution.py:30
  328.7 36.0 %collective-permute-start.36 = (bf16[4,128,1536]{2,1,0:T(8,128)(2,1)S(1)}, bf16[4,128,1536]{2,1,0:T(8,128)(2,1)S(1)}, u32[]{:S(2)}, u32[]{:S(2)}) collective-permute-start(bf16[4,128,1536]{2,1,0:T(8,128)(2,1)S(1)} %slice.168), channel_id=1, source_target_pairs={{0,2},{2,0},{1,3},{3,1},{4,6},{6,4},{5,7},{7,5},{8,10},{10,8},{9,1... | collective-permute-start | bytes 4718600 | tf_op jit(solution)/shard_map/ppermute | solution.py:30
  330.5 33.5 %collective-permute-start.35 = (bf16[5,192,768]{2,1,0:T(8,128)(2,1)S(1)}, bf16[5,192,768]{2,1,0:T(8,128)(2,1)S(1)}, u32[]{:S(2)}, u32[]{:S(2)}) collective-permute-start(bf16[5,192,768]{2,1,0:T(8,128)(2,1)S(1)} %fusion.3), channel_id=1, source_target_pairs={{0,4},{4,0},{1,5},{5,1},{2,6},{6,2},{3,7},{7,3},{8,12},{12,8},{9,1... | collective-permute-start | bytes 4423688 | tf_op jit(solution)/shard_map/ppermute | solution.py:30
  346.2 33.5 %collective-permute-start.37 = (bf16[128,1536]{1,0:T(8,128)(2,1)S(1)}, bf16[128,1536]{1,0:T(8,128)(2,1)S(1)}, u32[]{:S(2)}, u32[]{:S(2)}) collective-permute-start(bf16[128,1536]{1,0:T(8,128)(2,1)S(1)} %multiply_convert_fusion.refs_0_), channel_id=1, source_target_pairs={{0,16},{8,24},{16,0},{24,8},{1,17},{9,25},{17,1},{25,9},{2,18},{10... | collective-permute-start | bytes 1179656 | tf_op jit(solution)/shard_map/ppermute | solution.py:30
  373.6 33.3 %collective-permute-start.42 = (bf16[5,192,768]{2,1,0:T(8,128)(2,1)}, bf16[5,192,768]{2,1,0:T(8,128)(2,1)}, u32[]{:S(2)}, u32[]{:S(2)}) collective-permute-start(bf16[5,192,768]{2,1,0:T(8,128)(2,1)} %fusion.5), channel_id=1, source_target_pairs={{0,4},{4,0},{1,5},{5,1},{2,6},{6,2},{3,7},{7,3},{8,12},{12,8},{9,1... | collective-permute-start | bytes 4423688 | tf_op jit(solution)/shard_map/ppermute | solution.py:30
  380.6 33.6 %collective-permute-start.39 = (bf16[128,1536]{1,0:T(8,128)(2,1)S(1)}, bf16[128,1536]{1,0:T(8,128)(2,1)S(1)}, u32[]{:S(2)}, u32[]{:S(2)}) collective-permute-start(bf16[128,1536]{1,0:T(8,128)(2,1)S(1)} %get-tuple-element.333), channel_id=1, source_target_pairs={{0,8},{8,0},{16,24},{24,16},{1,9},{9,1},{17,25},{25,17},{2,10},{10... | collective-permute-start | bytes 1179656 | tf_op jit(solution)/shard_map/ppermute | solution.py:30
  415.2 40.5 %collective-permute-start.47 = (bf16[4,192,1024]{2,1,0:T(8,128)(2,1)}, bf16[4,192,1024]{2,1,0:T(8,128)(2,1)}, u32[]{:S(2)}, u32[]{:S(2)}) collective-permute-start(bf16[4,192,1024]{2,1,0:T(8,128)(2,1)} %get-tuple-element.271), channel_id=1, source_target_pairs={{0,1},{1,0},{2,3},{3,2},{4,5},{5,4},{6,7},{7,6},{8,9},{9,8},{10,11... | collective-permute-start | bytes 4718600 | tf_op jit(solution)/shard_map/ppermute | solution.py:30
  415.2 40.5 %collective-permute-start.48 = (bf16[5,192,768]{2,1,0:T(8,128)(2,1)}, bf16[5,192,768]{2,1,0:T(8,128)(2,1)}, u32[]{:S(2)}, u32[]{:S(2)}) collective-permute-start(bf16[5,192,768]{2,1,0:T(8,128)(2,1)} %fusion.4), channel_id=1, source_target_pairs={{0,4},{4,0},{1,5},{5,1},{2,6},{6,2},{3,7},{7,3},{8,12},{12,8},{9,1... | collective-permute-start | bytes 4423688 | tf_op jit(solution)/shard_map/ppermute | solution.py:30
  443.3 34.8 %collective-permute-start.58 = (bf16[5,192,768]{2,1,0:T(8,128)(2,1)}, bf16[5,192,768]{2,1,0:T(8,128)(2,1)}, u32[]{:S(2)}, u32[]{:S(2)}) collective-permute-start(bf16[5,192,768]{2,1,0:T(8,128)(2,1)} %fusion), channel_id=1, source_target_pairs={{0,2},{2,0},{1,3},{3,1},{4,6},{6,4},{5,7},{7,5},{8,10},{10,8},{9,1... | collective-permute-start | bytes 4423688 | tf_op jit(solution)/shard_map/ppermute | solution.py:30
  457.8 33.2 %collective-permute-start.52 = (f32[2,1536]{1,0:T(2,128)}, f32[2,1536]{1,0:T(2,128)}, u32[]{:S(2)}, u32[]{:S(2)}) collective-permute-start(f32[2,1536]{1,0:T(2,128)} %fusion.47), channel_id=1, source_target_pairs={{0,6},{2,4},{4,2},{6,0},{1,7},{3,5},{5,3},{7,1},{8,14},{10,12},{12... | collective-permute-start | bytes 36872 | tf_op jit(solution)/shard_map/ppermute | solution.py:175
  (93 other events, 1871.2 us)
Sparse Core Ops, SparseCore 0:
  46.3 70.3 all-gather.2
